TPU v7x, 32 devices: a whole 2x2x4 slice. The times are simulated.
32 devices in a mesh: vel: 4 (over y, core), pos: 8 (over z, x).
Axes of the slice: x: 2, y: 2, z: 4, core: 2. Of those that a mesh axis runs over, the one named last changes fastest.
Arguments:
- value_next: float32 [16, 64, 64, 512], P('pos', 'vel'), may hold values from -6 to 6
- density: float32 [16, 64, 64, 512], P('pos', 'vel'), as said below
Outputs:
- value_now: float32 [16, 64, 64, 512], P('pos', 'vel')
- density_next: float32 [16, 64, 64, 512], P('pos', 'vel')
Inputs may be any that keep to these rules, and one draw needn't show every extreme that they name: density is positive everywhere.
All inputs are finite; a program needn't handle non-finite values.
Results may differ from a plain program's by a relative error of at most 0.00002.
Values sent between devices are 32-bit elements; how exact they have to be, the bound alone decides.
No kernel may reach another device: no remote copies, remote signals or barrier semaphores. Data moves between devices by JAX's collectives and lax.ppermute only.
A program may use at most 192 MiB of HBM per device.

v0:
```python
import jax
import jax.numpy as jnp
from jax import lax
from jax.sharding import PartitionSpec as P

COURANT = 0.4
CONTROL_COST = 0.25
VISCOSITY = 0.15
CROWDING = 0.3


def from_behind(block, axis, distance):
    devices = range(lax.axis_size(axis))
    route = [((i - distance) % len(devices), i) for i in devices]
    return lax.ppermute(block, axis, route)


def passed_along(value, axis, steps):
    count = lax.axis_size(axis)
    leading, last = (max(0, -steps), min(count, count - steps))
    return lax.ppermute(value, axis, [(source, source + steps) for source in range(leading, last)])


def speeds(first, count, total):
    index = first + jnp.arange(count, dtype=jnp.int32)
    return COURANT * ((index.astype(jnp.float32) + 0.5 - total / 2) / (total / 2))


def along_second(array, step):
    rolled = jnp.roll(array, -step, 2)
    place = lax.broadcasted_iota(jnp.int32, array.shape, 2)
    edge = array.shape[2] - 1 if step > 0 else 0
    return jnp.where(place == edge, array, rolled)


def value_core(centre, x_up, x_dn, a_up, a_dn, speed_x, speed_y, crowding):
    along_x = speed_x[None, :, None, None]
    along_y = speed_y[None, None, :, None]
    carry_x = jnp.where(along_x > 0, along_x * (x_up - centre), along_x * (centre - x_dn))
    ahead_y = jnp.roll(centre, -1, 3) - centre
    behind_y = centre - jnp.roll(centre, 1, 3)
    carry_y = jnp.where(along_y > 0, along_y * ahead_y, along_y * behind_y)
    upper_v = a_up - centre
    lower_v = centre - a_dn
    upper_w = along_second(centre, 1) - centre
    lower_w = centre - along_second(centre, -1)
    hamilton = 0.5 * (
        jnp.square(jnp.maximum(lower_v, 0.0))
        + jnp.square(jnp.minimum(upper_v, 0.0))
        + jnp.square(jnp.maximum(lower_w, 0.0))
        + jnp.square(jnp.minimum(upper_w, 0.0))
    )
    laplace = upper_v - lower_v + upper_w - lower_w
    return (
        centre
        + carry_x
        + carry_y
        - CONTROL_COST * hamilton
        + VISCOSITY * laplace
        + crowding[:, None, None, :]
    )


def density_core(centre, x_up, x_dn, a_up, a_dn, control, control_up, control_dn, speed_x, speed_y):
    along_x = speed_x[None, :, None, None]
    along_y = speed_y[None, None, :, None]
    carry_x = jnp.where(along_x > 0, along_x * (centre - x_dn), along_x * (x_up - centre))
    behind_y = centre - jnp.roll(centre, 1, 3)
    ahead_y = jnp.roll(centre, -1, 3) - centre
    carry_y = jnp.where(along_y > 0, along_y * behind_y, along_y * ahead_y)
    speed_up = -CONTROL_COST * (control_up - control)
    speed_dn = -CONTROL_COST * (control - control_dn)
    flux_up = jnp.maximum(speed_up, 0.0) * centre + jnp.minimum(speed_up, 0.0) * a_up
    flux_dn = jnp.maximum(speed_dn, 0.0) * a_dn + jnp.minimum(speed_dn, 0.0) * centre
    b_up = along_second(centre, 1)
    b_dn = along_second(centre, -1)
    side_up = -CONTROL_COST * (along_second(control, 1) - control)
    side_dn = -CONTROL_COST * (control - along_second(control, -1))
    flux_right = jnp.maximum(side_up, 0.0) * centre + jnp.minimum(side_up, 0.0) * b_up
    flux_left = jnp.maximum(side_dn, 0.0) * b_dn + jnp.minimum(side_dn, 0.0) * centre
    spread = VISCOSITY * (a_up + a_dn - 2.0 * centre + b_up + b_dn - 2.0 * centre)
    return centre - carry_x - carry_y - (flux_up - flux_dn) - (flux_right - flux_left) + spread


def velocity_rows(field, from_low, from_high, bottom, summit):
    lower = jnp.concatenate([jnp.where(bottom, field[:, :1], from_low), field[:, :-1]], 1)
    upper = jnp.concatenate([field[:, 1:], jnp.where(summit, field[:, -1:], from_high)], 1)
    return (upper, lower)


def body(value_next, density):
    row_count = value_next.shape[1]
    grid_v = value_next.shape[2]
    vel_place = lax.axis_index("vel")
    vel_count = lax.axis_size("vel")
    partial_mass = jnp.sum(density, axis=(1, 2))
    mass = lax.psum(partial_mass, "vel") / (grid_v * grid_v)
    crowding = CROWDING * mass * mass
    speed_y = speeds(0, grid_v, grid_v)
    speed_x = speeds(vel_place * row_count, row_count, grid_v)
    negative = vel_place < vel_count // 2
    from_below = from_behind(jnp.where(negative, value_next[-1:], density[-1:]), "pos", 1)
    from_above = from_behind(jnp.where(negative, density[:1], value_next[:1]), "pos", -1)
    below_value, below_density = (from_below, from_below)
    above_value, above_density = (from_above, from_above)
    value_x_dn = jnp.concatenate([below_value, value_next[:-1]], 0)
    value_x_up = jnp.concatenate([value_next[1:], above_value], 0)
    density_x_dn = jnp.concatenate([below_density, density[:-1]], 0)
    density_x_up = jnp.concatenate([density[1:], above_density], 0)
    bottom = vel_place == 0
    summit = vel_place == vel_count - 1
    low_value, low_density = passed_along((value_next[:, -1:], density[:, -1:]), "vel", 1)
    high_value, high_density = passed_along((value_next[:, :1], density[:, :1]), "vel", -1)
    value_a_up, value_a_dn = velocity_rows(value_next, low_value, high_value, bottom, summit)
    density_a_up, density_a_dn = velocity_rows(density, low_density, high_density, bottom, summit)
    value_now = value_core(
        value_next, value_x_up, value_x_dn, value_a_up, value_a_dn, speed_x, speed_y, crowding
    )
    low_control = passed_along(value_now[:, -1:], "vel", 1)
    high_control = passed_along(value_now[:, :1], "vel", -1)
    control_up, control_dn = velocity_rows(value_now, low_control, high_control, bottom, summit)
    density_next = density_core(
        density,
        density_x_up,
        density_x_dn,
        density_a_up,
        density_a_dn,
        value_now,
        control_up,
        control_dn,
        speed_x,
        speed_y,
    )
    return (value_now, density_next)


def solution(mesh):
    placed = (P("pos", "vel", None, None), P("pos", "vel", None, None))
    return jax.shard_map(
        body,
        mesh=mesh,
        in_specs=placed,
        out_specs=(P("pos", "vel", None, None), P("pos", "vel", None, None)),
        check_vma=False,
    )
```

profile of v0, /device:TPU:0, one launch (start us, length us, event | category | flops | bytes accessed | tf_op | source)
XLA Modules:
  0.0 161.5 jit_solution(2821520289339802891)
XLA Ops:
  0.6 1.9 %fusion.40 = (f32[2,1,64,512]{3,2,1,0:T(8,128)}, f32[2,1,64,512]{3,2,1,0:T(8,128)}) fusion(f32[2,16,64,512]{3,2,1,0:T(8,128)} %param.2), kind=kLoop, calls=%fused_computation.75 | loop fusion | bytes 1048576 | tf_op jit(solution)/shard_map/slice | solution.py:112
  2.5 2.4 %collective-permute-start.2 = (f32[2,1,64,512]{3,2,1,0:T(8,128)}, f32[2,1,64,512]{3,2,1,0:T(8,128)S(1)}, u32[]{:S(2)}, u32[]{:S(2)}) collective-permute-start(f32[2,1,64,512]{3,2,1,0:T(8,128)} %get-tuple-element.34), channel_id=1, source_target_pairs={{0,8},{8,16},{16,24},{1,9},{9,17},{17,25},{2,10},{10,18},{18,26},{... | collective-permute-start | bytes 786440 | tf_op jit(solution)/shard_map/ppermute | solution.py:21
  4.9 1.3 collective-permute-start.3
  6.2 8.4 %broadcast_select_fusion.1 = (f32[1,16,64,512]{3,2,1,0:T(8,128)}, f32[1,16,64,512]{3,2,1,0:T(8,128)}, f32[1,16,64,512]{3,2,1,0:T(8,128)}, f32[1,16,64,512]{3,2,1...) fusion(pred[]{:T(512)S(6)} %lt.3, f32[2,16,64,512]{3,2,1,0:T(8,128)} %param.2, ...), kind=kLoop, calls=%fused_computation.51 | loop fusion | flops 1048576 | bytes 20971520 | tf_op jit(solution)/shard_map/jit(_where)/select_n | solution.py:103
  14.6 5.4 %collective-permute-start = (f32[1,16,64,512]{3,2,1,0:T(8,128)}, f32[1,16,64,512]{3,2,1,0:T(8,128)}, u32[]{:S(2)}, u32[]{:S(2)}) collective-permute-start(f32[1,16,64,512]{3,2,1,0:T(8,128)} %get-tuple-element.2), channel_id=1, source_target_pairs={{1,0},{2,1},{3,2},{4,3},{5,4},{6,5},{7,6},{0,7},{9,8},{10,9},{11,1... | collective-permute-start | bytes 6291464 | tf_op jit(solution)/shard_map/ppermute | solution.py:15
  20.0 0.8 fusion.33
  20.8 1.3 collective-permute-start.5
  22.1 4.2 %fusion.43 = (f32[2,16,63,512]{3,2,1,0:T(8,128)}, f32[2,16,63,512]{3,2,1,0:T(8,128)}) fusion(f32[2,16,64,512]{3,2,1,0:T(8,128)S(1)} %copy-done.3), kind=kLoop, calls=%fused_computation.78 | loop fusion | bytes 16515072 | tf_op jit(solution)/shard_map/jit(_roll_static)/slice | solution.py:30
  26.4 5.0 %fusion.45 = (f32[2,16,64,511]{3,2,1,0:T(8,128)}, f32[2,16,64,511]{3,2,1,0:T(8,128)}) fusion(f32[2,16,64,512]{3,2,1,0:T(8,128)S(1)} %copy-done.3), kind=kLoop, calls=%fused_computation.80 | loop fusion | bytes 16744448 | tf_op jit(solution)/shard_map/jit(_roll_static)/slice | solution.py:41
  31.3 4.1 %fusion.41 = (f32[2,15,64,512]{3,2,1,0:T(8,128)}, f32[2,15,64,512]{3,2,1,0:T(8,128)}) fusion(f32[2,16,64,512]{3,2,1,0:T(8,128)S(1)} %copy-done.3), kind=kLoop, calls=%fused_computation.76 | loop fusion | bytes 15728640 | tf_op jit(solution)/shard_map/slice | solution.py:86
  35.5 1.4 fusion.44
  37.0 4.2 %fusion.32 = (f32[2,15,64,512]{3,2,1,0:T(8,128)}, f32[2,15,64,512]{3,2,1,0:T(8,128)}) fusion(f32[2,16,64,512]{3,2,1,0:T(8,128)S(1)} %copy-done), kind=kLoop, calls=%fused_computation.67 | loop fusion | bytes 15728640 | tf_op jit(solution)/shard_map/slice | solution.py:87
  41.2 1.7 %fusion.39 = (f32[2,16,64,1]{3,2,1,0:T(8,128)}, f32[2,16,64,1]{3,2,1,0:T(8,128)}) fusion(f32[2,16,64,512]{3,2,1,0:T(8,128)S(1)} %copy-done), kind=kLoop, calls=%fused_computation.74 | loop fusion | bytes 32768 | tf_op jit(solution)/shard_map/jit(_roll_static)/slice | solution.py:69
  43.6 2.5 %reduce_sum.9 = f32[2,512]{1,0:T(2,128)S(1)} reduce(f32[2,16,64,512]{3,2,1,0:T(8,128)} %param.3, f32[]{:T(128)} %constant.19.clone.1), dimensions={1,2}, to_apply=%region_0.0 | reduce | flops 1047552 | bytes 4198404 | tf_op jit(solution)/shard_map/reduce_sum | solution.py:96
  46.1 11.5 %psum.7 = f32[2,512]{1,0:T(2,128)S(1)} all-reduce(f32[2,512]{1,0:T(2,128)S(1)} %reduce_sum.9), channel_id=1, replica_groups=mesh['vel'=4,'pos'=8] {'vel'}, use_global_device_ids=true, to_apply=%region_1.0 | all-reduce | flops 1024 | bytes 8192 | tf_op jit(solution)/shard_map/psum | solution.py:97
  57.7 8.4 %fusion.36 = (f32[2,16,63,512]{3,2,1,0:T(8,128)}, f32[2,16,63,512]{3,2,1,0:T(8,128)}) fusion(f32[2,16,64,512]{3,2,1,0:T(8,128)} %param.3), kind=kLoop, calls=%fused_computation.71 | loop fusion | bytes 16515072 | tf_op jit(solution)/shard_map/jit(_roll_static)/slice | solution.py:30
  66.1 4.8 %fusion.38 = (f32[2,16,64,511]{3,2,1,0:T(8,128)}, f32[2,16,64,511]{3,2,1,0:T(8,128)}) fusion(f32[2,16,64,512]{3,2,1,0:T(8,128)S(1)} %copy-done.1), kind=kLoop, calls=%fused_computation.73 | loop fusion | bytes 16744448 | tf_op jit(solution)/shard_map/jit(_roll_static)/slice | solution.py:69
  71.5 2.0 %collective-permute-start.7 = (f32[2,1,64,512]{3,2,1,0:T(8,128)}, f32[2,1,64,512]{3,2,1,0:T(8,128)}, u32[]{:S(2)}, u32[]{:S(2)}) collective-permute-start(f32[2,1,64,512]{3,2,1,0:T(8,128)} %get-tuple-element.15), channel_id=1, source_target_pairs={{0,8},{8,16},{16,24},{1,9},{9,17},{17,25},{2,10},{10,18},{18,26},{... | collective-permute-start | bytes 786440 | tf_op jit(solution)/shard_map/ppermute | solution.py:21
  74.1 1.3 broadcast_select_fusion.7
  75.5 1.9 %broadcast_select_fusion.2 = (f32[2,1,64,512]{3,2,1,0:T(8,128)S(1)}, f32[2,1,64,512]{3,2,1,0:T(8,128)}) fusion(f32[2,1,64,512]{3,2,1,0:T(8,128)} %collective-permute-done.5, pred[]{:T(512)S(6)} %eq.27, f32[2,16,64,512]{3,2,1,0:T(8,128)} %param.3, f32[2,1,64,512]{3,2,1,0:T(8,128)} %collective-permute-done.7, pred[]{:T(512)S(6)} %eq.26), kind=kLoop, calls=%fused_computation.52 | loop fusion | flops 131072 | bytes 1572866 | tf_op jit(solution)/shard_map/jit(_where)/select_n | solution.py:87
  77.4 29.3 %collective-permute-done = f32[1,16,64,512]{3,2,1,0:T(8,128)} collective-permute-done((f32[1,16,64,512]{3,2,1,0:T(8,128)}, f32[1,16,64,512]{3,2,1,0:T(8,128)}, u32[]{:S(2)}, u32[]{:S(2)}) %collective-permute-start) | collective-permute-done | bytes 2097184 | tf_op jit(solution)/shard_map/ppermute | solution.py:15
  106.6 2.4 %collective-permute-done.1 = f32[1,16,64,512]{3,2,1,0:T(8,128)} collective-permute-done((f32[1,16,64,512]{3,2,1,0:T(8,128)}, f32[1,16,64,512]{3,2,1,0:T(8,128)}, u32[]{:S(2)}, u32[]{:S(2)}) %collective-permute-start.1) | collective-permute-done | bytes 2097184 | tf_op jit(solution)/shard_map/ppermute | solution.py:15
  109.0 13.4 %fusion.7 = f32[2,16,64,512]{3,2,1,0:T(8,128)S(1)} fusion(f32[2,16,64,512]{3,2,1,0:T(8,128)} %param.2, f32[1,16,64,512]{3,2,1,0:T(8,128)} %collective-permute-done.1, f32[1,16,64,512]{3,2,1,0:T(8,128)} %collective-permute-done, f32[1,16,64,512]{3,2,1,0:T(8,128)S(1)} %copy-done.8, f32[1,16,64,512]{3,2,1,0:T(8,128)S(1)} %get-tuple-element.29, ...), kind=kLoop, calls=%fused_computation.15 | loop fusion | flops 47185920 | bytes 41947664 | tf_op jit(solution)/shard_map/add | solution.py:55
  122.4 0.9 fusion.31
  123.3 4.4 %fusion.34 = (f32[2,16,63,512]{3,2,1,0:T(8,128)}, f32[2,16,63,512]{3,2,1,0:T(8,128)}) fusion(f32[2,16,64,512]{3,2,1,0:T(8,128)S(1)} %fusion.7), kind=kLoop, calls=%fused_computation.69 | loop fusion | bytes 16515072 | tf_op jit(solution)/shard_map/jit(_roll_static)/slice | solution.py:30
  127.7 1.3 collective-permute-start.4
  129.0 3.2 %collective-permute-start.6 = (f32[2,1,64,512]{3,2,1,0:T(8,128)}, f32[2,1,64,512]{3,2,1,0:T(8,128)S(1)}, u32[]{:S(2)}, u32[]{:S(2)}) collective-permute-start(f32[2,1,64,512]{3,2,1,0:T(8,128)} %get-tuple-element.9), channel_id=1, source_target_pairs={{0,8},{8,16},{16,24},{1,9},{9,17},{17,25},{2,10},{10,18},{18,26},{... | collective-permute-start | bytes 786440 | tf_op jit(solution)/shard_map/ppermute | solution.py:21
  132.2 5.0 %fusion.30 = (f32[2,15,64,512]{3,2,1,0:T(8,128)}, f32[2,15,64,512]{3,2,1,0:T(8,128)}) fusion(f32[2,16,64,512]{3,2,1,0:T(8,128)S(1)} %fusion.7), kind=kLoop, calls=%fused_computation.65 | loop fusion | bytes 15728640 | tf_op jit(solution)/shard_map/slice | solution.py:87
  137.6 0.9 copy-done.5
  138.5 1.2 copy-done.6
  139.7 1.2 copy-done.7
  140.9 20.6 %fusion.15 = f32[2,16,64,512]{3,2,1,0:T(8,128)} fusion(f32[2,16,64,512]{3,2,1,0:T(8,128)S(1)} %copy-done.2, f32[1,16,64,512]{3,2,1,0:T(8,128)} %collective-permute-done.1, f32[1,16,64,512]{3,2,1,0:T(8,128)} %collective-permute-done, f32[1,16,64,512]{3,2,1,0:T(8,128)} %get-tuple-element.31, f32[1,16,64,512]{3,2,1,0:T(8,128)} %get-tuple-element.28, ...), kind=kLoop, calls=%fused_computation.23 | loop fusion | flops 71303168 | bytes 62915088 | tf_op jit(solution)/shard_map/add | solution.py:82
  (46 shorter events, 2.4 us)
Async XLA Ops:
  2.5 69.0 %collective-permute-start.2 = (f32[2,1,64,512]{3,2,1,0:T(8,128)}, f32[2,1,64,512]{3,2,1,0:T(8,128)S(1)}, u32[]{:S(2)}, u32[]{:S(2)}) collective-permute-start(f32[2,1,64,512]{3,2,1,0:T(8,128)} %get-tuple-element.34), channel_id=1, source_target_pairs={{0,8},{8,16},{16,24},{1,9},{9,17},{17,25},{2,10},{10,18},{18,26},{... | collective-permute-start | bytes 786440 | tf_op jit(solution)/shard_map/ppermute | solution.py:21
  4.9 69.2 %collective-permute-start.3 = (f32[2,1,64,512]{3,2,1,0:T(8,128)}, f32[2,1,64,512]{3,2,1,0:T(8,128)}, u32[]{:S(2)}, u32[]{:S(2)}) collective-permute-start(f32[2,1,64,512]{3,2,1,0:T(8,128)} %get-tuple-element.35), channel_id=1, source_target_pairs={{8,0},{16,8},{24,16},{9,1},{17,9},{25,17},{10,2},{18,10},{26,18},{... | collective-permute-start | bytes 786440 | tf_op jit(solution)/shard_map/ppermute | solution.py:21
  6.2 13.8 %copy-start = (f32[2,16,64,512]{3,2,1,0:T(8,128)S(1)}, f32[2,16,64,512]{3,2,1,0:T(8,128)}, u32[]{:S(2)}) copy-start(f32[2,16,64,512]{3,2,1,0:T(8,128)} %param.3) | copy-start | bytes 12582916
  6.2 16.0 %copy-start.3 = (f32[2,16,64,512]{3,2,1,0:T(8,128)S(1)}, f32[2,16,64,512]{3,2,1,0:T(8,128)}, u32[]{:S(2)}) copy-start(f32[2,16,64,512]{3,2,1,0:T(8,128)} %param.2) | copy-start | bytes 12582916
  14.6 92.0 %collective-permute-start = (f32[1,16,64,512]{3,2,1,0:T(8,128)}, f32[1,16,64,512]{3,2,1,0:T(8,128)}, u32[]{:S(2)}, u32[]{:S(2)}) collective-permute-start(f32[1,16,64,512]{3,2,1,0:T(8,128)} %get-tuple-element.2), channel_id=1, source_target_pairs={{1,0},{2,1},{3,2},{4,3},{5,4},{6,5},{7,6},{0,7},{9,8},{10,9},{11,1... | collective-permute-start | bytes 6291464 | tf_op jit(solution)/shard_map/ppermute | solution.py:15
  20.0 89.0 %collective-permute-start.1 = (f32[1,16,64,512]{3,2,1,0:T(8,128)}, f32[1,16,64,512]{3,2,1,0:T(8,128)}, u32[]{:S(2)}, u32[]{:S(2)}) collective-permute-start(f32[1,16,64,512]{3,2,1,0:T(8,128)} %get-tuple-element.3), channel_id=1, source_target_pairs={{7,0},{0,1},{1,2},{2,3},{3,4},{4,5},{5,6},{6,7},{15,8},{8,9},{9,10... | collective-permute-start | bytes 6291464 | tf_op jit(solution)/shard_map/ppermute | solution.py:15
  20.8 54.6 %collective-permute-start.5 = (f32[2,1,64,512]{3,2,1,0:T(8,128)}, f32[2,1,64,512]{3,2,1,0:T(8,128)}, u32[]{:S(2)}, u32[]{:S(2)}) collective-permute-start(f32[2,1,64,512]{3,2,1,0:T(8,128)} %get-tuple-element.14), channel_id=1, source_target_pairs={{8,0},{16,8},{24,16},{9,1},{17,9},{25,17},{10,2},{18,10},{26,18},{... | collective-permute-start | bytes 786440 | tf_op jit(solution)/shard_map/ppermute | solution.py:21
  57.6 8.4 %copy-start.1 = (f32[2,16,64,512]{3,2,1,0:T(8,128)S(1)}, f32[2,16,64,512]{3,2,1,0:T(8,128)}, u32[]{:S(2)}) copy-start(f32[2,16,64,512]{3,2,1,0:T(8,128)} %param.3) | copy-start | bytes 12582916
  71.5 3.9 %collective-permute-start.7 = (f32[2,1,64,512]{3,2,1,0:T(8,128)}, f32[2,1,64,512]{3,2,1,0:T(8,128)}, u32[]{:S(2)}, u32[]{:S(2)}) collective-permute-start(f32[2,1,64,512]{3,2,1,0:T(8,128)} %get-tuple-element.15), channel_id=1, source_target_pairs={{0,8},{8,16},{16,24},{1,9},{9,17},{17,25},{2,10},{10,18},{18,26},{... | collective-permute-start | bytes 786440 | tf_op jit(solution)/shard_map/ppermute | solution.py:21
  74.1 34.9 %copy-start.8 = (f32[1,16,64,512]{3,2,1,0:T(8,128)S(1)}, f32[1,16,64,512]{3,2,1,0:T(8,128)}, u32[]{:S(2)}) copy-start(f32[1,16,64,512]{3,2,1,0:T(8,128)} %get-tuple-element.30) | copy-start | bytes 6291460
  122.4 15.1 %copy-start.4 = (f32[2,16,64,512]{3,2,1,0:T(8,128)}, f32[2,16,64,512]{3,2,1,0:T(8,128)S(1)}, u32[]{:S(2)}) copy-start(f32[2,16,64,512]{3,2,1,0:T(8,128)S(1)} %fusion.7) | copy-start | bytes 12582916
  123.3 14.2 %copy-start.9 = (f32[2,16,64,1]{3,2,1,0:T(8,128)S(1)}, f32[2,16,64,1]{3,2,1,0:T(8,128)}, u32[]{:S(2)}) copy-start(f32[2,16,64,1]{3,2,1,0:T(8,128)} %get-tuple-element.26) | copy-start | bytes 24580
  127.7 9.7 %collective-permute-start.4 = (f32[2,1,64,512]{3,2,1,0:T(8,128)}, f32[2,1,64,512]{3,2,1,0:T(8,128)S(1)}, u32[]{:S(2)}, u32[]{:S(2)}) collective-permute-start(f32[2,1,64,512]{3,2,1,0:T(8,128)} %get-tuple-element.8), channel_id=1, source_target_pairs={{8,0},{16,8},{24,16},{9,1},{17,9},{25,17},{10,2},{18,10},{26,18},{... | collective-permute-start | bytes 786440 | tf_op jit(solution)/shard_map/ppermute | solution.py:21
  128.9 8.6 %copy-start.10 = (f32[2,1,64,512]{3,2,1,0:T(8,128)S(1)}, f32[2,1,64,512]{3,2,1,0:T(8,128)}, u32[]{:S(2)}) copy-start(f32[2,1,64,512]{3,2,1,0:T(8,128)} %get-tuple-element.13) | copy-start | bytes 786436
  129.0 8.6 %copy-start.11 = (f32[2,16,1,512]{3,2,1,0:T(1,128)S(1)}, f32[2,16,1,512]{3,2,1,0:T(1,128)}, u32[]{:S(2)}) copy-start(f32[2,16,1,512]{3,2,1,0:T(1,128)} %get-tuple-element.22) | copy-start | bytes 196612
  129.0 8.6 %copy-start.12 = (f32[2,16,1,512]{3,2,1,0:T(1,128)S(1)}, f32[2,16,1,512]{3,2,1,0:T(1,128)}, u32[]{:S(2)}) copy-start(f32[2,16,1,512]{3,2,1,0:T(1,128)} %get-tuple-element.23) | copy-start | bytes 196612
  129.0 8.6 %copy-start.13 = (pred[64]{0:T(512)(128)(4,1)S(1)}, pred[64]{0:T(512)(128)(4,1)}, u32[]{:S(2)}) copy-start(pred[64]{0:T(512)(128)(4,1)} %get-tuple-element.46) | copy-start | bytes 196
  129.0 8.6 %copy-start.14 = (pred[64]{0:T(512)(128)(4,1)S(1)}, pred[64]{0:T(512)(128)(4,1)}, u32[]{:S(2)}) copy-start(pred[64]{0:T(512)(128)(4,1)} %get-tuple-element.47) | copy-start | bytes 196
  129.0 8.6 %copy-start.15 = (pred[64]{0:T(512)(128)(4,1)S(1)}, pred[64]{0:T(512)(128)(4,1)}, u32[]{:S(2)}) copy-start(pred[64]{0:T(512)(128)(4,1)} %broadcast_compare_fusion) | copy-start | bytes 196
  129.0 8.4 %collective-permute-start.6 = (f32[2,1,64,512]{3,2,1,0:T(8,128)}, f32[2,1,64,512]{3,2,1,0:T(8,128)S(1)}, u32[]{:S(2)}, u32[]{:S(2)}) collective-permute-start(f32[2,1,64,512]{3,2,1,0:T(8,128)} %get-tuple-element.9), channel_id=1, source_target_pairs={{0,8},{8,16},{16,24},{1,9},{9,17},{17,25},{2,10},{10,18},{18,26},{... | collective-permute-start | bytes 786440 | tf_op jit(solution)/shard_map/ppermute | solution.py:21
  132.2 5.4 %copy-start.2 = (f32[2,16,64,512]{3,2,1,0:T(8,128)S(1)}, f32[2,16,64,512]{3,2,1,0:T(8,128)}, u32[]{:S(2)}) copy-start(f32[2,16,64,512]{3,2,1,0:T(8,128)} %param.3) | copy-start | bytes 12582916
  132.2 6.3 %copy-start.5 = (f32[2,16,63,512]{3,2,1,0:T(8,128)S(1)}, f32[2,16,63,512]{3,2,1,0:T(8,128)}, u32[]{:S(2)}) copy-start(f32[2,16,63,512]{3,2,1,0:T(8,128)} %get-tuple-element.20) | copy-start | bytes 12386308
  132.2 7.5 %copy-start.6 = (f32[2,16,63,512]{3,2,1,0:T(8,128)S(1)}, f32[2,16,63,512]{3,2,1,0:T(8,128)}, u32[]{:S(2)}) copy-start(f32[2,16,63,512]{3,2,1,0:T(8,128)} %get-tuple-element.21) | copy-start | bytes 12386308
  132.2 8.7 %copy-start.7 = (f32[2,16,64,511]{3,2,1,0:T(8,128)S(1)}, f32[2,16,64,511]{3,2,1,0:T(8,128)}, u32[]{:S(2)}) copy-start(f32[2,16,64,511]{3,2,1,0:T(8,128)} %get-tuple-element.24) | copy-start | bytes 12558340
where the time goes:
time: 164 us; the launch traced here: 162 us
  local copies, waits for them, and re-layouts  51.2 us (31%)
  other arithmetic  49.5 us (30%)
  waiting for transfers between devices  31.7 us (19%)
  starting transfers between devices  16.7 us (10%)
  blocking collectives  11.5 us (7%)
    ppermute x2, waiting for transfers between devices, from_behind(): return lax.ppermute(block, axis, route)  31.7 us
    add x1, other arithmetic, density_core(): centre - carry_x - carry_y - (flux_up - flux_dn) - (flux_right - flux_left)  20.6 us
    slice x6, local copies, waits for them, and re-layouts, along_second(): rolled = jnp.roll(array, -step, 2)  17.9 us
    add x1, other arithmetic, value_core(): centre + carry_x + carry_y - CONTROL_COST * hamilton + VISCOSITY * laplace  13.4 us
    psum x1, blocking collectives, body(): mass = lax.psum(partial_mass, 'vel') / (grid_v * grid_v)  11.5 us
    ppermute x6, starting transfers between devices, passed_along(): lax.ppermute(value, axis, [(source, source + steps) for source in range(l...  11.4 us
    slice x2, local copies, waits for them, and re-layouts, velocity_rows(): field[:, 1:]  9.17 us
    select_n x1, other arithmetic, body(): jnp.where(negative, density[:1], value_next[:1])  8.45 us
  transfers between devices with their start and end apart: 8, of which 2 were waited for; matrix products, arithmetic and copies ran while one was open for 35% of the time, Pallas kernels for 0%

commit v1 on v0

v1 whole, which is shorter than its diff:
```python
import functools

import jax
import jax.numpy as jnp
from jax import lax
from jax.experimental import pallas as pl
from jax.experimental.pallas import tpu as pltpu
from jax.sharding import PartitionSpec as P

COURANT = 0.4
CONTROL_COST = 0.25
VISCOSITY = 0.15
CROWDING = 0.3

SUB = 8
VMEM_LIMIT = 48 * 1024 * 1024
ANY = pl.BlockSpec(memory_space=pl.ANY)


def is_negative():
    return lax.axis_index("vel") < lax.axis_size("vel") // 2


def slant(first, total):
    return COURANT * (jnp.abs(first.astype(jnp.float32) + 0.5 - total / 2) / (total / 2))


def start_all(copies):
    for copy in copies:
        copy.start()


def wait_all(copies):
    for copy in copies:
        copy.wait()


def copier(sems):
    count = [0]

    def copy(source, target):
        count[0] += 1
        return pltpu.make_async_copy(source, target, sems.at[count[0] - 1])

    return copy


def value_rows_kernel(begin, end, value, sent, sems):
    row = jnp.where(is_negative(), value.shape[0] - 1, 0)
    copy = copier(sems)
    half = (end - begin) // 2
    parts = ((0, half), (half, end - begin)) if half else ((0, end - begin),)
    copies = [
        copy(value.at[row, pl.ds(begin + lo, hi - lo)], sent.at[pl.ds(lo, hi - lo)])
        for lo, hi in parts
    ]
    start_all(copies)
    wait_all(copies)


def value_rows(value, begin, end):
    shape = (end - begin,) + value.shape[2:]
    return pl.pallas_call(
        functools.partial(value_rows_kernel, begin, end),
        out_shape=jax.ShapeDtypeStruct(shape, value.dtype),
        in_specs=[ANY],
        out_specs=ANY,
        scratch_shapes=[pltpu.SemaphoreType.DMA((2,))],
        cost_estimate=pl.CostEstimate(
            flops=0, transcendentals=0, bytes_accessed=8 * shape[0] * shape[1] * shape[2]
        ),
        name="value_rows",
    )(value)


def edges_kernel(cuts, value, density, low, high, *rest):
    sent, sems = rest[:-1], rest[-1]
    count, rows = value.shape[:2]
    row = jnp.where(is_negative(), 0, count - 1)
    copy = copier(sems)
    copies = []
    for k, field in enumerate((value, density)):
        copies.append(copy(field.at[:, rows - 1], low.at[k]))
        copies.append(copy(field.at[:, 0], high.at[k]))
    for (begin, end), target in zip(cuts, sent):
        copies.append(copy(density.at[row, pl.ds(begin, end - begin)], target))
    start_all(copies)
    wait_all(copies)


def edges(value, density, cuts):
    count, rows, second, width = value.shape
    edge = jax.ShapeDtypeStruct((2, count, second, width), value.dtype)
    parts = [jax.ShapeDtypeStruct((e - b, second, width), value.dtype) for b, e in cuts]
    return pl.pallas_call(
        functools.partial(edges_kernel, cuts),
        out_shape=[edge, edge, *parts],
        in_specs=[ANY, ANY],
        out_specs=[ANY] * (2 + len(cuts)),
        scratch_shapes=[pltpu.SemaphoreType.DMA((4 + len(cuts),))],
        cost_estimate=pl.CostEstimate(
            flops=0, transcendentals=0, bytes_accessed=8 * (4 * count + rows) * second * width
        ),
        name="edges",
    )(value, density)


def padded_copies(copy, field, low, high, pad, i, first, last):
    rows = field.shape[1]
    centre = copy(field.at[i], pad.at[i, pl.ds(1, rows)])
    below = (copy(field.at[i, 0], pad.at[i, 0]), low, 0)
    above = (copy(field.at[i, rows - 1], pad.at[i, rows + 1]), high, rows + 1)
    return centre, [(first, below), (last, above)]


def second_tile(ref, index, at, total):
    here = ref[*index, pl.ds(at, SUB), :]
    place = lax.broadcasted_iota(jnp.int32, here.shape, 0)
    if at + SUB < total:
        above = ref[*index, pl.ds(at + 1, SUB), :]
    else:
        above = jnp.where(place == SUB - 1, here, pltpu.roll(here, SUB - 1, 0))
    if at > 0:
        below = ref[*index, pl.ds(at - 1, SUB), :]
    else:
        below = jnp.where(place == 0, here, pltpu.roll(here, 1, 0))
    return here, above, below


def value_kernel(value, low, high, crowding, *rest):
    parts = len(rest) - 9
    halos = rest[:parts]
    value_now, low_now, high_now, pad, halo, fresh, load, edge, store = rest[parts:]
    count, rows, second, width = value.shape
    negative = is_negative()
    first = lax.axis_index("vel") == 0
    last = lax.axis_index("vel") == lax.axis_size("vel") - 1
    base = lax.axis_index("vel") * rows
    total = rows * lax.axis_size("vel")
    order = [jnp.where(negative, t, count - 1 - t) for t in range(count)]

    begin = 0
    halo_copies = []
    for k, part in enumerate(halos):
        extent = part.shape[0]
        halo_copies.append(
            pltpu.make_async_copy(part, halo.at[pl.ds(begin, extent)], load.at[count + k])
        )
        begin += extent
    start_all(halo_copies)
    centre_copies = [
        pltpu.make_async_copy(value.at[i], pad.at[i, pl.ds(1, rows)], load.at[t])
        for t, i in enumerate(order)
    ]
    start_all(centre_copies)
    below_own = pltpu.make_async_copy(value.at[:, 0], pad.at[:, 0], edge.at[0])
    below_far = pltpu.make_async_copy(low.at[0], pad.at[:, 0], edge.at[0])
    above_own = pltpu.make_async_copy(value.at[:, rows - 1], pad.at[:, rows + 1], edge.at[1])
    above_far = pltpu.make_async_copy(high.at[0], pad.at[:, rows + 1], edge.at[1])
    pl.when(first)(below_own.start)
    pl.when(jnp.logical_not(first))(below_far.start)
    pl.when(last)(above_own.start)
    pl.when(jnp.logical_not(last))(above_far.start)
    below_far.wait()
    above_far.wait()
    wait_all(halo_copies)

    stores = []
    for t, i in enumerate(order):
        centre_copies[t].wait()

        def step(a, carry, t=t, i=i):
            steep = slant(base + a, total)
            for at in range(0, second, SUB):
                here, up_w, dn_w = second_tile(pad, (i, a + 1), at, second)
                if t == 0:
                    x_near = halo[a, pl.ds(at, SUB), :]
                else:
                    x_near = pad[order[t - 1], a + 1, pl.ds(at, SUB), :]
                y_near = pltpu.roll(here, 1 if at < second // 2 else width - 1, 1)
                index = at + lax.broadcasted_iota(jnp.int32, here.shape, 0)
                up_v = pad[i, a + 2, pl.ds(at, SUB), :] - here
                dn_v = here - pad[i, a, pl.ds(at, SUB), :]
                up_w = up_w - here
                dn_w = here - dn_w
                hamilton = (
                    jnp.square(jnp.maximum(dn_v, 0.0))
                    + jnp.square(jnp.minimum(up_v, 0.0))
                    + jnp.square(jnp.maximum(dn_w, 0.0))
                    + jnp.square(jnp.minimum(up_w, 0.0))
                )
                laplace = up_v - dn_v + up_w - dn_w
                fresh[i, a, pl.ds(at, SUB), :] = (
                    here
                    + steep * (x_near - here)
                    + slant(index, second) * (y_near - here)
                    - (0.5 * CONTROL_COST) * hamilton
                    + VISCOSITY * laplace
                    + crowding[pl.ds(i, 1), :]
                )
            return carry

        lax.fori_loop(0, rows, step, 0)
        stores.append(pltpu.make_async_copy(fresh.at[i], value_now.at[i], store.at[t]))
        stores[-1].start()
    stores.append(pltpu.make_async_copy(fresh.at[:, rows - 1], low_now, store.at[count]))
    stores.append(pltpu.make_async_copy(fresh.at[:, 0], high_now, store.at[count + 1]))
    start_all(stores[count:])
    wait_all(stores)


def value_step(value, low, high, crowding, halos):
    count, rows, second, width = value.shape
    cells = count * rows * second * width
    edge = jax.ShapeDtypeStruct((count, second, width), value.dtype)
    return pl.pallas_call(
        value_kernel,
        out_shape=[jax.ShapeDtypeStruct(value.shape, value.dtype), edge, edge],
        in_specs=[ANY, ANY, ANY, pl.BlockSpec(memory_space=pltpu.VMEM)] + [ANY] * len(halos),
        out_specs=[ANY] * 3,
        scratch_shapes=[
            pltpu.VMEM((count, rows + 2, second, width), value.dtype),
            pltpu.VMEM((rows, second, width), value.dtype),
            pltpu.VMEM(value.shape, value.dtype),
            pltpu.SemaphoreType.DMA((count + len(halos),)),
            pltpu.SemaphoreType.DMA((2,)),
            pltpu.SemaphoreType.DMA((count + 2,)),
        ],
        compiler_params=pltpu.CompilerParams(vmem_limit_bytes=VMEM_LIMIT),
        cost_estimate=pl.CostEstimate(
            flops=40 * cells, transcendentals=0, bytes_accessed=12 * cells
        ),
        name="value_step",
    )(value, low, high, crowding, *halos)


def density_kernel(
    density, control, low, high, low_now, high_now, out, pad, ctl, fresh, load, edge, store
):
    count, rows, second, width = density.shape
    negative = is_negative()
    first = lax.axis_index("vel") == 0
    last = lax.axis_index("vel") == lax.axis_size("vel") - 1
    base = lax.axis_index("vel") * rows
    total = rows * lax.axis_size("vel")
    order = [jnp.where(negative, count - 1 - t, t) for t in range(count)]

    centre_copies = []
    for t, i in enumerate(order):
        pair = [
            pltpu.make_async_copy(density.at[i], pad.at[i, pl.ds(1, rows)], load.at[2 * t]),
            pltpu.make_async_copy(control.at[i], ctl.at[i, pl.ds(1, rows)], load.at[2 * t + 1]),
        ]
        start_all(pair)
        centre_copies.append(pair)
    waits = []
    fields = ((density, low.at[1], high.at[1], pad), (control, low_now, high_now, ctl))
    for k, (field, below, above, padded) in enumerate(fields):
        for outer, own, far, place, sem in (
            (first, field.at[:, 0], below, 0, edge.at[2 * k]),
            (last, field.at[:, rows - 1], above, rows + 1, edge.at[2 * k + 1]),
        ):
            own_copy = pltpu.make_async_copy(own, padded.at[:, place], sem)
            far_copy = pltpu.make_async_copy(far, padded.at[:, place], sem)
            pl.when(outer)(own_copy.start)
            pl.when(jnp.logical_not(outer))(far_copy.start)
            waits.append(far_copy)
    wait_all(waits)

    stores = []
    for t, i in enumerate(order):
        wait_all(centre_copies[t])

        def step(a, carry, t=t, i=i):
            steep = slant(base + a, total)
            for at in range(0, second, SUB):
                here, up_w, dn_w = second_tile(pad, (i, a + 1), at, second)
                ctl_here, ctl_up_w, ctl_dn_w = second_tile(ctl, (i, a + 1), at, second)
                up_v = pad[i, a + 2, pl.ds(at, SUB), :]
                dn_v = pad[i, a, pl.ds(at, SUB), :]
                y_near = pltpu.roll(here, width - 1 if at < second // 2 else 1, 1)
                index = at + lax.broadcasted_iota(jnp.int32, here.shape, 0)
                if t == 0:
                    along_x = -steep * here
                else:
                    along_x = steep * (pad[order[t - 1], a + 1, pl.ds(at, SUB), :] - here)
                speed_up = -CONTROL_COST * (ctl[i, a + 2, pl.ds(at, SUB), :] - ctl_here)
                speed_dn = -CONTROL_COST * (ctl_here - ctl[i, a, pl.ds(at, SUB), :])
                flux_up = jnp.maximum(speed_up, 0.0) * here + jnp.minimum(speed_up, 0.0) * up_v
                flux_dn = jnp.maximum(speed_dn, 0.0) * dn_v + jnp.minimum(speed_dn, 0.0) * here
                side_up = -CONTROL_COST * (ctl_up_w - ctl_here)
                side_dn = -CONTROL_COST * (ctl_here - ctl_dn_w)
                flux_right = jnp.maximum(side_up, 0.0) * here + jnp.minimum(side_up, 0.0) * up_w
                flux_left = jnp.maximum(side_dn, 0.0) * dn_w + jnp.minimum(side_dn, 0.0) * here
                spread = up_v + dn_v - 2.0 * here + up_w + dn_w - 2.0 * here
                fresh[i, a, pl.ds(at, SUB), :] = (
                    here
                    + along_x
                    + slant(index, second) * (y_near - here)
                    - (flux_up - flux_dn)
                    - (flux_right - flux_left)
                    + VISCOSITY * spread
                )
            return carry

        lax.fori_loop(0, rows, step, 0)
        stores.append(pltpu.make_async_copy(fresh.at[i], out.at[i], store.at[t]))
        stores[-1].start()
    wait_all(stores)


def density_step(density, control, low, high, low_now, high_now):
    count, rows, second, width = density.shape
    cells = count * rows * second * width
    padded = pltpu.VMEM((count, rows + 2, second, width), density.dtype)
    return pl.pallas_call(
        density_kernel,
        out_shape=jax.ShapeDtypeStruct(density.shape, density.dtype),
        in_specs=[ANY] * 6,
        out_specs=ANY,
        scratch_shapes=[
            padded,
            padded,
            pltpu.VMEM(density.shape, density.dtype),
            pltpu.SemaphoreType.DMA((2 * count,)),
            pltpu.SemaphoreType.DMA((4,)),
            pltpu.SemaphoreType.DMA((count,)),
        ],
        compiler_params=pltpu.CompilerParams(vmem_limit_bytes=VMEM_LIMIT),
        cost_estimate=pl.CostEstimate(
            flops=60 * cells, transcendentals=0, bytes_accessed=12 * cells
        ),
        name="density_step",
    )(density, control, low, high, low_now, high_now)


def arrive_kernel(begin, partial, halo, out, held, near, sems):
    count, rows = partial.shape[:2]
    extent, second = halo.shape[:2]
    row = jnp.where(is_negative(), count - 1, 0)
    base = lax.axis_index("vel") * rows + begin
    total = rows * lax.axis_size("vel")
    loads = [
        pltpu.make_async_copy(partial.at[row, pl.ds(begin, extent)], held, sems.at[0]),
        pltpu.make_async_copy(halo, near, sems.at[1]),
    ]
    start_all(loads)
    wait_all(loads)

    def step(a, carry):
        held[a] = held[a] + slant(base + a, total) * near[a]
        return carry

    lax.fori_loop(0, extent, step, 0)
    back = pltpu.make_async_copy(held, out.at[row, pl.ds(begin, extent)], sems.at[2])
    back.start()
    back.wait()


def arrive(partial, halo, begin):
    block = pltpu.VMEM(halo.shape, halo.dtype)
    return pl.pallas_call(
        functools.partial(arrive_kernel, begin),
        out_shape=jax.ShapeDtypeStruct(partial.shape, partial.dtype),
        in_specs=[ANY, ANY],
        out_specs=ANY,
        scratch_shapes=[block, block, pltpu.SemaphoreType.DMA((3,))],
        input_output_aliases={0: 0},
        compiler_params=pltpu.CompilerParams(vmem_limit_bytes=VMEM_LIMIT),
        cost_estimate=pl.CostEstimate(
            flops=2 * halo.size, transcendentals=0, bytes_accessed=12 * halo.size
        ),
        name="arrive",
    )(partial, halo)


def routes(mesh):
    names = tuple(mesh.axis_names)
    sizes = [mesh.shape[name] for name in names]
    slabs, groups = mesh.shape["pos"], mesh.shape["vel"]

    def place(pos, vel):
        at = {"pos": pos % slabs, "vel": vel}
        index = 0
        for name, size in zip(names, sizes):
            index = index * size + at[name]
        return index

    value_route, density_route = [], []
    for pos in range(slabs):
        for vel in range(groups):
            onward = 1 if vel < groups // 2 else -1
            value_route.append((place(pos, vel), place(pos + onward, vel)))
            density_route.append((place(pos, vel), place(pos - onward, vel)))
    return names, value_route, density_route


def body(mesh, value_next, density):
    names, value_route, density_route = routes(mesh)
    groups = mesh.shape["vel"]
    count, rows, second, width = value_next.shape
    tail = max(1, rows // 8)
    cuts = ((0, rows - tail), (rows - tail, rows))
    onward = [(v, v + 1) for v in range(groups - 1)]
    back = [(v + 1, v) for v in range(groups - 1)]

    value_halos = []
    for begin, end in cuts:
        sent = value_rows(value_next, begin, end)
        value_halos.append(lax.ppermute(sent, names, value_route))
    low, high, *leaving = edges(value_next, density, cuts)
    low = lax.ppermute(low, "vel", onward)
    high = lax.ppermute(high, "vel", back)
    mass = lax.psum(jnp.sum(density, axis=(1, 2)), "vel") / (second * second)
    crowding = CROWDING * mass * mass

    *leaving, ready = lax.optimization_barrier((*leaving, value_halos[0]))
    value_halos[0] = ready
    density_halos = [lax.ppermute(part, names, density_route) for part in leaving]

    value_now, low_now, high_now = value_step(value_next, low, high, crowding, value_halos)
    low_now = lax.ppermute(low_now, "vel", onward)
    high_now = lax.ppermute(high_now, "vel", back)
    density_next = density_step(density, value_now, low, high, low_now, high_now)
    for (begin, _), halo in zip(cuts, density_halos):
        density_next = arrive(density_next, halo, begin)
    return value_now, density_next


def solution(mesh):
    placed = (P("pos", "vel", None, None), P("pos", "vel", None, None))
    return jax.shard_map(
        functools.partial(body, mesh),
        mesh=mesh,
        in_specs=placed,
        out_specs=placed,
        check_vma=False,
    )
```

time: 164 us -> 251 us (1.53)
  Pallas kernels: 0 us -> 190 us
  local copies, waits for them, and re-layouts: 51.2 us -> 2.73 us
  other arithmetic: 49.5 us -> 2.51 us
  waiting for transfers between devices: 31.7 us -> 19.6 us
    pallas_call x0 -> x7, Pallas kernels: none -> 190 us  [the longest x1 96.4 us: edges(): pl.pallas_call(functools.partial(edges_kernel, cuts), out_shape=[edge, ed...]
    slice x16 -> x0, local copies, waits for them, and re-layouts: 47.8 us -> none  [the longest x6 17.9 us: along_second(): rolled = jnp.roll(array, -step, 2)]
    add x2 -> x0, other arithmetic: 34 us -> none  [the longest x1 20.6 us: density_core(): centre - carry_x - carry_y - (flux_up - flux_dn) - (flux_right - flux_left)]
    ppermute x8, waiting for transfers between devices: 31.7 us -> 19.6 us  [the longest x2 16.7 us: body(): value_halos.append(lax.ppermute(sent, names, value_route))]
    select_n x4 -> x0, other arithmetic: 11.8 us -> none  [the longest x1 8.45 us: body(): jnp.where(negative, density[:1], value_next[:1])]
  transfers between devices with their start and end apart: 8 -> 8, of which waited for: 2 -> 2; matrix products, arithmetic and copies ran while one was open for 35% -> 1% of each run, Pallas kernels for 0% -> 53%
where the time goes in v1:
time: 251 us; the launch traced here: 247 us
  Pallas kernels  190 us (76%)
  waiting for transfers between devices  19.6 us (8%)
  starting transfers between devices  17.6 us (7%)
  blocking collectives  13.1 us (5%)
  local copies, waits for them, and re-layouts  2.73 us (1%)
    pallas_call x1, Pallas kernels, edges(): pl.pallas_call(functools.partial(edges_kernel, cuts), out_shape=[edge, ed...  96.4 us
    pallas_call x2, Pallas kernels, value_rows(): pl.pallas_call(functools.partial(value_rows_kernel, begin, end), out_shap...  65.8 us
    ppermute x2, waiting for transfers between devices, body(): value_halos.append(lax.ppermute(sent, names, value_route))  16.7 us
    pallas_call x1, Pallas kernels, density_step(): pl.pallas_call(density_kernel, out_shape=jax.ShapeDtypeStruct(density.sha...  13.5 us
    psum x1, blocking collectives, body(): mass = lax.psum(jnp.sum(density, axis=(1, 2)), 'vel') / (second * second)  13.1 us
    pallas_call x1, Pallas kernels, value_step(): pl.pallas_call(value_kernel, out_shape=[jax.ShapeDtypeStruct(value.shape,...  9.95 us
    ppermute x2, starting transfers between devices, body(): lax.ppermute(part, names, density_route)  8.96 us
  transfers between devices with their start and end apart: 8, of which 2 were waited for; matrix products, arithmetic and copies ran while one was open for 1% of the time, Pallas kernels for 53%

profile of v1, /device:TPU:0, one launch (start us, length us, event | category | flops | bytes accessed | tf_op | source)
XLA Modules:
  0.0 246.7 jit_solution(1187172672799622922)
XLA Ops:
  0.6 56.7 %value_rows.2 = f32[14,64,512]{2,1,0:T(8,128)} custom-call(f32[2,16,64,512]{3,2,1,0:T(8,128)} %value.7), custom_call_target="tpu_custom_call" | custom-call | bytes 3670016 | tf_op jit(solution)/shard_map/value_rows/pallas_call | solution.py:63
  57.4 3.0 %collective-permute-start.2 = (f32[14,64,512]{2,1,0:T(8,128)}, f32[14,64,512]{2,1,0:T(8,128)S(1)}, u32[]{:S(2)}, u32[]{:S(2)}) collective-permute-start(f32[14,64,512]{2,1,0:T(8,128)} %value_rows.2), channel_id=1, source_target_pairs={{0,1},{8,9},{16,23},{24,31},{1,2},{9,10},{17,16},{25,24},{2,3},{10... | collective-permute-start | bytes 5505032 | tf_op jit(solution)/shard_map/ppermute | solution.py:410
  60.3 96.4 %edges.1 = (f32[2,2,64,512]{3,2,1,0:T(8,128)}, f32[2,2,64,512]{3,2,1,0:T(8,128)}, f32[14,64,512]{2,1,0:T(8,128)}, f32[2,64,512]{2,1,0:T(8,128)}) custom-call(f32[2,16,64,512]{3,2,1,0:T(8,128)} %value.7, f32[2,16,64,512]{3,2,1,0:T(8,128)} %density.3), custom_call_target="tpu_custom_call" | custom-call | bytes 6291456 | tf_op jit(solution)/shard_map/edges/pallas_call | solution.py:95
  156.8 0.0 collective-permute-done.2.rest_0_
  156.8 0.0 copy-start.1
  156.8 1.2 copy-done.1
  158.0 3.1 %collective-permute-start.6 = (f32[14,64,512]{2,1,0:T(8,128)}, f32[14,64,512]{2,1,0:T(8,128)S(1)}, u32[]{:S(2)}, u32[]{:S(2)}) collective-permute-start(f32[14,64,512]{2,1,0:T(8,128)} %get-tuple-element.20), channel_id=1, source_target_pairs={{0,7},{8,15},{16,17},{24,25},{1,0},{9,8},{17,18},{25,26},{2,1},{10... | collective-permute-start | bytes 5505032 | tf_op jit(solution)/shard_map/ppermute | solution.py:419
  161.1 1.5 collective-permute-start
  162.6 1.3 collective-permute-start.1
  163.9 9.1 %value_rows.3 = f32[2,64,512]{2,1,0:T(8,128)} custom-call(f32[2,16,64,512]{3,2,1,0:T(8,128)} %value.7), custom_call_target="tpu_custom_call" | custom-call | bytes 524288 | tf_op jit(solution)/shard_map/value_rows/pallas_call | solution.py:63
  173.0 0.1 collective-permute-start.3
  173.0 0.0 copy-start.3
  173.0 2.5 %reduce_sum.9 = f32[2,512]{1,0:T(2,128)S(1)} reduce(f32[2,16,64,512]{3,2,1,0:T(8,128)} %density.3, f32[]{:T(128)} %constant.2.clone.1), dimensions={1,2}, to_apply=%region_0.0 | reduce | flops 1047552 | bytes 4198404 | tf_op jit(solution)/shard_map/reduce_sum | solution.py:414
  175.5 13.1 %psum.7 = f32[2,512]{1,0:T(2,128)S(1)} all-reduce(f32[2,512]{1,0:T(2,128)S(1)} %reduce_sum.9), channel_id=1, replica_groups=mesh['vel'=4,'pos'=8] {'vel'}, use_global_device_ids=true, to_apply=%region_1.0 | all-reduce | flops 1024 | bytes 8192 | tf_op jit(solution)/shard_map/psum | solution.py:414
  188.6 0.0 copy-start
  188.6 16.7 %collective-permute-done.3.rest_1_ = f32[2,64,512]{2,1,0:T(8,128)S(1)} collective-permute-done((f32[2,64,512]{2,1,0:T(8,128)}, f32[2,64,512]{2,1,0:T(8,128)S(1)}, u32[]{:S(2)}, u32[]{:S(2)}) %collective-permute-start.3) | collective-permute-done | bytes 262176 | tf_op jit(solution)/shard_map/ppermute | solution.py:410
  205.3 0.0 collective-permute-done.low
  205.3 0.0 collective-permute-done.1.high
  205.3 1.5 copy-done.2
  206.8 10.0 %value_step.1 = (f32[2,16,64,512]{3,2,1,0:T(8,128)}, f32[2,64,512]{2,1,0:T(8,128)S(1)}, f32[2,64,512]{2,1,0:T(8,128)S(1)}) custom-call(f32[2,16,64,512]{3,2,1,0:T(8,128)} %value.7, f32[2,2,64,512]{3,2,1,0:T(8,128)S(1)} %collective-permute-done.low, f32[2,2,64,512]{3,2,1,0:T(8,128)S(1)} %collective-permute-done.1.high, ...), custom_call_target="tpu_custom_call" | custom-call | flops 41943040 | bytes 12582912 | tf_op jit(solution)/shard_map/value_step/pallas_call | solution.py:216
  216.8 1.5 collective-permute-start.4
  218.3 1.3 collective-permute-start.5
  219.6 0.0 copy-done.3
  219.6 5.9 %collective-permute-start.7 = (f32[2,64,512]{2,1,0:T(8,128)S(1)}, f32[2,64,512]{2,1,0:T(8,128)S(1)}, u32[]{:S(2)}, u32[]{:S(2)}) collective-permute-start(f32[2,64,512]{2,1,0:T(8,128)S(1)} %copy-done.3), channel_id=1, source_target_pairs={{0,7},{8,15},{16,17},{24,25},{1,0},{9,8},{17,18},{25,26},{2,1},{10... | collective-permute-start | bytes 786440 | tf_op jit(solution)/shard_map/ppermute | solution.py:419
  225.5 0.0 collective-permute-done.4.low_now
  225.5 2.9 %collective-permute-done.5.high_now = f32[2,64,512]{2,1,0:T(8,128)S(1)} collective-permute-done((f32[2,64,512]{2,1,0:T(8,128)S(1)}, f32[2,64,512]{2,1,0:T(8,128)S(1)}, u32[]{:S(2)}, u32[]{:S(2)}) %collective-permute-start.5) | collective-permute-done | bytes 262176 | tf_op jit(solution)/shard_map/ppermute | solution.py:423
  228.4 0.0 copy-done
  228.4 13.5 %density_step.1.partial = f32[2,16,64,512]{3,2,1,0:T(8,128)} custom-call(f32[2,16,64,512]{3,2,1,0:T(8,128)S(1)} %copy-done, f32[2,16,64,512]{3,2,1,0:T(8,128)} %get-tuple-element.10.control, f32[2,2,64,512]{3,2,1,0:T(8,128)S(1)} %collective-permute-done.low, f32[2,2,64,512]{3,2,1,0:T(8,128)S(1)} %collective-permute-done.1.high, ...), custom_call_target="tpu_custom_call" | custom-call | flops 62914560 | bytes 12582912 | tf_op jit(solution)/shard_map/density_step/pallas_call | solution.py:316
  241.9 0.0 collective-permute-done.6.halo
  241.9 3.0 %arrive.2.partial = f32[2,16,64,512]{3,2,1,0:T(8,128)} custom-call(f32[2,16,64,512]{3,2,1,0:T(8,128)} %density_step.1.partial, f32[14,64,512]{2,1,0:T(8,128)S(1)} %collective-permute-done.6.halo), custom_call_target="tpu_custom_call", output_to_operand_aliasing={{}: (0, {})} | custom-call | flops 917504 | bytes 5505024 | tf_op jit(solution)/shard_map/arrive/pallas_call | solution.py:362
  244.9 0.0 collective-permute-done.7.halo
  244.9 1.7 arrive.3
  (2 shorter events, 0.0 us)
Async XLA Ops:
  57.4 99.4 %collective-permute-start.2 = (f32[14,64,512]{2,1,0:T(8,128)}, f32[14,64,512]{2,1,0:T(8,128)S(1)}, u32[]{:S(2)}, u32[]{:S(2)}) collective-permute-start(f32[14,64,512]{2,1,0:T(8,128)} %value_rows.2), channel_id=1, source_target_pairs={{0,1},{8,9},{16,23},{24,31},{1,2},{9,10},{17,16},{25,24},{2,3},{10... | collective-permute-start | bytes 5505032 | tf_op jit(solution)/shard_map/ppermute | solution.py:410
  156.8 1.2 copy-start.1
  158.0 83.9 %collective-permute-start.6 = (f32[14,64,512]{2,1,0:T(8,128)}, f32[14,64,512]{2,1,0:T(8,128)S(1)}, u32[]{:S(2)}, u32[]{:S(2)}) collective-permute-start(f32[14,64,512]{2,1,0:T(8,128)} %get-tuple-element.20), channel_id=1, source_target_pairs={{0,7},{8,15},{16,17},{24,25},{1,0},{9,8},{17,18},{25,26},{2,1},{10... | collective-permute-start | bytes 5505032 | tf_op jit(solution)/shard_map/ppermute | solution.py:419
  161.1 44.2 %collective-permute-start = (f32[2,2,64,512]{3,2,1,0:T(8,128)}, f32[2,2,64,512]{3,2,1,0:T(8,128)S(1)}, u32[]{:S(2)}, u32[]{:S(2)}) collective-permute-start(f32[2,2,64,512]{3,2,1,0:T(8,128)} %get-tuple-element.12), channel_id=1, source_target_pairs={{0,8},{8,16},{16,24},{1,9},{9,17},{17,25},{2,10},{10,18},{18,26},{... | collective-permute-start | bytes 1572872 | tf_op jit(solution)/shard_map/ppermute | solution.py:412
  162.6 42.7 %collective-permute-start.1 = (f32[2,2,64,512]{3,2,1,0:T(8,128)}, f32[2,2,64,512]{3,2,1,0:T(8,128)S(1)}, u32[]{:S(2)}, u32[]{:S(2)}) collective-permute-start(f32[2,2,64,512]{3,2,1,0:T(8,128)} %get-tuple-element.13), channel_id=1, source_target_pairs={{8,0},{16,8},{24,16},{9,1},{17,9},{25,17},{10,2},{18,10},{26,18},{... | collective-permute-start | bytes 1572872 | tf_op jit(solution)/shard_map/ppermute | solution.py:413
  173.0 32.3 %collective-permute-start.3 = (f32[2,64,512]{2,1,0:T(8,128)}, f32[2,64,512]{2,1,0:T(8,128)S(1)}, u32[]{:S(2)}, u32[]{:S(2)}) collective-permute-start(f32[2,64,512]{2,1,0:T(8,128)} %value_rows.3), channel_id=1, source_target_pairs={{0,1},{8,9},{16,23},{24,31},{1,2},{9,10},{17,16},{25,24},{2,3},{10... | collective-permute-start | bytes 786440 | tf_op jit(solution)/shard_map/ppermute | solution.py:410
  173.0 46.6 %copy-start.3 = (f32[2,64,512]{2,1,0:T(8,128)S(1)}, f32[2,64,512]{2,1,0:T(8,128)}, u32[]{:S(2)}) copy-start(f32[2,64,512]{2,1,0:T(8,128)} %get-tuple-element.21) | copy-start | bytes 786436
  188.6 39.8 %copy-start = (f32[2,16,64,512]{3,2,1,0:T(8,128)S(1)}, f32[2,16,64,512]{3,2,1,0:T(8,128)}, u32[]{:S(2)}) copy-start(f32[2,16,64,512]{3,2,1,0:T(8,128)} %density.3) | copy-start | bytes 12582916
  205.3 1.5 copy-start.2
  216.8 8.7 %collective-permute-start.4 = (f32[2,64,512]{2,1,0:T(8,128)S(1)}, f32[2,64,512]{2,1,0:T(8,128)S(1)}, u32[]{:S(2)}, u32[]{:S(2)}) collective-permute-start(f32[2,64,512]{2,1,0:T(8,128)S(1)} %get-tuple-element.18), channel_id=1, source_target_pairs={{0,8},{8,16},{16,24},{1,9},{9,17},{17,25},{2,10},{10,18},{18,26},{... | collective-permute-start | bytes 786440 | tf_op jit(solution)/shard_map/ppermute | solution.py:422
  218.3 10.1 %collective-permute-start.5 = (f32[2,64,512]{2,1,0:T(8,128)S(1)}, f32[2,64,512]{2,1,0:T(8,128)S(1)}, u32[]{:S(2)}, u32[]{:S(2)}) collective-permute-start(f32[2,64,512]{2,1,0:T(8,128)S(1)} %get-tuple-element.19), channel_id=1, source_target_pairs={{8,0},{16,8},{24,16},{9,1},{17,9},{25,17},{10,2},{18,10},{26,18},{... | collective-permute-start | bytes 786440 | tf_op jit(solution)/shard_map/ppermute | solution.py:423
  219.6 25.3 %collective-permute-start.7 = (f32[2,64,512]{2,1,0:T(8,128)S(1)}, f32[2,64,512]{2,1,0:T(8,128)S(1)}, u32[]{:S(2)}, u32[]{:S(2)}) collective-permute-start(f32[2,64,512]{2,1,0:T(8,128)S(1)} %copy-done.3), channel_id=1, source_target_pairs={{0,7},{8,15},{16,17},{24,25},{1,0},{9,8},{17,18},{25,26},{2,1},{10... | collective-permute-start | bytes 786440 | tf_op jit(solution)/shard_map/ppermute | solution.py:419

commit v2 on v1

--- a/solution.py
+++ b/solution.py
@@ -13,8 +13,10 @@
 CROWDING = 0.3
 
 SUB = 8
-VMEM_LIMIT = 48 * 1024 * 1024
+VMEM_LIMIT = 60 * 1024 * 1024
 ANY = pl.BlockSpec(memory_space=pl.ANY)
+HBM = pl.BlockSpec(memory_space=pltpu.HBM)
+VMEM = pl.BlockSpec(memory_space=pltpu.VMEM)
 
 
 def is_negative():
@@ -35,39 +37,29 @@
         copy.wait()
 
 
-def copier(sems):
-    count = [0]
-
-    def copy(source, target):
-        count[0] += 1
-        return pltpu.make_async_copy(source, target, sems.at[count[0] - 1])
-
-    return copy
-
-
-def value_rows_kernel(begin, end, value, sent, sems):
+def value_rows_kernel(cuts, value, *rest):
+    sent, sems = rest[:-1], rest[-1]
     row = jnp.where(is_negative(), value.shape[0] - 1, 0)
-    copy = copier(sems)
-    half = (end - begin) // 2
-    parts = ((0, half), (half, end - begin)) if half else ((0, end - begin),)
     copies = [
-        copy(value.at[row, pl.ds(begin + lo, hi - lo)], sent.at[pl.ds(lo, hi - lo)])
-        for lo, hi in parts
+        pltpu.make_async_copy(value.at[row, pl.ds(begin, end - begin)], target, sems.at[k])
+        for k, ((begin, end), target) in enumerate(zip(cuts, sent))
     ]
     start_all(copies)
     wait_all(copies)
 
 
-def value_rows(value, begin, end):
-    shape = (end - begin,) + value.shape[2:]
+def value_rows(value, cuts):
+    _, rows, second, width = value.shape
+    parts = [jax.ShapeDtypeStruct((e - b, second, width), value.dtype) for b, e in cuts]
     return pl.pallas_call(
-        functools.partial(value_rows_kernel, begin, end),
-        out_shape=jax.ShapeDtypeStruct(shape, value.dtype),
-        in_specs=[ANY],
-        out_specs=ANY,
-        scratch_shapes=[pltpu.SemaphoreType.DMA((2,))],
+        functools.partial(value_rows_kernel, cuts),
+        out_shape=parts,
+        in_specs=[HBM],
+        out_specs=[VMEM] * len(cuts),
+        scratch_shapes=[pltpu.SemaphoreType.DMA((len(cuts),))],
+        compiler_params=pltpu.CompilerParams(vmem_limit_bytes=VMEM_LIMIT),
         cost_estimate=pl.CostEstimate(
-            flops=0, transcendentals=0, bytes_accessed=8 * shape[0] * shape[1] * shape[2]
+            flops=0, transcendentals=0, bytes_accessed=8 * rows * second * width
         ),
         name="value_rows",
     )(value)
@@ -77,13 +69,13 @@
     sent, sems = rest[:-1], rest[-1]
     count, rows = value.shape[:2]
     row = jnp.where(is_negative(), 0, count - 1)
-    copy = copier(sems)
-    copies = []
+    pairs = []
     for k, field in enumerate((value, density)):
-        copies.append(copy(field.at[:, rows - 1], low.at[k]))
-        copies.append(copy(field.at[:, 0], high.at[k]))
+        pairs.append((field.at[:, rows - 1], low.at[k]))
+        pairs.append((field.at[:, 0], high.at[k]))
     for (begin, end), target in zip(cuts, sent):
-        copies.append(copy(density.at[row, pl.ds(begin, end - begin)], target))
+        pairs.append((density.at[row, pl.ds(begin, end - begin)], target))
+    copies = [pltpu.make_async_copy(s, t, sems.at[k]) for k, (s, t) in enumerate(pairs)]
     start_all(copies)
     wait_all(copies)
 
@@ -95,22 +87,15 @@
     return pl.pallas_call(
         functools.partial(edges_kernel, cuts),
         out_shape=[edge, edge, *parts],
-        in_specs=[ANY, ANY],
-        out_specs=[ANY] * (2 + len(cuts)),
+        in_specs=[HBM, HBM],
+        out_specs=[VMEM] * (2 + len(cuts)),
         scratch_shapes=[pltpu.SemaphoreType.DMA((4 + len(cuts),))],
+        compiler_params=pltpu.CompilerParams(vmem_limit_bytes=VMEM_LIMIT),
         cost_estimate=pl.CostEstimate(
             flops=0, transcendentals=0, bytes_accessed=8 * (4 * count + rows) * second * width
         ),
         name="edges",
     )(value, density)
-
-
-def padded_copies(copy, field, low, high, pad, i, first, last):
-    rows = field.shape[1]
-    centre = copy(field.at[i], pad.at[i, pl.ds(1, rows)])
-    below = (copy(field.at[i, 0], pad.at[i, 0]), low, 0)
-    above = (copy(field.at[i, rows - 1], pad.at[i, rows + 1]), high, rows + 1)
-    return centre, [(first, below), (last, above)]
 
 
 def second_tile(ref, index, at, total):
@@ -216,7 +201,7 @@
     return pl.pallas_call(
         value_kernel,
         out_shape=[jax.ShapeDtypeStruct(value.shape, value.dtype), edge, edge],
-        in_specs=[ANY, ANY, ANY, pl.BlockSpec(memory_space=pltpu.VMEM)] + [ANY] * len(halos),
+        in_specs=[ANY, ANY, ANY, VMEM] + [ANY] * len(halos),
         out_specs=[ANY] * 3,
         scratch_shapes=[
             pltpu.VMEM((count, rows + 2, second, width), value.dtype),
@@ -404,18 +389,18 @@
     onward = [(v, v + 1) for v in range(groups - 1)]
     back = [(v + 1, v) for v in range(groups - 1)]
 
-    value_halos = []
-    for begin, end in cuts:
-        sent = value_rows(value_next, begin, end)
-        value_halos.append(lax.ppermute(sent, names, value_route))
+    value_halos = [
+        lax.ppermute(part, names, value_route) for part in value_rows(value_next, ((0, rows),))
+    ]
     low, high, *leaving = edges(value_next, density, cuts)
     low = lax.ppermute(low, "vel", onward)
     high = lax.ppermute(high, "vel", back)
     mass = lax.psum(jnp.sum(density, axis=(1, 2)), "vel") / (second * second)
     crowding = CROWDING * mass * mass
 
-    *leaving, ready = lax.optimization_barrier((*leaving, value_halos[0]))
-    value_halos[0] = ready
+    held = (*leaving, *value_halos, crowding, low, high)
+    *leaving, value_halo, crowding, low, high = lax.optimization_barrier(held)
+    value_halos = [value_halo]
     density_halos = [lax.ppermute(part, names, density_route) for part in leaving]
 
     value_now, low_now, high_now = value_step(value_next, low, high, crowding, value_halos)

time: 251 us -> 106 us (0.42); the launches traced: 247 us -> 105 us
  Pallas kernels: 190 us -> 37.9 us
  waiting for transfers between devices: 19.6 us -> 38.3 us
  starting transfers between devices: 17.6 us -> 11.6 us
    pallas_call x1, Pallas kernels: 96.4 us -> 3.55 us  [edges(): pl.pallas_call(functools.partial(edges_kernel, cuts), out_shape=[edge, ed...]
    pallas_call x2 -> x1, Pallas kernels: 65.8 us -> 2.93 us  [value_rows(): pl.pallas_call(functools.partial(value_rows_kernel, cuts), out_shape=part...]
    ppermute x2 -> x1, waiting for transfers between devices: 16.7 us -> 27.5 us  [body(): lax.ppermute(part, names, value_route)]
    ppermute x2, waiting for transfers between devices: 0.01 us -> 9.25 us  [body(): lax.ppermute(part, names, density_route)]
    ppermute x2, starting transfers between devices: 8.96 us -> 3.23 us  [body(): lax.ppermute(part, names, density_route)]
  transfers between devices with their start and end apart: 8 -> 7, of which waited for: 2 -> 4; matrix products, arithmetic and copies ran while one was open for 1% -> 3% of each run, Pallas kernels for 53% -> 32%
where the time goes in v2:
time: 106 us; the launch traced here: 105 us
  waiting for transfers between devices  38.3 us (36%)
  Pallas kernels  37.9 us (36%)
  blocking collectives  11.9 us (11%)
  starting transfers between devices  11.6 us (11%)
  other arithmetic  3.05 us (3%)
  local copies, waits for them, and re-layouts  1.43 us (1%)
    ppermute x1, waiting for transfers between devices, body(): lax.ppermute(part, names, value_route)  27.5 us
    pallas_call x1, Pallas kernels, density_step(): pl.pallas_call(density_kernel, out_shape=jax.ShapeDtypeStruct(density.sha...  14.8 us
    psum x1, blocking collectives, body(): mass = lax.psum(jnp.sum(density, axis=(1, 2)), 'vel') / (second * second)  11.9 us
    pallas_call x1, Pallas kernels, value_step(): pl.pallas_call(value_kernel, out_shape=[jax.ShapeDtypeStruct(value.shape,...  11.3 us
    ppermute x2, waiting for transfers between devices, body(): lax.ppermute(part, names, density_route)  9.25 us
    pallas_call x2, Pallas kernels, arrive(): pl.pallas_call(functools.partial(arrive_kernel, begin), out_shape=jax.Sha...  5.35 us
    pallas_call x1, Pallas kernels, edges(): pl.pallas_call(functools.partial(edges_kernel, cuts), out_shape=[edge, ed...  3.55 us
    ppermute x2, starting transfers between devices, body(): lax.ppermute(part, names, density_route)  3.23 us
  transfers between devices with their start and end apart: 7, of which 4 were waited for; matrix products, arithmetic and copies ran while one was open for 3% of the time, Pallas kernels for 32%

profile of v2, /device:TPU:0, one launch (start us, length us, event | category | flops | bytes accessed | tf_op | source)
XLA Modules:
  0.0 105.0 jit_solution(16808261543942066175)
XLA Ops:
  0.6 2.9 %value_rows.1 = f32[16,64,512]{2,1,0:T(8,128)} custom-call(f32[2,16,64,512]{3,2,1,0:T(8,128)} %value.5), custom_call_target="tpu_custom_call" | custom-call | bytes 4194304 | tf_op jit(solution)/shard_map/value_rows/pallas_call | solution.py:54
  3.6 3.0 %collective-permute-start = (f32[16,64,512]{2,1,0:T(8,128)}, f32[16,64,512]{2,1,0:T(8,128)S(1)}, u32[]{:S(2)}, u32[]{:S(2)}) collective-permute-start(f32[16,64,512]{2,1,0:T(8,128)} %value_rows.1), channel_id=1, source_target_pairs={{0,1},{8,9},{16,23},{24,31},{1,2},{9,10},{17,16},{25,24},{2,3},{10... | collective-permute-start | bytes 6291464 | tf_op jit(solution)/shard_map/ppermute | solution.py:393
  6.6 3.5 %edges.1 = (f32[2,2,64,512]{3,2,1,0:T(8,128)}, f32[2,2,64,512]{3,2,1,0:T(8,128)}, f32[14,64,512]{2,1,0:T(8,128)}, f32[2,64,512]{2,1,0:T(8,128)}) custom-call(f32[2,16,64,512]{3,2,1,0:T(8,128)} %value.5, f32[2,16,64,512]{3,2,1,0:T(8,128)} %density.3), custom_call_target="tpu_custom_call" | custom-call | bytes 6291456 | tf_op jit(solution)/shard_map/edges/pallas_call | solution.py:87
  10.1 1.5 %collective-permute-start.1 = (f32[2,2,64,512]{3,2,1,0:T(8,128)}, f32[2,2,64,512]{3,2,1,0:T(8,128)S(1)}, u32[]{:S(2)}, u32[]{:S(2)}) collective-permute-start(f32[2,2,64,512]{3,2,1,0:T(8,128)} %get-tuple-element.17), channel_id=1, source_target_pairs={{0,8},{8,16},{16,24},{1,9},{9,17},{17,25},{2,10},{10,18},{18,26},{... | collective-permute-start | bytes 1572872 | tf_op jit(solution)/shard_map/ppermute | solution.py:396
  11.6 1.3 %collective-permute-start.2 = (f32[2,2,64,512]{3,2,1,0:T(8,128)}, f32[2,2,64,512]{3,2,1,0:T(8,128)S(1)}, u32[]{:S(2)}, u32[]{:S(2)}) collective-permute-start(f32[2,2,64,512]{3,2,1,0:T(8,128)} %get-tuple-element.18), channel_id=1, source_target_pairs={{8,0},{16,8},{24,16},{9,1},{17,9},{25,17},{10,2},{18,10},{26,18},{... | collective-permute-start | bytes 1572872 | tf_op jit(solution)/shard_map/ppermute | solution.py:397
  12.9 2.5 %reduce_sum.9 = f32[2,512]{1,0:T(2,128)S(1)} reduce(f32[2,16,64,512]{3,2,1,0:T(8,128)} %density.3, f32[]{:T(128)} %constant.2.clone.1), dimensions={1,2}, to_apply=%region_0.0 | reduce | flops 1047552 | bytes 4198404 | tf_op jit(solution)/shard_map/reduce_sum | solution.py:398
  15.4 0.0 copy-start.6
  15.4 11.9 %psum.7 = f32[2,512]{1,0:T(2,128)S(1)} all-reduce(f32[2,512]{1,0:T(2,128)S(1)} %reduce_sum.9), channel_id=1, replica_groups=mesh['vel'=4,'pos'=8] {'vel'}, use_global_device_ids=true, to_apply=%region_1.0 | all-reduce | flops 1024 | bytes 8192 | tf_op jit(solution)/shard_map/psum | solution.py:398
  27.3 0.6 multiply_multiply_fusion.crowding
  27.9 0.0 collective-permute-done.1.low
  27.9 0.0 collective-permute-done.2.high
  27.9 0.0 copy-start.1
  27.9 27.5 %collective-permute-done.rest_0_ = f32[16,64,512]{2,1,0:T(8,128)S(1)} collective-permute-done((f32[16,64,512]{2,1,0:T(8,128)}, f32[16,64,512]{2,1,0:T(8,128)S(1)}, u32[]{:S(2)}, u32[]{:S(2)}) %collective-permute-start) | collective-permute-done | bytes 2097184 | tf_op jit(solution)/shard_map/ppermute | solution.py:393
  55.4 1.7 %collective-permute-start.5 = (f32[14,64,512]{2,1,0:T(8,128)}, f32[14,64,512]{2,1,0:T(8,128)}, u32[]{:S(2)}, u32[]{:S(2)}) collective-permute-start(f32[14,64,512]{2,1,0:T(8,128)} %get-tuple-element.26), channel_id=1, source_target_pairs={{0,7},{8,15},{16,17},{24,25},{1,0},{9,8},{17,18},{25,26},{2,1},{10... | collective-permute-start | bytes 5505032 | tf_op jit(solution)/shard_map/ppermute | solution.py:404
  57.2 0.0 copy-done
  57.2 0.0 copy-done.1
  57.2 0.0 copy-done.2
  57.2 11.3 %value_step.1 = (f32[2,16,64,512]{3,2,1,0:T(8,128)}, f32[2,64,512]{2,1,0:T(8,128)}, f32[2,64,512]{2,1,0:T(8,128)}) custom-call(f32[2,16,64,512]{3,2,1,0:T(8,128)} %value.5, f32[2,2,64,512]{3,2,1,0:T(8,128)} %copy-done, f32[2,2,64,512]{3,2,1,0:T(8,128)} %copy-done.1, f32[2,512]{1,0:T(2,128)} %multiply_multiply_fusion.crowding, f32[16,64,512]{2,1,0:T(8,128)} %copy-done.2), custom_call_target="tpu_custom_call" | custom-call | flops 41943040 | bytes 12582912 | tf_op jit(solution)/shard_map/value_step/pallas_call | solution.py:201
  68.5 1.3 %collective-permute-start.3 = (f32[2,64,512]{2,1,0:T(8,128)}, f32[2,64,512]{2,1,0:T(8,128)S(1)}, u32[]{:S(2)}, u32[]{:S(2)}) collective-permute-start(f32[2,64,512]{2,1,0:T(8,128)} %get-tuple-element.24), channel_id=1, source_target_pairs={{0,8},{8,16},{16,24},{1,9},{9,17},{17,25},{2,10},{10,18},{18,26},{... | collective-permute-start | bytes 786440 | tf_op jit(solution)/shard_map/ppermute | solution.py:407
  69.8 1.3 %collective-permute-start.4 = (f32[2,64,512]{2,1,0:T(8,128)}, f32[2,64,512]{2,1,0:T(8,128)S(1)}, u32[]{:S(2)}, u32[]{:S(2)}) collective-permute-start(f32[2,64,512]{2,1,0:T(8,128)} %get-tuple-element.25), channel_id=1, source_target_pairs={{8,0},{16,8},{24,16},{9,1},{17,9},{25,17},{10,2},{18,10},{26,18},{... | collective-permute-start | bytes 786440 | tf_op jit(solution)/shard_map/ppermute | solution.py:408
  71.1 0.0 copy-done.6
  71.1 1.5 %collective-permute-start.6 = (f32[2,64,512]{2,1,0:T(8,128)S(1)}, f32[2,64,512]{2,1,0:T(8,128)S(1)}, u32[]{:S(2)}, u32[]{:S(2)}) collective-permute-start(f32[2,64,512]{2,1,0:T(8,128)S(1)} %copy-done.6), channel_id=1, source_target_pairs={{0,7},{8,15},{16,17},{24,25},{1,0},{9,8},{17,18},{25,26},{2,1},{10... | collective-permute-start | bytes 786440 | tf_op jit(solution)/shard_map/ppermute | solution.py:404
  72.6 0.0 collective-permute-done.3.low_now
  72.6 1.5 %collective-permute-done.4.high_now = f32[2,64,512]{2,1,0:T(8,128)S(1)} collective-permute-done((f32[2,64,512]{2,1,0:T(8,128)}, f32[2,64,512]{2,1,0:T(8,128)S(1)}, u32[]{:S(2)}, u32[]{:S(2)}) %collective-permute-start.4) | collective-permute-done | bytes 262176 | tf_op jit(solution)/shard_map/ppermute | solution.py:408
  74.1 0.0 copy-done.3
  74.1 0.7 copy-done.4
  74.8 14.8 %density_step.1.partial = f32[2,16,64,512]{3,2,1,0:T(8,128)} custom-call(f32[2,16,64,512]{3,2,1,0:T(8,128)} %density.3, f32[2,16,64,512]{3,2,1,0:T(8,128)} %get-tuple-element.13.control, f32[2,2,64,512]{3,2,1,0:T(8,128)} %copy-done, f32[2,2,64,512]{3,2,1,0:T(8,128)} %copy-done.1, f32[2,64,512]{2,1,0:T(8,128)} %copy-done.3, f32[2,64,512]{2,1,0:T(8,128)} %copy-done.4), custom_call_target="tpu_custom_call" | custom-call | flops 62914560 | bytes 12582912 | tf_op jit(solution)/shard_map/density_step/pallas_call | solution.py:301
  89.6 9.1 %collective-permute-done.5.halo = f32[14,64,512]{2,1,0:T(8,128)} collective-permute-done((f32[14,64,512]{2,1,0:T(8,128)}, f32[14,64,512]{2,1,0:T(8,128)}, u32[]{:S(2)}, u32[]{:S(2)}) %collective-permute-start.5) | collective-permute-done | bytes 1835040 | tf_op jit(solution)/shard_map/ppermute | solution.py:404
  98.7 3.6 %arrive.2.partial = f32[2,16,64,512]{3,2,1,0:T(8,128)} custom-call(f32[2,16,64,512]{3,2,1,0:T(8,128)} %density_step.1.partial, f32[14,64,512]{2,1,0:T(8,128)} %collective-permute-done.5.halo), custom_call_target="tpu_custom_call", output_to_operand_aliasing={{}: (0, {})} | custom-call | flops 917504 | bytes 5505024 | tf_op jit(solution)/shard_map/arrive/pallas_call | solution.py:347
  102.3 0.2 collective-permute-done.6.halo
  102.5 0.7 copy-done.5
  103.2 1.8 %arrive.3 = f32[2,16,64,512]{3,2,1,0:T(8,128)} custom-call(f32[2,16,64,512]{3,2,1,0:T(8,128)} %arrive.2.partial, f32[2,64,512]{2,1,0:T(8,128)} %copy-done.5), custom_call_target="tpu_custom_call", output_to_operand_aliasing={{}: (0, {})} | custom-call | flops 131072 | bytes 786432 | tf_op jit(solution)/shard_map/arrive/pallas_call | solution.py:347
  (5 shorter events, 0.0 us)
Async XLA Ops:
  3.6 51.9 %collective-permute-start = (f32[16,64,512]{2,1,0:T(8,128)}, f32[16,64,512]{2,1,0:T(8,128)S(1)}, u32[]{:S(2)}, u32[]{:S(2)}) collective-permute-start(f32[16,64,512]{2,1,0:T(8,128)} %value_rows.1), channel_id=1, source_target_pairs={{0,1},{8,9},{16,23},{24,31},{1,2},{9,10},{17,16},{25,24},{2,3},{10... | collective-permute-start | bytes 6291464 | tf_op jit(solution)/shard_map/ppermute | solution.py:393
  10.1 17.8 %collective-permute-start.1 = (f32[2,2,64,512]{3,2,1,0:T(8,128)}, f32[2,2,64,512]{3,2,1,0:T(8,128)S(1)}, u32[]{:S(2)}, u32[]{:S(2)}) collective-permute-start(f32[2,2,64,512]{3,2,1,0:T(8,128)} %get-tuple-element.17), channel_id=1, source_target_pairs={{0,8},{8,16},{16,24},{1,9},{9,17},{17,25},{2,10},{10,18},{18,26},{... | collective-permute-start | bytes 1572872 | tf_op jit(solution)/shard_map/ppermute | solution.py:396
  11.6 16.3 %collective-permute-start.2 = (f32[2,2,64,512]{3,2,1,0:T(8,128)}, f32[2,2,64,512]{3,2,1,0:T(8,128)S(1)}, u32[]{:S(2)}, u32[]{:S(2)}) collective-permute-start(f32[2,2,64,512]{3,2,1,0:T(8,128)} %get-tuple-element.18), channel_id=1, source_target_pairs={{8,0},{16,8},{24,16},{9,1},{17,9},{25,17},{10,2},{18,10},{26,18},{... | collective-permute-start | bytes 1572872 | tf_op jit(solution)/shard_map/ppermute | solution.py:397
  15.4 55.8 %copy-start.6 = (f32[2,64,512]{2,1,0:T(8,128)S(1)}, f32[2,64,512]{2,1,0:T(8,128)}, u32[]{:S(2)}) copy-start(f32[2,64,512]{2,1,0:T(8,128)} %get-tuple-element.27) | copy-start | bytes 786436
  27.9 29.3 %copy-start = (f32[2,2,64,512]{3,2,1,0:T(8,128)}, f32[2,2,64,512]{3,2,1,0:T(8,128)S(1)}, u32[]{:S(2)}) copy-start(f32[2,2,64,512]{3,2,1,0:T(8,128)S(1)} %collective-permute-done.1.low) | copy-start | bytes 1572868
  27.9 29.3 %copy-start.1 = (f32[2,2,64,512]{3,2,1,0:T(8,128)}, f32[2,2,64,512]{3,2,1,0:T(8,128)S(1)}, u32[]{:S(2)}) copy-start(f32[2,2,64,512]{3,2,1,0:T(8,128)S(1)} %collective-permute-done.2.high) | copy-start | bytes 1572868
  55.4 1.8 %copy-start.2 = (f32[16,64,512]{2,1,0:T(8,128)}, f32[16,64,512]{2,1,0:T(8,128)S(1)}, u32[]{:S(2)}) copy-start(f32[16,64,512]{2,1,0:T(8,128)S(1)} %collective-permute-done.rest_0_) | copy-start | bytes 6291460
  55.4 43.3 %collective-permute-start.5 = (f32[14,64,512]{2,1,0:T(8,128)}, f32[14,64,512]{2,1,0:T(8,128)}, u32[]{:S(2)}, u32[]{:S(2)}) collective-permute-start(f32[14,64,512]{2,1,0:T(8,128)} %get-tuple-element.26), channel_id=1, source_target_pairs={{0,7},{8,15},{16,17},{24,25},{1,0},{9,8},{17,18},{25,26},{2,1},{10... | collective-permute-start | bytes 5505032 | tf_op jit(solution)/shard_map/ppermute | solution.py:404
  68.5 4.1 %collective-permute-start.3 = (f32[2,64,512]{2,1,0:T(8,128)}, f32[2,64,512]{2,1,0:T(8,128)S(1)}, u32[]{:S(2)}, u32[]{:S(2)}) collective-permute-start(f32[2,64,512]{2,1,0:T(8,128)} %get-tuple-element.24), channel_id=1, source_target_pairs={{0,8},{8,16},{16,24},{1,9},{9,17},{17,25},{2,10},{10,18},{18,26},{... | collective-permute-start | bytes 786440 | tf_op jit(solution)/shard_map/ppermute | solution.py:407
  69.8 4.3 %collective-permute-start.4 = (f32[2,64,512]{2,1,0:T(8,128)}, f32[2,64,512]{2,1,0:T(8,128)S(1)}, u32[]{:S(2)}, u32[]{:S(2)}) collective-permute-start(f32[2,64,512]{2,1,0:T(8,128)} %get-tuple-element.25), channel_id=1, source_target_pairs={{8,0},{16,8},{24,16},{9,1},{17,9},{25,17},{10,2},{18,10},{26,18},{... | collective-permute-start | bytes 786440 | tf_op jit(solution)/shard_map/ppermute | solution.py:408
  71.1 31.3 %collective-permute-start.6 = (f32[2,64,512]{2,1,0:T(8,128)S(1)}, f32[2,64,512]{2,1,0:T(8,128)S(1)}, u32[]{:S(2)}, u32[]{:S(2)}) collective-permute-start(f32[2,64,512]{2,1,0:T(8,128)S(1)} %copy-done.6), channel_id=1, source_target_pairs={{0,7},{8,15},{16,17},{24,25},{1,0},{9,8},{17,18},{25,26},{2,1},{10... | collective-permute-start | bytes 786440 | tf_op jit(solution)/shard_map/ppermute | solution.py:404
  72.6 1.5 %copy-start.3 = (f32[2,64,512]{2,1,0:T(8,128)}, f32[2,64,512]{2,1,0:T(8,128)S(1)}, u32[]{:S(2)}) copy-start(f32[2,64,512]{2,1,0:T(8,128)S(1)} %collective-permute-done.3.low_now) | copy-start | bytes 786436
  74.1 0.7 copy-start.4
  102.5 0.7 copy-start.5

commit v3 on v2

--- a/solution.py
+++ b/solution.py
@@ -13,7 +13,7 @@
 CROWDING = 0.3
 
 SUB = 8
-VMEM_LIMIT = 60 * 1024 * 1024
+VMEM_LIMIT = 18 * 1024 * 1024
 ANY = pl.BlockSpec(memory_space=pl.ANY)
 HBM = pl.BlockSpec(memory_space=pltpu.HBM)
 VMEM = pl.BlockSpec(memory_space=pltpu.VMEM)
@@ -37,47 +37,71 @@
         copy.wait()
 
 
-def value_rows_kernel(cuts, value, *rest):
-    sent, sems = rest[:-1], rest[-1]
+def in_hbm(array):
+    return pltpu.with_memory_space_constraint(array, pltpu.HBM)
+
+
+def in_vmem(array):
+    return pltpu.with_memory_space_constraint(array, pltpu.VMEM)
+
+
+def relay(pairs, held, load, store):
+    inward = [
+        pltpu.make_async_copy(source, held.at[k], load.at[k]) for k, (source, _) in enumerate(pairs)
+    ]
+    outward = [
+        pltpu.make_async_copy(held.at[k], target, store.at[k]) for k, (_, target) in enumerate(pairs)
+    ]
+    start_all(inward)
+    for come, go in zip(inward, outward):
+        come.wait()
+        go.start()
+    wait_all(outward)
+
+
+def relay_scratch(slots, second, width, dtype):
+    sems = pltpu.SemaphoreType.DMA((slots,))
+    return [pltpu.VMEM((slots, second, width), dtype), sems, sems]
+
+
+def leaving_rows(field, row, cuts, sent):
+    return [
+        (field.at[row, a], target.at[a - begin])
+        for (begin, end), target in zip(cuts, sent)
+        for a in range(begin, end)
+    ]
+
+
+def value_rows_kernel(begin, end, value, sent, *scratch):
     row = jnp.where(is_negative(), value.shape[0] - 1, 0)
-    copies = [
-        pltpu.make_async_copy(value.at[row, pl.ds(begin, end - begin)], target, sems.at[k])
-        for k, ((begin, end), target) in enumerate(zip(cuts, sent))
-    ]
-    start_all(copies)
-    wait_all(copies)
-
-
-def value_rows(value, cuts):
-    _, rows, second, width = value.shape
-    parts = [jax.ShapeDtypeStruct((e - b, second, width), value.dtype) for b, e in cuts]
-    return pl.pallas_call(
-        functools.partial(value_rows_kernel, cuts),
-        out_shape=parts,
-        in_specs=[HBM],
-        out_specs=[VMEM] * len(cuts),
-        scratch_shapes=[pltpu.SemaphoreType.DMA((len(cuts),))],
-        compiler_params=pltpu.CompilerParams(vmem_limit_bytes=VMEM_LIMIT),
-        cost_estimate=pl.CostEstimate(
-            flops=0, transcendentals=0, bytes_accessed=8 * rows * second * width
-        ),
+    relay(leaving_rows(value, row, ((begin, end),), (sent,)), *scratch)
+
+
+def value_rows(value, begin, end):
+    shape = (end - begin,) + value.shape[2:]
+    sent = jax.ShapeDtypeStruct(shape, value.dtype)
+    return pl.pallas_call(
+        functools.partial(value_rows_kernel, begin, end),
+        out_shape=sent,
+        in_specs=[ANY],
+        out_specs=ANY,
+        scratch_shapes=relay_scratch(*shape, value.dtype),
+        compiler_params=pltpu.CompilerParams(vmem_limit_bytes=VMEM_LIMIT),
+        cost_estimate=pl.CostEstimate(flops=0, transcendentals=0, bytes_accessed=8 * sent.size),
         name="value_rows",
-    )(value)
+    )(in_hbm(value))
 
 
 def edges_kernel(cuts, value, density, low, high, *rest):
-    sent, sems = rest[:-1], rest[-1]
     count, rows = value.shape[:2]
     row = jnp.where(is_negative(), 0, count - 1)
     pairs = []
     for k, field in enumerate((value, density)):
-        pairs.append((field.at[:, rows - 1], low.at[k]))
-        pairs.append((field.at[:, 0], high.at[k]))
-    for (begin, end), target in zip(cuts, sent):
-        pairs.append((density.at[row, pl.ds(begin, end - begin)], target))
-    copies = [pltpu.make_async_copy(s, t, sems.at[k]) for k, (s, t) in enumerate(pairs)]
-    start_all(copies)
-    wait_all(copies)
+        for i in range(count):
+            pairs.append((field.at[i, rows - 1], low.at[k, i]))
+            pairs.append((field.at[i, 0], high.at[k, i]))
+    pairs += leaving_rows(density, row, cuts, rest[: len(cuts)])
+    relay(pairs, *rest[len(cuts) :])
 
 
 def edges(value, density, cuts):
@@ -87,15 +111,15 @@
     return pl.pallas_call(
         functools.partial(edges_kernel, cuts),
         out_shape=[edge, edge, *parts],
-        in_specs=[HBM, HBM],
-        out_specs=[VMEM] * (2 + len(cuts)),
-        scratch_shapes=[pltpu.SemaphoreType.DMA((4 + len(cuts),))],
+        in_specs=[ANY, ANY],
+        out_specs=[ANY] * (2 + len(cuts)),
+        scratch_shapes=relay_scratch(4 * count + rows, second, width, value.dtype),
         compiler_params=pltpu.CompilerParams(vmem_limit_bytes=VMEM_LIMIT),
         cost_estimate=pl.CostEstimate(
             flops=0, transcendentals=0, bytes_accessed=8 * (4 * count + rows) * second * width
         ),
         name="edges",
-    )(value, density)
+    )(in_hbm(value), in_hbm(density))
 
 
 def second_tile(ref, index, at, total):
@@ -216,11 +240,11 @@
             flops=40 * cells, transcendentals=0, bytes_accessed=12 * cells
         ),
         name="value_step",
-    )(value, low, high, crowding, *halos)
+    )(in_hbm(value), low, high, crowding, *halos)
 
 
 def density_kernel(
-    density, control, low, high, low_now, high_now, out, pad, ctl, fresh, load, edge, store
+    density, control, low, high, low_now, high_now, out, rest, pad, ctl, fresh, load, edge, store
 ):
     count, rows, second, width = density.shape
     negative = is_negative()
@@ -291,18 +315,24 @@
         lax.fori_loop(0, rows, step, 0)
         stores.append(pltpu.make_async_copy(fresh.at[i], out.at[i], store.at[t]))
         stores[-1].start()
+        if t == 0:
+            extent = rest.shape[0]
+            rest[...] = fresh[i, pl.ds(rows - extent, extent)]
     wait_all(stores)
 
 
-def density_step(density, control, low, high, low_now, high_now):
+def density_step(density, control, low, high, low_now, high_now, extent):
     count, rows, second, width = density.shape
     cells = count * rows * second * width
     padded = pltpu.VMEM((count, rows + 2, second, width), density.dtype)
     return pl.pallas_call(
         density_kernel,
-        out_shape=jax.ShapeDtypeStruct(density.shape, density.dtype),
+        out_shape=[
+            jax.ShapeDtypeStruct(density.shape, density.dtype),
+            pltpu.VMEM((extent, second, width), density.dtype),
+        ],
         in_specs=[ANY] * 6,
-        out_specs=ANY,
+        out_specs=[ANY, VMEM],
         scratch_shapes=[
             padded,
             padded,
@@ -316,7 +346,7 @@
             flops=60 * cells, transcendentals=0, bytes_accessed=12 * cells
         ),
         name="density_step",
-    )(density, control, low, high, low_now, high_now)
+    )(in_hbm(density), in_hbm(control), low, high, low_now, high_now)
 
 
 def arrive_kernel(begin, partial, halo, out, held, near, sems):
@@ -325,21 +355,18 @@
     row = jnp.where(is_negative(), count - 1, 0)
     base = lax.axis_index("vel") * rows + begin
     total = rows * lax.axis_size("vel")
-    loads = [
-        pltpu.make_async_copy(partial.at[row, pl.ds(begin, extent)], held, sems.at[0]),
-        pltpu.make_async_copy(halo, near, sems.at[1]),
-    ]
+    loads = []
+    for a in range(extent):
+        loads.append(pltpu.make_async_copy(partial.at[row, begin + a], held.at[a], sems.at[a]))
+        loads.append(pltpu.make_async_copy(halo.at[a], near.at[a], sems.at[extent + a]))
     start_all(loads)
-    wait_all(loads)
-
-    def step(a, carry):
+    stores = []
+    for a in range(extent):
+        wait_all(loads[2 * a : 2 * a + 2])
         held[a] = held[a] + slant(base + a, total) * near[a]
-        return carry
-
-    lax.fori_loop(0, extent, step, 0)
-    back = pltpu.make_async_copy(held, out.at[row, pl.ds(begin, extent)], sems.at[2])
-    back.start()
-    back.wait()
+        stores.append(pltpu.make_async_copy(held.at[a], out.at[row, begin + a], sems.at[2 * extent + a]))
+        stores[-1].start()
+    wait_all(stores)
 
 
 def arrive(partial, halo, begin):
@@ -349,14 +376,44 @@
         out_shape=jax.ShapeDtypeStruct(partial.shape, partial.dtype),
         in_specs=[ANY, ANY],
         out_specs=ANY,
-        scratch_shapes=[block, block, pltpu.SemaphoreType.DMA((3,))],
+        scratch_shapes=[block, block, pltpu.SemaphoreType.DMA((3 * halo.shape[0],))],
         input_output_aliases={0: 0},
         compiler_params=pltpu.CompilerParams(vmem_limit_bytes=VMEM_LIMIT),
         cost_estimate=pl.CostEstimate(
             flops=2 * halo.size, transcendentals=0, bytes_accessed=12 * halo.size
         ),
         name="arrive",
-    )(partial, halo)
+    )(in_hbm(partial), halo)
+
+
+def arrive_last_kernel(partial, rest, halo, out, held, sem):
+    count, rows = partial.shape[:2]
+    extent = halo.shape[0]
+    row = jnp.where(is_negative(), count - 1, 0)
+    base = lax.axis_index("vel") * rows + rows - extent
+    total = rows * lax.axis_size("vel")
+    copies = []
+    for a in range(extent):
+        held[a] = rest[a] + slant(base + a, total) * halo[a]
+        copies.append(pltpu.make_async_copy(held.at[a], out.at[row, rows - extent + a], sem.at[a]))
+        copies[-1].start()
+    wait_all(copies)
+
+
+def arrive_last(partial, rest, halo):
+    return pl.pallas_call(
+        arrive_last_kernel,
+        out_shape=jax.ShapeDtypeStruct(partial.shape, partial.dtype),
+        in_specs=[ANY, VMEM, VMEM],
+        out_specs=ANY,
+        scratch_shapes=[pltpu.VMEM(halo.shape, halo.dtype), pltpu.SemaphoreType.DMA((halo.shape[0],))],
+        input_output_aliases={0: 0},
+        compiler_params=pltpu.CompilerParams(vmem_limit_bytes=VMEM_LIMIT),
+        cost_estimate=pl.CostEstimate(
+            flops=2 * halo.size, transcendentals=0, bytes_accessed=8 * halo.size
+        ),
+        name="arrive_last",
+    )(in_hbm(partial), in_vmem(rest), in_vmem(halo))
 
 
 def routes(mesh):
@@ -389,9 +446,7 @@
     onward = [(v, v + 1) for v in range(groups - 1)]
     back = [(v + 1, v) for v in range(groups - 1)]
 
-    value_halos = [
-        lax.ppermute(part, names, value_route) for part in value_rows(value_next, ((0, rows),))
-    ]
+    value_halos = [lax.ppermute(value_rows(value_next, 0, rows), names, value_route)]
     low, high, *leaving = edges(value_next, density, cuts)
     low = lax.ppermute(low, "vel", onward)
     high = lax.ppermute(high, "vel", back)
@@ -406,9 +461,11 @@
     value_now, low_now, high_now = value_step(value_next, low, high, crowding, value_halos)
     low_now = lax.ppermute(low_now, "vel", onward)
     high_now = lax.ppermute(high_now, "vel", back)
-    density_next = density_step(density, value_now, low, high, low_now, high_now)
-    for (begin, _), halo in zip(cuts, density_halos):
-        density_next = arrive(density_next, halo, begin)
+    density_next, rest = density_step(
+        density, value_now, low, high, low_now, high_now, tail
+    )
+    density_next = arrive(density_next, density_halos[0], 0)
+    density_next = arrive_last(density_next, rest, density_halos[1])
     return value_now, density_next
 
 

time: 106 us -> 104 us (0.981)
    ppermute x2, waiting for transfers between devices: 9.25 us -> 12.1 us  [body(): lax.ppermute(part, names, density_route)]
    ppermute x1, waiting for transfers between devices: 27.5 us -> 25.6 us  [body(): lax.ppermute(value_rows(value_next, 0, rows), names, value_route)]
    pallas_call x1, Pallas kernels: 11.3 us -> 9.94 us  [value_step(): pl.pallas_call(value_kernel, out_shape=[jax.ShapeDtypeStruct(value.shape,...]
    pallas_call x1, Pallas kernels: 3.55 us -> 4.89 us  [edges(): pl.pallas_call(functools.partial(edges_kernel, cuts), out_shape=[edge, ed...]
    pallas_call x2 -> x1, Pallas kernels: 5.35 us -> 4.18 us  [arrive(): pl.pallas_call(functools.partial(arrive_kernel, begin), out_shape=jax.Sha...]
    pallas_call x2 -> x3, Pallas kernels: 17.7 us -> 17.9 us  [the longest x1 14.6 us: density_step(): pl.pallas_call(density_kernel, out_shape=[jax.ShapeDtypeStruct(density.sh...]
  transfers between devices with their start and end apart: 7 -> 7, of which waited for: 4 -> 3; matrix products, arithmetic and copies ran while one was open for 3% -> 2% of each run, Pallas kernels for 32% -> 33%
where the time goes in v3:
time: 104 us; the launch traced here: 103 us
  waiting for transfers between devices  38.4 us (37%)
  Pallas kernels  36.9 us (35%)
  blocking collectives  11.8 us (11%)
  starting transfers between devices  11.6 us (11%)
  other arithmetic  2.47 us (2%)
  local copies, waits for them, and re-layouts  1.24 us (1%)
    ppermute x1, waiting for transfers between devices, body(): lax.ppermute(value_rows(value_next, 0, rows), names, value_route)  25.6 us
    pallas_call x1, Pallas kernels, density_step(): pl.pallas_call(density_kernel, out_shape=[jax.ShapeDtypeStruct(density.sh...  14.6 us
    ppermute x2, waiting for transfers between devices, body(): lax.ppermute(part, names, density_route)  12.1 us
    psum x1, blocking collectives, body(): mass = lax.psum(jnp.sum(density, axis=(1, 2)), 'vel') / (second * second)  11.8 us
    pallas_call x1, Pallas kernels, value_step(): pl.pallas_call(value_kernel, out_shape=[jax.ShapeDtypeStruct(value.shape,...  9.94 us
    pallas_call x1, Pallas kernels, edges(): pl.pallas_call(functools.partial(edges_kernel, cuts), out_shape=[edge, ed...  4.89 us
    pallas_call x1, Pallas kernels, arrive(): pl.pallas_call(functools.partial(arrive_kernel, begin), out_shape=jax.Sha...  4.18 us
    ppermute x2, starting transfers between devices, body(): lax.ppermute(part, names, density_route)  3.23 us
  transfers between devices with their start and end apart: 7, of which 3 were waited for; matrix products, arithmetic and copies ran while one was open for 2% of the time, Pallas kernels for 33%

profile of v3, /device:TPU:0, one launch (start us, length us, event | category | flops | bytes accessed | tf_op | source)
XLA Modules:
  0.0 103.2 jit_solution(4139728677224807529)
XLA Ops:
  0.6 2.6 %value_rows.1 = f32[16,64,512]{2,1,0:T(8,128)} custom-call(f32[2,16,64,512]{3,2,1,0:T(8,128)} %value.5), custom_call_target="tpu_custom_call" | custom-call | bytes 4194304 | tf_op jit(solution)/shard_map/value_rows/pallas_call | solution.py:83
  3.2 3.0 %collective-permute-start = (f32[16,64,512]{2,1,0:T(8,128)}, f32[16,64,512]{2,1,0:T(8,128)S(1)}, u32[]{:S(2)}, u32[]{:S(2)}) collective-permute-start(f32[16,64,512]{2,1,0:T(8,128)} %value_rows.1), channel_id=1, source_target_pairs={{0,1},{8,9},{16,23},{24,31},{1,2},{9,10},{17,16},{25,24},{2,3},{10... | collective-permute-start | bytes 6291464 | tf_op jit(solution)/shard_map/ppermute | solution.py:449
  6.2 4.9 %edges.1 = (f32[2,2,64,512]{3,2,1,0:T(8,128)}, f32[2,2,64,512]{3,2,1,0:T(8,128)}, f32[14,64,512]{2,1,0:T(8,128)S(1)}, f32[2,64,512]{2,1,0:T(8,128)S(1)}) custom-call(f32[2,16,64,512]{3,2,1,0:T(8,128)} %value.5, f32[2,16,64,512]{3,2,1,0:T(8,128)} %density.3), custom_call_target="tpu_custom_call" | custom-call | bytes 6291456 | tf_op jit(solution)/shard_map/edges/pallas_call | solution.py:111
  11.1 0.0 copy-start
  11.1 1.2 %copy-done = f32[14,64,512]{2,1,0:T(8,128)} copy-done((f32[14,64,512]{2,1,0:T(8,128)}, f32[14,64,512]{2,1,0:T(8,128)S(1)}, u32[]{:S(2)}) %copy-start) | copy-done | bytes 1835032
  12.4 1.5 %collective-permute-start.1 = (f32[2,2,64,512]{3,2,1,0:T(8,128)}, f32[2,2,64,512]{3,2,1,0:T(8,128)S(1)}, u32[]{:S(2)}, u32[]{:S(2)}) collective-permute-start(f32[2,2,64,512]{3,2,1,0:T(8,128)} %get-tuple-element.19), channel_id=1, source_target_pairs={{0,8},{8,16},{16,24},{1,9},{9,17},{17,25},{2,10},{10,18},{18,26},{... | collective-permute-start | bytes 1572872 | tf_op jit(solution)/shard_map/ppermute | solution.py:451
  13.8 1.3 %collective-permute-start.2 = (f32[2,2,64,512]{3,2,1,0:T(8,128)}, f32[2,2,64,512]{3,2,1,0:T(8,128)S(1)}, u32[]{:S(2)}, u32[]{:S(2)}) collective-permute-start(f32[2,2,64,512]{3,2,1,0:T(8,128)} %get-tuple-element.20), channel_id=1, source_target_pairs={{8,0},{16,8},{24,16},{9,1},{17,9},{25,17},{10,2},{18,10},{26,18},{... | collective-permute-start | bytes 1572872 | tf_op jit(solution)/shard_map/ppermute | solution.py:452
  15.1 2.5 %reduce_sum.9 = f32[2,512]{1,0:T(2,128)S(1)} reduce(f32[2,16,64,512]{3,2,1,0:T(8,128)} %density.3, f32[]{:T(128)} %constant.2.clone.1), dimensions={1,2}, to_apply=%region_0.0 | reduce | flops 1047552 | bytes 4198404 | tf_op jit(solution)/shard_map/reduce_sum | solution.py:453
  17.6 11.8 %psum.7 = f32[2,512]{1,0:T(2,128)S(1)} all-reduce(f32[2,512]{1,0:T(2,128)S(1)} %reduce_sum.9), channel_id=1, replica_groups=mesh['vel'=4,'pos'=8] {'vel'}, use_global_device_ids=true, to_apply=%region_1.0 | all-reduce | flops 1024 | bytes 8192 | tf_op jit(solution)/shard_map/psum | solution.py:453
  29.4 0.0 collective-permute-done.1.low
  29.4 0.0 collective-permute-done.2.high
  29.5 25.6 %collective-permute-done.rest_0_ = f32[16,64,512]{2,1,0:T(8,128)S(1)} collective-permute-done((f32[16,64,512]{2,1,0:T(8,128)}, f32[16,64,512]{2,1,0:T(8,128)S(1)}, u32[]{:S(2)}, u32[]{:S(2)}) %collective-permute-start) | collective-permute-done | bytes 2097184 | tf_op jit(solution)/shard_map/ppermute | solution.py:449
  55.1 1.7 %collective-permute-start.5 = (f32[14,64,512]{2,1,0:T(8,128)}, f32[14,64,512]{2,1,0:T(8,128)S(1)}, u32[]{:S(2)}, u32[]{:S(2)}) collective-permute-start(f32[14,64,512]{2,1,0:T(8,128)} %copy-done), channel_id=1, source_target_pairs={{0,7},{8,15},{16,17},{24,25},{1,0},{9,8},{17,18},{25,26},{2,1},{10... | collective-permute-start | bytes 5505032 | tf_op jit(solution)/shard_map/ppermute | solution.py:459
  56.8 9.9 %value_step.1 = (f32[2,16,64,512]{3,2,1,0:T(8,128)}, f32[2,64,512]{2,1,0:T(8,128)S(1)}, f32[2,64,512]{2,1,0:T(8,128)S(1)}) custom-call(f32[2,16,64,512]{3,2,1,0:T(8,128)} %value.5, f32[2,2,64,512]{3,2,1,0:T(8,128)S(1)} %collective-permute-done.1.low, f32[2,2,64,512]{3,2,1,0:T(8,128)S(1)} %collective-permute-done.2.high, ...), custom_call_target="tpu_custom_call" | custom-call | flops 41943040 | bytes 12582912 | tf_op jit(solution)/shard_map/value_step/pallas_call | solution.py:225
  66.8 1.3 %collective-permute-start.3 = (f32[2,64,512]{2,1,0:T(8,128)S(1)}, f32[2,64,512]{2,1,0:T(8,128)S(1)}, u32[]{:S(2)}, u32[]{:S(2)}) collective-permute-start(f32[2,64,512]{2,1,0:T(8,128)S(1)} %get-tuple-element.26), channel_id=1, source_target_pairs={{0,8},{8,16},{16,24},{1,9},{9,17},{17,25},{2,10},{10,18},{18,26},{... | collective-permute-start | bytes 786440 | tf_op jit(solution)/shard_map/ppermute | solution.py:462
  68.1 1.3 %collective-permute-start.4 = (f32[2,64,512]{2,1,0:T(8,128)S(1)}, f32[2,64,512]{2,1,0:T(8,128)S(1)}, u32[]{:S(2)}, u32[]{:S(2)}) collective-permute-start(f32[2,64,512]{2,1,0:T(8,128)S(1)} %get-tuple-element.27), channel_id=1, source_target_pairs={{8,0},{16,8},{24,16},{9,1},{17,9},{25,17},{10,2},{18,10},{26,18},{... | collective-permute-start | bytes 786440 | tf_op jit(solution)/shard_map/ppermute | solution.py:463
  69.4 1.5 %collective-permute-start.6 = (f32[2,64,512]{2,1,0:T(8,128)S(1)}, f32[2,64,512]{2,1,0:T(8,128)S(1)}, u32[]{:S(2)}, u32[]{:S(2)}) collective-permute-start(f32[2,64,512]{2,1,0:T(8,128)S(1)} %get-tuple-element.31), channel_id=1, source_target_pairs={{0,7},{8,15},{16,17},{24,25},{1,0},{9,8},{17,18},{25,26},{2,1},{10... | collective-permute-start | bytes 786440 | tf_op jit(solution)/shard_map/ppermute | solution.py:459
  70.9 0.0 collective-permute-done.3.low_now
  70.9 0.6 collective-permute-done.4.high_now
  71.5 14.6 %density_step.1 = (f32[2,16,64,512]{3,2,1,0:T(8,128)}, f32[2,64,512]{2,1,0:T(8,128)S(1)}) custom-call(f32[2,16,64,512]{3,2,1,0:T(8,128)} %density.3, f32[2,16,64,512]{3,2,1,0:T(8,128)} %get-tuple-element.15.control, f32[2,2,64,512]{3,2,1,0:T(8,128)S(1)} %collective-permute-done.1.low, f32[2,2,64,512]{3,2,1,0:T(8,128)S(1)} %collective-permute-done.2.high, ...), custom_call_target="tpu_custom_call" | custom-call | flops 62914560 | bytes 12582912 | tf_op jit(solution)/shard_map/density_step/pallas_call | solution.py:328
  86.1 12.1 %collective-permute-done.5.halo = f32[14,64,512]{2,1,0:T(8,128)S(1)} collective-permute-done((f32[14,64,512]{2,1,0:T(8,128)}, f32[14,64,512]{2,1,0:T(8,128)S(1)}, u32[]{:S(2)}, u32[]{:S(2)}) %collective-permute-start.5) | collective-permute-done | bytes 1835040 | tf_op jit(solution)/shard_map/ppermute | solution.py:459
  98.2 4.2 %arrive.1.partial = f32[2,16,64,512]{3,2,1,0:T(8,128)} custom-call(f32[2,16,64,512]{3,2,1,0:T(8,128)} %get-tuple-element.28.partial, f32[14,64,512]{2,1,0:T(8,128)S(1)} %collective-permute-done.5.halo), custom_call_target="tpu_custom_call", output_to_operand_aliasing={{}: (0, {})} | custom-call | flops 917504 | bytes 5505024 | tf_op jit(solution)/shard_map/arrive/pallas_call | solution.py:374
  102.4 0.0 collective-permute-done.6.halo
  102.4 0.7 arrive_last.1
  (1 shorter events, 0.0 us)
Async XLA Ops:
  3.2 51.9 %collective-permute-start = (f32[16,64,512]{2,1,0:T(8,128)}, f32[16,64,512]{2,1,0:T(8,128)S(1)}, u32[]{:S(2)}, u32[]{:S(2)}) collective-permute-start(f32[16,64,512]{2,1,0:T(8,128)} %value_rows.1), channel_id=1, source_target_pairs={{0,1},{8,9},{16,23},{24,31},{1,2},{9,10},{17,16},{25,24},{2,3},{10... | collective-permute-start | bytes 6291464 | tf_op jit(solution)/shard_map/ppermute | solution.py:449
  11.1 1.2 %copy-start = (f32[14,64,512]{2,1,0:T(8,128)}, f32[14,64,512]{2,1,0:T(8,128)S(1)}, u32[]{:S(2)}) copy-start(f32[14,64,512]{2,1,0:T(8,128)S(1)} %get-tuple-element.29) | copy-start | bytes 5505028
  12.4 17.1 %collective-permute-start.1 = (f32[2,2,64,512]{3,2,1,0:T(8,128)}, f32[2,2,64,512]{3,2,1,0:T(8,128)S(1)}, u32[]{:S(2)}, u32[]{:S(2)}) collective-permute-start(f32[2,2,64,512]{3,2,1,0:T(8,128)} %get-tuple-element.19), channel_id=1, source_target_pairs={{0,8},{8,16},{16,24},{1,9},{9,17},{17,25},{2,10},{10,18},{18,26},{... | collective-permute-start | bytes 1572872 | tf_op jit(solution)/shard_map/ppermute | solution.py:451
  13.8 15.6 %collective-permute-start.2 = (f32[2,2,64,512]{3,2,1,0:T(8,128)}, f32[2,2,64,512]{3,2,1,0:T(8,128)S(1)}, u32[]{:S(2)}, u32[]{:S(2)}) collective-permute-start(f32[2,2,64,512]{3,2,1,0:T(8,128)} %get-tuple-element.20), channel_id=1, source_target_pairs={{8,0},{16,8},{24,16},{9,1},{17,9},{25,17},{10,2},{18,10},{26,18},{... | collective-permute-start | bytes 1572872 | tf_op jit(solution)/shard_map/ppermute | solution.py:452
  55.1 43.2 %collective-permute-start.5 = (f32[14,64,512]{2,1,0:T(8,128)}, f32[14,64,512]{2,1,0:T(8,128)S(1)}, u32[]{:S(2)}, u32[]{:S(2)}) collective-permute-start(f32[14,64,512]{2,1,0:T(8,128)} %copy-done), channel_id=1, source_target_pairs={{0,7},{8,15},{16,17},{24,25},{1,0},{9,8},{17,18},{25,26},{2,1},{10... | collective-permute-start | bytes 5505032 | tf_op jit(solution)/shard_map/ppermute | solution.py:459
  66.8 4.1 %collective-permute-start.3 = (f32[2,64,512]{2,1,0:T(8,128)S(1)}, f32[2,64,512]{2,1,0:T(8,128)S(1)}, u32[]{:S(2)}, u32[]{:S(2)}) collective-permute-start(f32[2,64,512]{2,1,0:T(8,128)S(1)} %get-tuple-element.26), channel_id=1, source_target_pairs={{0,8},{8,16},{16,24},{1,9},{9,17},{17,25},{2,10},{10,18},{18,26},{... | collective-permute-start | bytes 786440 | tf_op jit(solution)/shard_map/ppermute | solution.py:462
  68.1 3.4 %collective-permute-start.4 = (f32[2,64,512]{2,1,0:T(8,128)S(1)}, f32[2,64,512]{2,1,0:T(8,128)S(1)}, u32[]{:S(2)}, u32[]{:S(2)}) collective-permute-start(f32[2,64,512]{2,1,0:T(8,128)S(1)} %get-tuple-element.27), channel_id=1, source_target_pairs={{8,0},{16,8},{24,16},{9,1},{17,9},{25,17},{10,2},{18,10},{26,18},{... | collective-permute-start | bytes 786440 | tf_op jit(solution)/shard_map/ppermute | solution.py:463
  69.4 33.0 %collective-permute-start.6 = (f32[2,64,512]{2,1,0:T(8,128)S(1)}, f32[2,64,512]{2,1,0:T(8,128)S(1)}, u32[]{:S(2)}, u32[]{:S(2)}) collective-permute-start(f32[2,64,512]{2,1,0:T(8,128)S(1)} %get-tuple-element.31), channel_id=1, source_target_pairs={{0,7},{8,15},{16,17},{24,25},{1,0},{9,8},{17,18},{25,26},{2,1},{10... | collective-permute-start | bytes 786440 | tf_op jit(solution)/shard_map/ppermute | solution.py:459

commit v4 on v3

--- a/solution.py
+++ b/solution.py
@@ -15,8 +15,8 @@
 SUB = 8
 VMEM_LIMIT = 18 * 1024 * 1024
 ANY = pl.BlockSpec(memory_space=pl.ANY)
-HBM = pl.BlockSpec(memory_space=pltpu.HBM)
 VMEM = pl.BlockSpec(memory_space=pltpu.VMEM)
+LIGHT = pl.CostEstimate(flops=0, transcendentals=0, bytes_accessed=0)
 
 
 def is_negative():
@@ -79,7 +79,7 @@
 
 def value_rows(value, begin, end):
     shape = (end - begin,) + value.shape[2:]
-    sent = jax.ShapeDtypeStruct(shape, value.dtype)
+    sent = pltpu.HBM(shape, value.dtype)
     return pl.pallas_call(
         functools.partial(value_rows_kernel, begin, end),
         out_shape=sent,
@@ -87,7 +87,7 @@
         out_specs=ANY,
         scratch_shapes=relay_scratch(*shape, value.dtype),
         compiler_params=pltpu.CompilerParams(vmem_limit_bytes=VMEM_LIMIT),
-        cost_estimate=pl.CostEstimate(flops=0, transcendentals=0, bytes_accessed=8 * sent.size),
+        cost_estimate=LIGHT,
         name="value_rows",
     )(in_hbm(value))
 
@@ -106,8 +106,8 @@
 
 def edges(value, density, cuts):
     count, rows, second, width = value.shape
-    edge = jax.ShapeDtypeStruct((2, count, second, width), value.dtype)
-    parts = [jax.ShapeDtypeStruct((e - b, second, width), value.dtype) for b, e in cuts]
+    edge = pltpu.HBM((2, count, second, width), value.dtype)
+    parts = [pltpu.HBM((e - b, second, width), value.dtype) for b, e in cuts]
     return pl.pallas_call(
         functools.partial(edges_kernel, cuts),
         out_shape=[edge, edge, *parts],
@@ -115,9 +115,7 @@
         out_specs=[ANY] * (2 + len(cuts)),
         scratch_shapes=relay_scratch(4 * count + rows, second, width, value.dtype),
         compiler_params=pltpu.CompilerParams(vmem_limit_bytes=VMEM_LIMIT),
-        cost_estimate=pl.CostEstimate(
-            flops=0, transcendentals=0, bytes_accessed=8 * (4 * count + rows) * second * width
-        ),
+        cost_estimate=LIGHT,
         name="edges",
     )(in_hbm(value), in_hbm(density))
 
@@ -236,9 +234,7 @@
             pltpu.SemaphoreType.DMA((count + 2,)),
         ],
         compiler_params=pltpu.CompilerParams(vmem_limit_bytes=VMEM_LIMIT),
-        cost_estimate=pl.CostEstimate(
-            flops=40 * cells, transcendentals=0, bytes_accessed=12 * cells
-        ),
+        cost_estimate=LIGHT,
         name="value_step",
     )(in_hbm(value), low, high, crowding, *halos)
 
@@ -342,78 +338,90 @@
             pltpu.SemaphoreType.DMA((count,)),
         ],
         compiler_params=pltpu.CompilerParams(vmem_limit_bytes=VMEM_LIMIT),
-        cost_estimate=pl.CostEstimate(
-            flops=60 * cells, transcendentals=0, bytes_accessed=12 * cells
-        ),
+        cost_estimate=LIGHT,
         name="density_step",
     )(in_hbm(density), in_hbm(control), low, high, low_now, high_now)
 
 
-def arrive_kernel(begin, partial, halo, out, held, near, sems):
+def arrive_kernel(partial, *refs):
+    halos, (out, held, near, load, store) = refs[:-5], refs[-5:]
     count, rows = partial.shape[:2]
-    extent, second = halo.shape[:2]
     row = jnp.where(is_negative(), count - 1, 0)
-    base = lax.axis_index("vel") * rows + begin
+    base = lax.axis_index("vel") * rows
     total = rows * lax.axis_size("vel")
     loads = []
-    for a in range(extent):
-        loads.append(pltpu.make_async_copy(partial.at[row, begin + a], held.at[a], sems.at[a]))
-        loads.append(pltpu.make_async_copy(halo.at[a], near.at[a], sems.at[extent + a]))
-    start_all(loads)
+    for halo in halos:
+        for k in range(halo.shape[0]):
+            a = len(loads)
+            pair = [
+                pltpu.make_async_copy(partial.at[row, a], held.at[a], load.at[2 * a]),
+                pltpu.make_async_copy(halo.at[k], near.at[a], load.at[2 * a + 1]),
+            ]
+            start_all(pair)
+            loads.append(pair)
     stores = []
-    for a in range(extent):
-        wait_all(loads[2 * a : 2 * a + 2])
+    for a, pair in enumerate(loads):
+        wait_all(pair)
         held[a] = held[a] + slant(base + a, total) * near[a]
-        stores.append(pltpu.make_async_copy(held.at[a], out.at[row, begin + a], sems.at[2 * extent + a]))
+        stores.append(pltpu.make_async_copy(held.at[a], out.at[row, a], store.at[a]))
         stores[-1].start()
     wait_all(stores)
 
 
-def arrive(partial, halo, begin):
-    block = pltpu.VMEM(halo.shape, halo.dtype)
-    return pl.pallas_call(
-        functools.partial(arrive_kernel, begin),
+def arrive(partial, halos):
+    extent = sum(halo.shape[0] for halo in halos)
+    block = pltpu.VMEM((extent,) + partial.shape[2:], partial.dtype)
+    return pl.pallas_call(
+        arrive_kernel,
         out_shape=jax.ShapeDtypeStruct(partial.shape, partial.dtype),
-        in_specs=[ANY, ANY],
+        in_specs=[ANY] * (1 + len(halos)),
         out_specs=ANY,
-        scratch_shapes=[block, block, pltpu.SemaphoreType.DMA((3 * halo.shape[0],))],
+        scratch_shapes=[
+            block,
+            block,
+            pltpu.SemaphoreType.DMA((2 * extent,)),
+            pltpu.SemaphoreType.DMA((extent,)),
+        ],
         input_output_aliases={0: 0},
         compiler_params=pltpu.CompilerParams(vmem_limit_bytes=VMEM_LIMIT),
-        cost_estimate=pl.CostEstimate(
-            flops=2 * halo.size, transcendentals=0, bytes_accessed=12 * halo.size
-        ),
+        cost_estimate=LIGHT,
         name="arrive",
-    )(in_hbm(partial), halo)
-
-
-def arrive_last_kernel(partial, rest, halo, out, held, sem):
+    )(in_hbm(partial), *halos)
+
+
+def arrive_last_kernel(partial, rest, *refs):
+    halos, (out, held, sems) = refs[:-3], refs[-3:]
     count, rows = partial.shape[:2]
-    extent = halo.shape[0]
+    extent = rest.shape[0]
     row = jnp.where(is_negative(), count - 1, 0)
     base = lax.axis_index("vel") * rows + rows - extent
     total = rows * lax.axis_size("vel")
     copies = []
-    for a in range(extent):
-        held[a] = rest[a] + slant(base + a, total) * halo[a]
-        copies.append(pltpu.make_async_copy(held.at[a], out.at[row, rows - extent + a], sem.at[a]))
-        copies[-1].start()
+    for halo in halos:
+        for k in range(halo.shape[0]):
+            a = len(copies)
+            held[a] = rest[a] + slant(base + a, total) * halo[k]
+            target = out.at[row, rows - extent + a]
+            copies.append(pltpu.make_async_copy(held.at[a], target, sems.at[a]))
+            copies[-1].start()
     wait_all(copies)
 
 
-def arrive_last(partial, rest, halo):
+def arrive_last(partial, rest, halos):
     return pl.pallas_call(
         arrive_last_kernel,
         out_shape=jax.ShapeDtypeStruct(partial.shape, partial.dtype),
-        in_specs=[ANY, VMEM, VMEM],
+        in_specs=[ANY] + [VMEM] * (1 + len(halos)),
         out_specs=ANY,
-        scratch_shapes=[pltpu.VMEM(halo.shape, halo.dtype), pltpu.SemaphoreType.DMA((halo.shape[0],))],
+        scratch_shapes=[
+            pltpu.VMEM(rest.shape, rest.dtype),
+            pltpu.SemaphoreType.DMA((rest.shape[0],)),
+        ],
         input_output_aliases={0: 0},
         compiler_params=pltpu.CompilerParams(vmem_limit_bytes=VMEM_LIMIT),
-        cost_estimate=pl.CostEstimate(
-            flops=2 * halo.size, transcendentals=0, bytes_accessed=8 * halo.size
-        ),
+        cost_estimate=LIGHT,
         name="arrive_last",
-    )(in_hbm(partial), in_vmem(rest), in_vmem(halo))
+    )(in_hbm(partial), in_vmem(rest), *[in_vmem(halo) for halo in halos])
 
 
 def routes(mesh):
@@ -428,44 +436,54 @@
             index = index * size + at[name]
         return index
 
-    value_route, density_route = [], []
+    value_route, density_route, over_route, swap_route = [], [], [], []
     for pos in range(slabs):
         for vel in range(groups):
             onward = 1 if vel < groups // 2 else -1
             value_route.append((place(pos, vel), place(pos + onward, vel)))
             density_route.append((place(pos, vel), place(pos - onward, vel)))
-    return names, value_route, density_route
+            leads = slabs % 2 == 0 and (pos % 2 == 0) == (onward > 0)
+            over_route.append((place(pos, vel), place(pos - 2 * onward if leads else pos, vel)))
+            swap_route.append((place(pos, vel), place(pos + onward if leads else pos - onward, vel)))
+    return names, value_route, density_route, over_route, swap_route
 
 
 def body(mesh, value_next, density):
-    names, value_route, density_route = routes(mesh)
+    names, value_route, density_route, over_route, swap_route = routes(mesh)
     groups = mesh.shape["vel"]
     count, rows, second, width = value_next.shape
     tail = max(1, rows // 8)
-    cuts = ((0, rows - tail), (rows - tail, rows))
+    near = rows // 2 - tail - 1
+    cuts = (
+        (0, near),
+        (near, rows - 2 * tail),
+        (rows - 2 * tail, rows - tail),
+        (rows - tail, rows),
+    )
     onward = [(v, v + 1) for v in range(groups - 1)]
     back = [(v + 1, v) for v in range(groups - 1)]
 
-    value_halos = [lax.ppermute(value_rows(value_next, 0, rows), names, value_route)]
-    low, high, *leaving = edges(value_next, density, cuts)
+    value_halo = lax.ppermute(value_rows(value_next, 0, rows), names, value_route)
+    low, high, *parts = edges(value_next, density, cuts)
+    fillers = [lax.ppermute(part, names, over_route) for part in parts[1::2]]
     low = lax.ppermute(low, "vel", onward)
     high = lax.ppermute(high, "vel", back)
     mass = lax.psum(jnp.sum(density, axis=(1, 2)), "vel") / (second * second)
     crowding = CROWDING * mass * mass
 
-    held = (*leaving, *value_halos, crowding, low, high)
-    *leaving, value_halo, crowding, low, high = lax.optimization_barrier(held)
-    value_halos = [value_halo]
-    density_halos = [lax.ppermute(part, names, density_route) for part in leaving]
-
-    value_now, low_now, high_now = value_step(value_next, low, high, crowding, value_halos)
+    held = (*parts[::2], value_halo, crowding, low, high, *fillers)
+    *parts, value_halo, crowding, low, high = lax.optimization_barrier(held)[: -len(fillers)]
+    fillers = [lax.ppermute(part, names, swap_route) for part in fillers]
+    parts = [lax.ppermute(part, names, density_route) for part in parts]
+
+    value_now, low_now, high_now = value_step(value_next, low, high, crowding, [value_halo])
     low_now = lax.ppermute(low_now, "vel", onward)
     high_now = lax.ppermute(high_now, "vel", back)
     density_next, rest = density_step(
-        density, value_now, low, high, low_now, high_now, tail
+        density, value_now, low, high, low_now, high_now, 2 * tail
     )
-    density_next = arrive(density_next, density_halos[0], 0)
-    density_next = arrive_last(density_next, rest, density_halos[1])
+    density_next = arrive(density_next, (parts[0], fillers[0]))
+    density_next = arrive_last(density_next, rest, (parts[1], fillers[1]))
     return value_now, density_next
 
 

time: 104 us -> 102 us (0.981)
  starting transfers between devices: 11.6 us -> 20.8 us
  blocking collectives: 11.8 us -> 6.33 us
  waiting for transfers between devices: 38.4 us -> 35.6 us
  Pallas kernels: 36.9 us -> 34.8 us
  local copies, waits for them, and re-layouts: 1.24 us -> 0.01 us
    ppermute x1, waiting for transfers between devices: 25.6 us -> 10.2 us  [body(): lax.ppermute(value_rows(value_next, 0, rows), names, value_route)]
    ppermute x2 -> x6, waiting for transfers between devices: 12.1 us -> 25.3 us  [the longest x2 16.1 us: body(): fillers = [lax.ppermute(part, names, over_route) for part in parts[1::2]]]
    ppermute x2 -> x6, starting transfers between devices: 3.23 us -> 12.6 us  [the longest x2 7.87 us: body(): fillers = [lax.ppermute(part, names, over_route) for part in parts[1::2]]]
    psum x1, blocking collectives: 11.8 us -> 6.33 us  [body(): mass = lax.psum(jnp.sum(density, axis=(1, 2)), 'vel') / (second * second)]
    pallas_call x1, Pallas kernels: 4.89 us -> 3.34 us  [edges(): pl.pallas_call(functools.partial(edges_kernel, cuts), out_shape=[edge, ed...]
    unnamed x2, local copies, waits for them, and re-layouts: 1.24 us -> 0.01 us
  transfers between devices with their start and end apart: 7 -> 11, of which waited for: 3 -> 6; matrix products, arithmetic and copies ran while one was open for 2% -> 2% of each run, Pallas kernels for 33% -> 31%
where the time goes in v4:
time: 102 us; the launch traced here: 101 us
  waiting for transfers between devices  35.6 us (35%)
  Pallas kernels  34.8 us (34%)
  starting transfers between devices  20.8 us (20%)
  blocking collectives  6.33 us (6%)
  other arithmetic  2.46 us (2%)
    ppermute x2, waiting for transfers between devices, body(): fillers = [lax.ppermute(part, names, over_route) for part in parts[1::2]]  16.1 us
    pallas_call x1, Pallas kernels, density_step(): pl.pallas_call(density_kernel, out_shape=[jax.ShapeDtypeStruct(density.sh...  14.7 us
    ppermute x1, waiting for transfers between devices, body(): lax.ppermute(value_rows(value_next, 0, rows), names, value_route)  10.2 us
    pallas_call x1, Pallas kernels, value_step(): pl.pallas_call(value_kernel, out_shape=[jax.ShapeDtypeStruct(value.shape,...  9.94 us
    ppermute x2, starting transfers between devices, body(): fillers = [lax.ppermute(part, names, over_route) for part in parts[1::2]]  7.87 us
    psum x1, blocking collectives, body(): mass = lax.psum(jnp.sum(density, axis=(1, 2)), 'vel') / (second * second)  6.33 us
    ppermute x2, waiting for transfers between devices, body(): fillers = [lax.ppermute(part, names, swap_route) for part in fillers]  5.53 us
    ppermute x2, starting transfers between devices, body(): parts = [lax.ppermute(part, names, density_route) for part in parts]  4.67 us
  transfers between devices with their start and end apart: 11, of which 6 were waited for; matrix products, arithmetic and copies ran while one was open for 2% of the time, Pallas kernels for 31%

profile of v4, /device:TPU:0, one launch (start us, length us, event | category | flops | bytes accessed | tf_op | source)
XLA Modules:
  0.0 100.9 jit_solution(8940372818636817251)
XLA Ops:
  0.6 2.6 %value_rows.1 = f32[16,64,512]{2,1,0:T(8,128)} custom-call(f32[2,16,64,512]{3,2,1,0:T(8,128)} %value.5), custom_call_target="tpu_custom_call" | custom-call | tf_op jit(solution)/shard_map/value_rows/pallas_call | solution.py:83
  3.2 3.0 %collective-permute-start = (f32[16,64,512]{2,1,0:T(8,128)}, f32[16,64,512]{2,1,0:T(8,128)S(1)}, u32[]{:S(2)}, u32[]{:S(2)}) collective-permute-start(f32[16,64,512]{2,1,0:T(8,128)} %value_rows.1), channel_id=1, source_target_pairs={{0,1},{8,9},{16,23},{24,31},{1,2},{9,10},{17,16},{25,24},{2,3},{10... | collective-permute-start | bytes 6291464 | tf_op jit(solution)/shard_map/ppermute | solution.py:466
  6.2 3.3 %edges.1 = (f32[2,2,64,512]{3,2,1,0:T(8,128)}, f32[2,2,64,512]{3,2,1,0:T(8,128)}, f32[5,64,512]{2,1,0:T(8,128)}, f32[7,64,512]{2,1,0:T(8,128)}, f32[2,64,512]{2,1,0:T(8,128)}, /*index=5*/f32[2,64,512]{2,1,0:T(8,128)}) custom-call(f32[2,16,64,512]{3,2,1,0:T(8,128)} %value.5, f32[2,16,64,512]{3,2,1,0:T(8,128)} %density.3), custom_call_target="tpu_custom_call" | custom-call | tf_op jit(solution)/shard_map/edges/pallas_call | solution.py:111
  9.6 5.5 %collective-permute-start.3 = (f32[7,64,512]{2,1,0:T(8,128)}, f32[7,64,512]{2,1,0:T(8,128)}, u32[]{:S(2)}, u32[]{:S(2)}) collective-permute-start(f32[7,64,512]{2,1,0:T(8,128)} %get-tuple-element.23), channel_id=1, source_target_pairs={{0,6},{8,14},{16,16},{24,24},{1,1},{9,9},{17,19},{25,27},{2,0},{10... | collective-permute-start | bytes 2752520 | tf_op jit(solution)/shard_map/ppermute | solution.py:468
  15.1 1.3 %collective-permute-start.1 = (f32[2,2,64,512]{3,2,1,0:T(8,128)}, f32[2,2,64,512]{3,2,1,0:T(8,128)S(1)}, u32[]{:S(2)}, u32[]{:S(2)}) collective-permute-start(f32[2,2,64,512]{3,2,1,0:T(8,128)} %get-tuple-element.21), channel_id=1, source_target_pairs={{0,8},{8,16},{16,24},{1,9},{9,17},{17,25},{2,10},{10,18},{18,26},{... | collective-permute-start | bytes 1572872 | tf_op jit(solution)/shard_map/ppermute | solution.py:469
  16.4 1.3 %collective-permute-start.2 = (f32[2,2,64,512]{3,2,1,0:T(8,128)}, f32[2,2,64,512]{3,2,1,0:T(8,128)S(1)}, u32[]{:S(2)}, u32[]{:S(2)}) collective-permute-start(f32[2,2,64,512]{3,2,1,0:T(8,128)} %get-tuple-element.22), channel_id=1, source_target_pairs={{8,0},{16,8},{24,16},{9,1},{17,9},{25,17},{10,2},{18,10},{26,18},{... | collective-permute-start | bytes 1572872 | tf_op jit(solution)/shard_map/ppermute | solution.py:470
  17.7 2.4 %collective-permute-start.4 = (f32[2,64,512]{2,1,0:T(8,128)}, f32[2,64,512]{2,1,0:T(8,128)}, u32[]{:S(2)}, u32[]{:S(2)}) collective-permute-start(f32[2,64,512]{2,1,0:T(8,128)} %get-tuple-element.24), channel_id=1, source_target_pairs={{0,6},{8,14},{16,16},{24,24},{1,1},{9,9},{17,19},{25,27},{2,0},{10... | collective-permute-start | bytes 786440 | tf_op jit(solution)/shard_map/ppermute | solution.py:468
  20.1 16.1 %collective-permute-done.3 = f32[7,64,512]{2,1,0:T(8,128)} collective-permute-done((f32[7,64,512]{2,1,0:T(8,128)}, f32[7,64,512]{2,1,0:T(8,128)}, u32[]{:S(2)}, u32[]{:S(2)}) %collective-permute-start.3) | collective-permute-done | bytes 917536 | tf_op jit(solution)/shard_map/ppermute | solution.py:468
  36.2 0.0 collective-permute-start.8
  36.2 2.5 %reduce_sum.9 = f32[2,512]{1,0:T(2,128)S(1)} reduce(f32[2,16,64,512]{3,2,1,0:T(8,128)} %density.3, f32[]{:T(128)} %constant.2.clone.1), dimensions={1,2}, to_apply=%region_0.0 | reduce | flops 1047552 | bytes 4198404 | tf_op jit(solution)/shard_map/reduce_sum | solution.py:471
  38.6 0.0 copy-start
  38.6 6.3 %psum.7 = f32[2,512]{1,0:T(2,128)S(1)} all-reduce(f32[2,512]{1,0:T(2,128)S(1)} %reduce_sum.9), channel_id=1, replica_groups=mesh['vel'=4,'pos'=8] {'vel'}, use_global_device_ids=true, to_apply=%region_1.0 | all-reduce | flops 1024 | bytes 8192 | tf_op jit(solution)/shard_map/psum | solution.py:471
  45.0 0.0 collective-permute-done.4
  45.0 0.0 collective-permute-done.1.low
  45.0 0.0 collective-permute-done.2.high
  45.0 10.2 %collective-permute-done.rest_0_ = f32[16,64,512]{2,1,0:T(8,128)S(1)} collective-permute-done((f32[16,64,512]{2,1,0:T(8,128)}, f32[16,64,512]{2,1,0:T(8,128)S(1)}, u32[]{:S(2)}, u32[]{:S(2)}) %collective-permute-start) | collective-permute-done | bytes 2097184 | tf_op jit(solution)/shard_map/ppermute | solution.py:466
  55.2 2.8 %collective-permute-start.7 = (f32[5,64,512]{2,1,0:T(8,128)}, f32[5,64,512]{2,1,0:T(8,128)S(1)}, u32[]{:S(2)}, u32[]{:S(2)}) collective-permute-start(f32[5,64,512]{2,1,0:T(8,128)} %get-tuple-element.33), channel_id=1, source_target_pairs={{0,7},{8,15},{16,17},{24,25},{1,0},{9,8},{17,18},{25,26},{2,1},{10... | collective-permute-start | bytes 1966088 | tf_op jit(solution)/shard_map/ppermute | solution.py:477
  58.0 9.9 %value_step.1 = (f32[2,16,64,512]{3,2,1,0:T(8,128)}, f32[2,64,512]{2,1,0:T(8,128)S(1)}, f32[2,64,512]{2,1,0:T(8,128)S(1)}) custom-call(f32[2,16,64,512]{3,2,1,0:T(8,128)} %value.5, f32[2,2,64,512]{3,2,1,0:T(8,128)S(1)} %collective-permute-done.1.low, f32[2,2,64,512]{3,2,1,0:T(8,128)S(1)} %collective-permute-done.2.high, ...), custom_call_target="tpu_custom_call" | custom-call | tf_op jit(solution)/shard_map/value_step/pallas_call | solution.py:223
  67.9 1.3 %collective-permute-start.5 = (f32[2,64,512]{2,1,0:T(8,128)S(1)}, f32[2,64,512]{2,1,0:T(8,128)S(1)}, u32[]{:S(2)}, u32[]{:S(2)}) collective-permute-start(f32[2,64,512]{2,1,0:T(8,128)S(1)} %get-tuple-element.30), channel_id=1, source_target_pairs={{0,8},{8,16},{16,24},{1,9},{9,17},{17,25},{2,10},{10,18},{18,26},{... | collective-permute-start | bytes 786440 | tf_op jit(solution)/shard_map/ppermute | solution.py:480
  69.2 1.3 %collective-permute-start.6 = (f32[2,64,512]{2,1,0:T(8,128)S(1)}, f32[2,64,512]{2,1,0:T(8,128)S(1)}, u32[]{:S(2)}, u32[]{:S(2)}) collective-permute-start(f32[2,64,512]{2,1,0:T(8,128)S(1)} %get-tuple-element.31), channel_id=1, source_target_pairs={{8,0},{16,8},{24,16},{9,1},{17,9},{25,17},{10,2},{18,10},{26,18},{... | collective-permute-start | bytes 786440 | tf_op jit(solution)/shard_map/ppermute | solution.py:481
  70.5 0.1 collective-permute-start.10
  70.6 0.0 collective-permute-done.5.low_now
  70.6 0.0 copy-done
  70.6 1.9 %collective-permute-start.9 = (f32[2,64,512]{2,1,0:T(8,128)S(1)}, f32[2,64,512]{2,1,0:T(8,128)S(1)}, u32[]{:S(2)}, u32[]{:S(2)}) collective-permute-start(f32[2,64,512]{2,1,0:T(8,128)S(1)} %copy-done), channel_id=1, source_target_pairs={{0,7},{8,15},{16,17},{24,25},{1,0},{9,8},{17,18},{25,26},{2,1},{10... | collective-permute-start | bytes 786440 | tf_op jit(solution)/shard_map/ppermute | solution.py:477
  72.5 0.1 collective-permute-done.6.high_now
  72.7 14.7 %density_step.1 = (f32[2,16,64,512]{3,2,1,0:T(8,128)}, f32[4,64,512]{2,1,0:T(8,128)S(1)}) custom-call(f32[2,16,64,512]{3,2,1,0:T(8,128)} %density.3, f32[2,16,64,512]{3,2,1,0:T(8,128)} %get-tuple-element.17.control, f32[2,2,64,512]{3,2,1,0:T(8,128)S(1)} %collective-permute-done.1.low, f32[2,2,64,512]{3,2,1,0:T(8,128)S(1)} %collective-permute-done.2.high, ...), custom_call_target="tpu_custom_call" | custom-call | tf_op jit(solution)/shard_map/density_step/pallas_call | solution.py:324
  87.3 4.6 %collective-permute-done.8.refs_1_ = f32[7,64,512]{2,1,0:T(8,128)} collective-permute-done((f32[7,64,512]{2,1,0:T(8,128)}, f32[7,64,512]{2,1,0:T(8,128)}, u32[]{:S(2)}, u32[]{:S(2)}) %collective-permute-start.8) | collective-permute-done | bytes 917536 | tf_op jit(solution)/shard_map/ppermute | solution.py:476
  91.9 0.0 collective-permute-done.7.refs_0_
  91.9 3.5 %arrive.1.partial = f32[2,16,64,512]{3,2,1,0:T(8,128)} custom-call(f32[2,16,64,512]{3,2,1,0:T(8,128)} %get-tuple-element.32.partial, f32[5,64,512]{2,1,0:T(8,128)S(1)} %collective-permute-done.7.refs_0_, f32[7,64,512]{2,1,0:T(8,128)} %collective-permute-done.8.refs_1_), custom_call_target="tpu_custom_call", output_to_operand_aliasing={{}: (0, {})} | custom-call | tf_op jit(solution)/shard_map/arrive/pallas_call | solution.py:374
  95.4 1.0 collective-permute-done.10.refs_1_
  96.4 3.7 %collective-permute-done.9.refs_0_ = f32[2,64,512]{2,1,0:T(8,128)S(1)} collective-permute-done((f32[2,64,512]{2,1,0:T(8,128)S(1)}, f32[2,64,512]{2,1,0:T(8,128)S(1)}, u32[]{:S(2)}, u32[]{:S(2)}) %collective-permute-start.9) | collective-permute-done | bytes 262176 | tf_op jit(solution)/shard_map/ppermute | solution.py:477
  100.0 0.8 arrive_last.1
  (1 shorter events, 0.0 us)
Async XLA Ops:
  3.2 52.0 %collective-permute-start = (f32[16,64,512]{2,1,0:T(8,128)}, f32[16,64,512]{2,1,0:T(8,128)S(1)}, u32[]{:S(2)}, u32[]{:S(2)}) collective-permute-start(f32[16,64,512]{2,1,0:T(8,128)} %value_rows.1), channel_id=1, source_target_pairs={{0,1},{8,9},{16,23},{24,31},{1,2},{9,10},{17,16},{25,24},{2,3},{10... | collective-permute-start | bytes 6291464 | tf_op jit(solution)/shard_map/ppermute | solution.py:466
  9.6 26.6 %collective-permute-start.3 = (f32[7,64,512]{2,1,0:T(8,128)}, f32[7,64,512]{2,1,0:T(8,128)}, u32[]{:S(2)}, u32[]{:S(2)}) collective-permute-start(f32[7,64,512]{2,1,0:T(8,128)} %get-tuple-element.23), channel_id=1, source_target_pairs={{0,6},{8,14},{16,16},{24,24},{1,1},{9,9},{17,19},{25,27},{2,0},{10... | collective-permute-start | bytes 2752520 | tf_op jit(solution)/shard_map/ppermute | solution.py:468
  15.1 29.9 %collective-permute-start.1 = (f32[2,2,64,512]{3,2,1,0:T(8,128)}, f32[2,2,64,512]{3,2,1,0:T(8,128)S(1)}, u32[]{:S(2)}, u32[]{:S(2)}) collective-permute-start(f32[2,2,64,512]{3,2,1,0:T(8,128)} %get-tuple-element.21), channel_id=1, source_target_pairs={{0,8},{8,16},{16,24},{1,9},{9,17},{17,25},{2,10},{10,18},{18,26},{... | collective-permute-start | bytes 1572872 | tf_op jit(solution)/shard_map/ppermute | solution.py:469
  16.4 28.6 %collective-permute-start.2 = (f32[2,2,64,512]{3,2,1,0:T(8,128)}, f32[2,2,64,512]{3,2,1,0:T(8,128)S(1)}, u32[]{:S(2)}, u32[]{:S(2)}) collective-permute-start(f32[2,2,64,512]{3,2,1,0:T(8,128)} %get-tuple-element.22), channel_id=1, source_target_pairs={{8,0},{16,8},{24,16},{9,1},{17,9},{25,17},{10,2},{18,10},{26,18},{... | collective-permute-start | bytes 1572872 | tf_op jit(solution)/shard_map/ppermute | solution.py:470
  17.7 27.3 %collective-permute-start.4 = (f32[2,64,512]{2,1,0:T(8,128)}, f32[2,64,512]{2,1,0:T(8,128)}, u32[]{:S(2)}, u32[]{:S(2)}) collective-permute-start(f32[2,64,512]{2,1,0:T(8,128)} %get-tuple-element.24), channel_id=1, source_target_pairs={{0,6},{8,14},{16,16},{24,24},{1,1},{9,9},{17,19},{25,27},{2,0},{10... | collective-permute-start | bytes 786440 | tf_op jit(solution)/shard_map/ppermute | solution.py:468
  36.2 55.7 %collective-permute-start.8 = (f32[7,64,512]{2,1,0:T(8,128)}, f32[7,64,512]{2,1,0:T(8,128)}, u32[]{:S(2)}, u32[]{:S(2)}) collective-permute-start(f32[7,64,512]{2,1,0:T(8,128)} %collective-permute-done.3), channel_id=1, source_target_pairs={{0,1},{8,9},{16,17},{24,25},{1,0},{9,8},{17,16},{25,24},{2,3},{10,... | collective-permute-start | bytes 2752520 | tf_op jit(solution)/shard_map/ppermute | solution.py:476
  38.6 32.0 %copy-start = (f32[2,64,512]{2,1,0:T(8,128)S(1)}, f32[2,64,512]{2,1,0:T(8,128)}, u32[]{:S(2)}) copy-start(f32[2,64,512]{2,1,0:T(8,128)} %get-tuple-element.35) | copy-start | bytes 786436
  55.2 36.7 %collective-permute-start.7 = (f32[5,64,512]{2,1,0:T(8,128)}, f32[5,64,512]{2,1,0:T(8,128)S(1)}, u32[]{:S(2)}, u32[]{:S(2)}) collective-permute-start(f32[5,64,512]{2,1,0:T(8,128)} %get-tuple-element.33), channel_id=1, source_target_pairs={{0,7},{8,15},{16,17},{24,25},{1,0},{9,8},{17,18},{25,26},{2,1},{10... | collective-permute-start | bytes 1966088 | tf_op jit(solution)/shard_map/ppermute | solution.py:477
  67.9 2.7 %collective-permute-start.5 = (f32[2,64,512]{2,1,0:T(8,128)S(1)}, f32[2,64,512]{2,1,0:T(8,128)S(1)}, u32[]{:S(2)}, u32[]{:S(2)}) collective-permute-start(f32[2,64,512]{2,1,0:T(8,128)S(1)} %get-tuple-element.30), channel_id=1, source_target_pairs={{0,8},{8,16},{16,24},{1,9},{9,17},{17,25},{2,10},{10,18},{18,26},{... | collective-permute-start | bytes 786440 | tf_op jit(solution)/shard_map/ppermute | solution.py:480
  69.2 3.4 %collective-permute-start.6 = (f32[2,64,512]{2,1,0:T(8,128)S(1)}, f32[2,64,512]{2,1,0:T(8,128)S(1)}, u32[]{:S(2)}, u32[]{:S(2)}) collective-permute-start(f32[2,64,512]{2,1,0:T(8,128)S(1)} %get-tuple-element.31), channel_id=1, source_target_pairs={{8,0},{16,8},{24,16},{9,1},{17,9},{25,17},{10,2},{18,10},{26,18},{... | collective-permute-start | bytes 786440 | tf_op jit(solution)/shard_map/ppermute | solution.py:481
  70.5 25.8 %collective-permute-start.10 = (f32[2,64,512]{2,1,0:T(8,128)}, f32[2,64,512]{2,1,0:T(8,128)S(1)}, u32[]{:S(2)}, u32[]{:S(2)}) collective-permute-start(f32[2,64,512]{2,1,0:T(8,128)} %collective-permute-done.4), channel_id=1, source_target_pairs={{0,1},{8,9},{16,17},{24,25},{1,0},{9,8},{17,16},{25,24},{2,3},{10,... | collective-permute-start | bytes 786440 | tf_op jit(solution)/shard_map/ppermute | solution.py:476
  70.6 29.4 %collective-permute-start.9 = (f32[2,64,512]{2,1,0:T(8,128)S(1)}, f32[2,64,512]{2,1,0:T(8,128)S(1)}, u32[]{:S(2)}, u32[]{:S(2)}) collective-permute-start(f32[2,64,512]{2,1,0:T(8,128)S(1)} %copy-done), channel_id=1, source_target_pairs={{0,7},{8,15},{16,17},{24,25},{1,0},{9,8},{17,18},{25,26},{2,1},{10... | collective-permute-start | bytes 786440 | tf_op jit(solution)/shard_map/ppermute | solution.py:477

commit v5 on v4

--- a/solution.py
+++ b/solution.py
@@ -72,24 +72,26 @@
     ]
 
 
-def value_rows_kernel(begin, end, value, sent, *scratch):
+def value_rows_kernel(begin, end, value, sent, sems):
     row = jnp.where(is_negative(), value.shape[0] - 1, 0)
-    relay(leaving_rows(value, row, ((begin, end),), (sent,)), *scratch)
+    pairs = leaving_rows(value, row, ((begin, end),), (sent,))
+    copies = [pltpu.make_async_copy(s, t, sems.at[k]) for k, (s, t) in enumerate(pairs)]
+    start_all(copies)
+    wait_all(copies)
 
 
 def value_rows(value, begin, end):
     shape = (end - begin,) + value.shape[2:]
-    sent = pltpu.HBM(shape, value.dtype)
     return pl.pallas_call(
         functools.partial(value_rows_kernel, begin, end),
-        out_shape=sent,
+        out_shape=[pltpu.VMEM(shape, value.dtype)],
         in_specs=[ANY],
-        out_specs=ANY,
-        scratch_shapes=relay_scratch(*shape, value.dtype),
+        out_specs=[VMEM],
+        scratch_shapes=[pltpu.SemaphoreType.DMA((end - begin,))],
         compiler_params=pltpu.CompilerParams(vmem_limit_bytes=VMEM_LIMIT),
         cost_estimate=LIGHT,
         name="value_rows",
-    )(in_hbm(value))
+    )(in_hbm(value))[0]
 
 
 def edges_kernel(cuts, value, density, low, high, *rest):
@@ -463,7 +465,11 @@
     onward = [(v, v + 1) for v in range(groups - 1)]
     back = [(v + 1, v) for v in range(groups - 1)]
 
-    value_halo = lax.ppermute(value_rows(value_next, 0, rows), names, value_route)
+    split = rows // 2 + 1
+    value_halos = [
+        lax.ppermute(value_rows(value_next, begin, end), names, value_route)
+        for begin, end in ((0, split), (split, rows))
+    ]
     low, high, *parts = edges(value_next, density, cuts)
     fillers = [lax.ppermute(part, names, over_route) for part in parts[1::2]]
     low = lax.ppermute(low, "vel", onward)
@@ -471,12 +477,12 @@
     mass = lax.psum(jnp.sum(density, axis=(1, 2)), "vel") / (second * second)
     crowding = CROWDING * mass * mass
 
-    held = (*parts[::2], value_halo, crowding, low, high, *fillers)
-    *parts, value_halo, crowding, low, high = lax.optimization_barrier(held)[: -len(fillers)]
+    held = (parts[::2], value_halos, crowding, low, high, fillers)
+    parts, value_halos, crowding, low, high, _ = lax.optimization_barrier(held)
     fillers = [lax.ppermute(part, names, swap_route) for part in fillers]
     parts = [lax.ppermute(part, names, density_route) for part in parts]
 
-    value_now, low_now, high_now = value_step(value_next, low, high, crowding, [value_halo])
+    value_now, low_now, high_now = value_step(value_next, low, high, crowding, value_halos)
     low_now = lax.ppermute(low_now, "vel", onward)
     high_now = lax.ppermute(high_now, "vel", back)
     density_next, rest = density_step(

time: 102 us -> 100 us (0.980)
  waiting for transfers between devices: 35.6 us -> 23.7 us
  starting transfers between devices: 20.8 us -> 27 us
  blocking collectives: 6.33 us -> 9.24 us
  Pallas kernels: 34.8 us -> 36.3 us
    ppermute x1 -> x2, waiting for transfers between devices: 10.2 us -> 1.6 us  [body(): lax.ppermute(value_rows(value_next, begin, end), names, value_route)]
    ppermute x1 -> x2, starting transfers between devices: 2.99 us -> 7.38 us  [body(): lax.ppermute(value_rows(value_next, begin, end), names, value_route)]
    psum x1, blocking collectives: 6.33 us -> 9.24 us  [body(): mass = lax.psum(jnp.sum(density, axis=(1, 2)), 'vel') / (second * second)]
    ppermute x2, waiting for transfers between devices: 16.1 us -> 13.2 us  [body(): fillers = [lax.ppermute(part, names, over_route) for part in parts[1::2]]]
    ppermute x2, starting transfers between devices: 7.87 us -> 9.6 us  [body(): fillers = [lax.ppermute(part, names, over_route) for part in parts[1::2]]]
    ppermute x2, waiting for transfers between devices: 5.53 us -> 3.98 us  [body(): fillers = [lax.ppermute(part, names, swap_route) for part in fillers]]
    pallas_call x1 -> x2, Pallas kernels: 2.58 us -> 3.65 us  [value_rows(): pl.pallas_call(functools.partial(value_rows_kernel, begin, end), out_shap...]
    ppermute x2, waiting for transfers between devices: 3.68 us -> 4.74 us  [body(): parts = [lax.ppermute(part, names, density_route) for part in parts]]
  transfers between devices with their start and end apart: 11 -> 12, of which waited for: 6 -> 7; matrix products, arithmetic and copies ran while one was open for 2% -> 2% of each run, Pallas kernels for 31% -> 34%
where the time goes in v5:
time: 100 us; the launch traced here: 99.5 us
  Pallas kernels  36.3 us (36%)
  starting transfers between devices  27 us (27%)
  waiting for transfers between devices  23.7 us (24%)
  blocking collectives  9.24 us (9%)
  other arithmetic  2.46 us (2%)
    pallas_call x1, Pallas kernels, density_step(): pl.pallas_call(density_kernel, out_shape=[jax.ShapeDtypeStruct(density.sh...  14.7 us
    ppermute x2, waiting for transfers between devices, body(): fillers = [lax.ppermute(part, names, over_route) for part in parts[1::2]]  13.2 us
    pallas_call x1, Pallas kernels, value_step(): pl.pallas_call(value_kernel, out_shape=[jax.ShapeDtypeStruct(value.shape,...  10.3 us
    ppermute x2, starting transfers between devices, body(): fillers = [lax.ppermute(part, names, over_route) for part in parts[1::2]]  9.6 us
    psum x1, blocking collectives, body(): mass = lax.psum(jnp.sum(density, axis=(1, 2)), 'vel') / (second * second)  9.24 us
    ppermute x2, starting transfers between devices, body(): lax.ppermute(value_rows(value_next, begin, end), names, value_route)  7.38 us
    ppermute x2, waiting for transfers between devices, body(): parts = [lax.ppermute(part, names, density_route) for part in parts]  4.74 us
    ppermute x2, starting transfers between devices, body(): parts = [lax.ppermute(part, names, density_route) for part in parts]  4.67 us
  transfers between devices with their start and end apart: 12, of which 7 were waited for; matrix products, arithmetic and copies ran while one was open for 2% of the time, Pallas kernels for 34%

profile of v5, /device:TPU:0, one launch (start us, length us, event | category | flops | bytes accessed | tf_op | source)
XLA Modules:
  0.0 99.5 jit_solution(18062776089485876264)
XLA Ops:
  0.6 1.4 %value_rows.2 = f32[9,64,512]{2,1,0:T(8,128)S(1)} custom-call(f32[2,16,64,512]{3,2,1,0:T(8,128)} %value.7), custom_call_target="tpu_custom_call" | custom-call | tf_op jit(solution)/shard_map/value_rows/pallas_call | solution.py:85
  2.0 3.0 %collective-permute-start = (f32[9,64,512]{2,1,0:T(8,128)S(1)}, f32[9,64,512]{2,1,0:T(8,128)S(1)}, u32[]{:S(2)}, u32[]{:S(2)}) collective-permute-start(f32[9,64,512]{2,1,0:T(8,128)S(1)} %value_rows.2), channel_id=1, source_target_pairs={{0,1},{8,9},{16,23},{24,31},{1,2},{9,10},{17,16},{25,24},{2,3},{10... | collective-permute-start | bytes 3538952 | tf_op jit(solution)/shard_map/ppermute | solution.py:470
  5.0 3.3 %edges.1 = (f32[2,2,64,512]{3,2,1,0:T(8,128)}, f32[2,2,64,512]{3,2,1,0:T(8,128)}, f32[5,64,512]{2,1,0:T(8,128)}, f32[7,64,512]{2,1,0:T(8,128)}, f32[2,64,512]{2,1,0:T(8,128)}, /*index=5*/f32[2,64,512]{2,1,0:T(8,128)}) custom-call(f32[2,16,64,512]{3,2,1,0:T(8,128)} %value.7, f32[2,16,64,512]{3,2,1,0:T(8,128)} %density.3), custom_call_target="tpu_custom_call" | custom-call | tf_op jit(solution)/shard_map/edges/pallas_call | solution.py:113
  8.4 5.6 %collective-permute-start.4 = (f32[7,64,512]{2,1,0:T(8,128)}, f32[7,64,512]{2,1,0:T(8,128)}, u32[]{:S(2)}, u32[]{:S(2)}) collective-permute-start(f32[7,64,512]{2,1,0:T(8,128)} %get-tuple-element.24), channel_id=1, source_target_pairs={{0,6},{8,14},{16,16},{24,24},{1,1},{9,9},{17,19},{25,27},{2,0},{10... | collective-permute-start | bytes 2752520 | tf_op jit(solution)/shard_map/ppermute | solution.py:474
  14.1 2.2 %value_rows.3 = f32[7,64,512]{2,1,0:T(8,128)} custom-call(f32[2,16,64,512]{3,2,1,0:T(8,128)} %value.7), custom_call_target="tpu_custom_call" | custom-call | tf_op jit(solution)/shard_map/value_rows/pallas_call | solution.py:85
  16.3 4.4 %collective-permute-start.1 = (f32[7,64,512]{2,1,0:T(8,128)}, f32[7,64,512]{2,1,0:T(8,128)}, u32[]{:S(2)}, u32[]{:S(2)}) collective-permute-start(f32[7,64,512]{2,1,0:T(8,128)} %value_rows.3), channel_id=1, source_target_pairs={{0,1},{8,9},{16,23},{24,31},{1,2},{9,10},{17,16},{25,24},{2,3},{10... | collective-permute-start | bytes 2752520 | tf_op jit(solution)/shard_map/ppermute | solution.py:470
  20.7 4.0 %collective-permute-start.5 = (f32[2,64,512]{2,1,0:T(8,128)S(1)}, f32[2,64,512]{2,1,0:T(8,128)S(1)}, u32[]{:S(2)}, u32[]{:S(2)}) collective-permute-start(f32[2,64,512]{2,1,0:T(8,128)S(1)} %copy-done.3), channel_id=1, source_target_pairs={{0,6},{8,14},{16,16},{24,24},{1,1},{9,9},{17,19},{25,27},{2,0},{10... | collective-permute-start | bytes 786440 | tf_op jit(solution)/shard_map/ppermute | solution.py:474
  24.7 1.3 %collective-permute-start.2 = (f32[2,2,64,512]{3,2,1,0:T(8,128)}, f32[2,2,64,512]{3,2,1,0:T(8,128)S(1)}, u32[]{:S(2)}, u32[]{:S(2)}) collective-permute-start(f32[2,2,64,512]{3,2,1,0:T(8,128)} %get-tuple-element.22), channel_id=1, source_target_pairs={{0,8},{8,16},{16,24},{1,9},{9,17},{17,25},{2,10},{10,18},{18,26},{... | collective-permute-start | bytes 1572872 | tf_op jit(solution)/shard_map/ppermute | solution.py:475
  26.0 13.2 %collective-permute-done.5 = f32[2,64,512]{2,1,0:T(8,128)S(1)} collective-permute-done((f32[2,64,512]{2,1,0:T(8,128)S(1)}, f32[2,64,512]{2,1,0:T(8,128)S(1)}, u32[]{:S(2)}, u32[]{:S(2)}) %collective-permute-start.5) | collective-permute-done | bytes 262176 | tf_op jit(solution)/shard_map/ppermute | solution.py:474
  39.2 1.3 %collective-permute-start.3 = (f32[2,2,64,512]{3,2,1,0:T(8,128)}, f32[2,2,64,512]{3,2,1,0:T(8,128)S(1)}, u32[]{:S(2)}, u32[]{:S(2)}) collective-permute-start(f32[2,2,64,512]{3,2,1,0:T(8,128)} %get-tuple-element.23), channel_id=1, source_target_pairs={{8,0},{16,8},{24,16},{9,1},{17,9},{25,17},{10,2},{18,10},{26,18},{... | collective-permute-start | bytes 1572872 | tf_op jit(solution)/shard_map/ppermute | solution.py:476
  40.5 0.0 collective-permute-done.4
  40.5 0.1 collective-permute-start.9
  40.6 2.5 %reduce_sum.9 = f32[2,512]{1,0:T(2,128)S(1)} reduce(f32[2,16,64,512]{3,2,1,0:T(8,128)} %density.3, f32[]{:T(128)} %constant.2.clone.1), dimensions={1,2}, to_apply=%region_0.0 | reduce | flops 1047552 | bytes 4198404 | tf_op jit(solution)/shard_map/reduce_sum | solution.py:477
  43.0 9.2 %psum.7 = f32[2,512]{1,0:T(2,128)S(1)} all-reduce(f32[2,512]{1,0:T(2,128)S(1)} %reduce_sum.9), channel_id=1, replica_groups=mesh['vel'=4,'pos'=8] {'vel'}, use_global_device_ids=true, to_apply=%region_1.0 | all-reduce | flops 1024 | bytes 8192 | tf_op jit(solution)/shard_map/psum | solution.py:477
  52.3 0.0 collective-permute-done.2.low
  52.3 0.0 collective-permute-done.3.high
  52.3 1.6 %collective-permute-done.1.rest_1_ = f32[7,64,512]{2,1,0:T(8,128)} collective-permute-done((f32[7,64,512]{2,1,0:T(8,128)}, f32[7,64,512]{2,1,0:T(8,128)}, u32[]{:S(2)}, u32[]{:S(2)}) %collective-permute-start.1) | collective-permute-done | bytes 917536 | tf_op jit(solution)/shard_map/ppermute | solution.py:470
  53.9 0.0 collective-permute-done.rest_0_
  53.9 2.8 %collective-permute-start.8 = (f32[5,64,512]{2,1,0:T(8,128)}, f32[5,64,512]{2,1,0:T(8,128)S(1)}, u32[]{:S(2)}, u32[]{:S(2)}) collective-permute-start(f32[5,64,512]{2,1,0:T(8,128)} %get-tuple-element.35), channel_id=1, source_target_pairs={{0,7},{8,15},{16,17},{24,25},{1,0},{9,8},{17,18},{25,26},{2,1},{10... | collective-permute-start | bytes 1966088 | tf_op jit(solution)/shard_map/ppermute | solution.py:483
  56.7 10.3 %value_step.1 = (f32[2,16,64,512]{3,2,1,0:T(8,128)}, f32[2,64,512]{2,1,0:T(8,128)S(1)}, f32[2,64,512]{2,1,0:T(8,128)S(1)}) custom-call(f32[2,16,64,512]{3,2,1,0:T(8,128)} %value.7, f32[2,2,64,512]{3,2,1,0:T(8,128)S(1)} %collective-permute-done.2.low, f32[2,2,64,512]{3,2,1,0:T(8,128)S(1)} %collective-permute-done.3.high, ...), custom_call_target="tpu_custom_call" | custom-call | tf_op jit(solution)/shard_map/value_step/pallas_call | solution.py:225
  67.0 1.3 %collective-permute-start.6 = (f32[2,64,512]{2,1,0:T(8,128)S(1)}, f32[2,64,512]{2,1,0:T(8,128)S(1)}, u32[]{:S(2)}, u32[]{:S(2)}) collective-permute-start(f32[2,64,512]{2,1,0:T(8,128)S(1)} %get-tuple-element.32), channel_id=1, source_target_pairs={{0,8},{8,16},{16,24},{1,9},{9,17},{17,25},{2,10},{10,18},{18,26},{... | collective-permute-start | bytes 786440 | tf_op jit(solution)/shard_map/ppermute | solution.py:486
  68.3 1.3 %collective-permute-start.7 = (f32[2,64,512]{2,1,0:T(8,128)S(1)}, f32[2,64,512]{2,1,0:T(8,128)S(1)}, u32[]{:S(2)}, u32[]{:S(2)}) collective-permute-start(f32[2,64,512]{2,1,0:T(8,128)S(1)} %get-tuple-element.33), channel_id=1, source_target_pairs={{8,0},{16,8},{24,16},{9,1},{17,9},{25,17},{10,2},{18,10},{26,18},{... | collective-permute-start | bytes 786440 | tf_op jit(solution)/shard_map/ppermute | solution.py:487
  69.7 0.1 collective-permute-start.11
  69.8 1.9 %collective-permute-start.10 = (f32[2,64,512]{2,1,0:T(8,128)S(1)}, f32[2,64,512]{2,1,0:T(8,128)S(1)}, u32[]{:S(2)}, u32[]{:S(2)}) collective-permute-start(f32[2,64,512]{2,1,0:T(8,128)S(1)} %copy-done), channel_id=1, source_target_pairs={{0,7},{8,15},{16,17},{24,25},{1,0},{9,8},{17,18},{25,26},{2,1},{10... | collective-permute-start | bytes 786440 | tf_op jit(solution)/shard_map/ppermute | solution.py:483
  71.6 0.1 collective-permute-done.7.high_now
  71.8 14.7 %density_step.1 = (f32[2,16,64,512]{3,2,1,0:T(8,128)}, f32[4,64,512]{2,1,0:T(8,128)S(1)}) custom-call(f32[2,16,64,512]{3,2,1,0:T(8,128)} %density.3, f32[2,16,64,512]{3,2,1,0:T(8,128)} %get-tuple-element.18.control, f32[2,2,64,512]{3,2,1,0:T(8,128)S(1)} %collective-permute-done.2.low, f32[2,2,64,512]{3,2,1,0:T(8,128)S(1)} %collective-permute-done.3.high, ...), custom_call_target="tpu_custom_call" | custom-call | tf_op jit(solution)/shard_map/density_step/pallas_call | solution.py:326
  86.4 1.0 collective-permute-done.8.refs_0_
  87.4 3.1 %collective-permute-done.9.refs_1_ = f32[7,64,512]{2,1,0:T(8,128)} collective-permute-done((f32[7,64,512]{2,1,0:T(8,128)}, f32[7,64,512]{2,1,0:T(8,128)}, u32[]{:S(2)}, u32[]{:S(2)}) %collective-permute-start.9) | collective-permute-done | bytes 917536 | tf_op jit(solution)/shard_map/ppermute | solution.py:482
  90.5 3.5 %arrive.1.partial = f32[2,16,64,512]{3,2,1,0:T(8,128)} custom-call(f32[2,16,64,512]{3,2,1,0:T(8,128)} %get-tuple-element.34.partial, f32[5,64,512]{2,1,0:T(8,128)S(1)} %collective-permute-done.8.refs_0_, f32[7,64,512]{2,1,0:T(8,128)} %collective-permute-done.9.refs_1_), custom_call_target="tpu_custom_call", output_to_operand_aliasing={{}: (0, {})} | custom-call | tf_op jit(solution)/shard_map/arrive/pallas_call | solution.py:376
  94.0 0.9 collective-permute-done.11.refs_1_
  94.9 3.8 %collective-permute-done.10.refs_0_ = f32[2,64,512]{2,1,0:T(8,128)S(1)} collective-permute-done((f32[2,64,512]{2,1,0:T(8,128)S(1)}, f32[2,64,512]{2,1,0:T(8,128)S(1)}, u32[]{:S(2)}, u32[]{:S(2)}) %collective-permute-start.10) | collective-permute-done | bytes 262176 | tf_op jit(solution)/shard_map/ppermute | solution.py:483
  98.6 0.8 arrive_last.1
  (10 shorter events, 0.0 us)
Async XLA Ops:
  2.0 51.9 %collective-permute-start = (f32[9,64,512]{2,1,0:T(8,128)S(1)}, f32[9,64,512]{2,1,0:T(8,128)S(1)}, u32[]{:S(2)}, u32[]{:S(2)}) collective-permute-start(f32[9,64,512]{2,1,0:T(8,128)S(1)} %value_rows.2), channel_id=1, source_target_pairs={{0,1},{8,9},{16,23},{24,31},{1,2},{9,10},{17,16},{25,24},{2,3},{10... | collective-permute-start | bytes 3538952 | tf_op jit(solution)/shard_map/ppermute | solution.py:470
  8.4 12.3 %copy-start.3 = (f32[2,64,512]{2,1,0:T(8,128)S(1)}, f32[2,64,512]{2,1,0:T(8,128)}, u32[]{:S(2)}) copy-start(f32[2,64,512]{2,1,0:T(8,128)} %get-tuple-element.25) | copy-start | bytes 786436
  8.4 32.1 %collective-permute-start.4 = (f32[7,64,512]{2,1,0:T(8,128)}, f32[7,64,512]{2,1,0:T(8,128)}, u32[]{:S(2)}, u32[]{:S(2)}) collective-permute-start(f32[7,64,512]{2,1,0:T(8,128)} %get-tuple-element.24), channel_id=1, source_target_pairs={{0,6},{8,14},{16,16},{24,24},{1,1},{9,9},{17,19},{25,27},{2,0},{10... | collective-permute-start | bytes 2752520 | tf_op jit(solution)/shard_map/ppermute | solution.py:474
  16.3 37.6 %collective-permute-start.1 = (f32[7,64,512]{2,1,0:T(8,128)}, f32[7,64,512]{2,1,0:T(8,128)}, u32[]{:S(2)}, u32[]{:S(2)}) collective-permute-start(f32[7,64,512]{2,1,0:T(8,128)} %value_rows.3), channel_id=1, source_target_pairs={{0,1},{8,9},{16,23},{24,31},{1,2},{9,10},{17,16},{25,24},{2,3},{10... | collective-permute-start | bytes 2752520 | tf_op jit(solution)/shard_map/ppermute | solution.py:470
  20.7 18.5 %collective-permute-start.5 = (f32[2,64,512]{2,1,0:T(8,128)S(1)}, f32[2,64,512]{2,1,0:T(8,128)S(1)}, u32[]{:S(2)}, u32[]{:S(2)}) collective-permute-start(f32[2,64,512]{2,1,0:T(8,128)S(1)} %copy-done.3), channel_id=1, source_target_pairs={{0,6},{8,14},{16,16},{24,24},{1,1},{9,9},{17,19},{25,27},{2,0},{10... | collective-permute-start | bytes 786440 | tf_op jit(solution)/shard_map/ppermute | solution.py:474
  24.7 27.6 %collective-permute-start.2 = (f32[2,2,64,512]{3,2,1,0:T(8,128)}, f32[2,2,64,512]{3,2,1,0:T(8,128)S(1)}, u32[]{:S(2)}, u32[]{:S(2)}) collective-permute-start(f32[2,2,64,512]{3,2,1,0:T(8,128)} %get-tuple-element.22), channel_id=1, source_target_pairs={{0,8},{8,16},{16,24},{1,9},{9,17},{17,25},{2,10},{10,18},{18,26},{... | collective-permute-start | bytes 1572872 | tf_op jit(solution)/shard_map/ppermute | solution.py:475
  39.2 1.3 %copy-start.1 = (f32[2,64,512]{2,1,0:T(8,128)}, f32[2,64,512]{2,1,0:T(8,128)S(1)}, u32[]{:S(2)}) copy-start(f32[2,64,512]{2,1,0:T(8,128)S(1)} %collective-permute-done.5) | copy-start | bytes 786436
  39.2 13.1 %collective-permute-start.3 = (f32[2,2,64,512]{3,2,1,0:T(8,128)}, f32[2,2,64,512]{3,2,1,0:T(8,128)S(1)}, u32[]{:S(2)}, u32[]{:S(2)}) collective-permute-start(f32[2,2,64,512]{3,2,1,0:T(8,128)} %get-tuple-element.23), channel_id=1, source_target_pairs={{8,0},{16,8},{24,16},{9,1},{17,9},{25,17},{10,2},{18,10},{26,18},{... | collective-permute-start | bytes 1572872 | tf_op jit(solution)/shard_map/ppermute | solution.py:476
  40.5 50.0 %collective-permute-start.9 = (f32[7,64,512]{2,1,0:T(8,128)}, f32[7,64,512]{2,1,0:T(8,128)}, u32[]{:S(2)}, u32[]{:S(2)}) collective-permute-start(f32[7,64,512]{2,1,0:T(8,128)} %collective-permute-done.4), channel_id=1, source_target_pairs={{0,1},{8,9},{16,17},{24,25},{1,0},{9,8},{17,16},{25,24},{2,3},{10,... | collective-permute-start | bytes 2752520 | tf_op jit(solution)/shard_map/ppermute | solution.py:482
  52.3 17.4 %copy-start.2 = (f32[2,64,512]{2,1,0:T(8,128)S(1)}, f32[2,64,512]{2,1,0:T(8,128)}, u32[]{:S(2)}) copy-start(f32[2,64,512]{2,1,0:T(8,128)} %copy-done.1) | copy-start | bytes 786436
  52.3 17.5 %copy-start = (f32[2,64,512]{2,1,0:T(8,128)S(1)}, f32[2,64,512]{2,1,0:T(8,128)}, u32[]{:S(2)}) copy-start(f32[2,64,512]{2,1,0:T(8,128)} %get-tuple-element.37) | copy-start | bytes 786436
  53.9 33.5 %collective-permute-start.8 = (f32[5,64,512]{2,1,0:T(8,128)}, f32[5,64,512]{2,1,0:T(8,128)S(1)}, u32[]{:S(2)}, u32[]{:S(2)}) collective-permute-start(f32[5,64,512]{2,1,0:T(8,128)} %get-tuple-element.35), channel_id=1, source_target_pairs={{0,7},{8,15},{16,17},{24,25},{1,0},{9,8},{17,18},{25,26},{2,1},{10... | collective-permute-start | bytes 1966088 | tf_op jit(solution)/shard_map/ppermute | solution.py:483
  67.0 2.7 %collective-permute-start.6 = (f32[2,64,512]{2,1,0:T(8,128)S(1)}, f32[2,64,512]{2,1,0:T(8,128)S(1)}, u32[]{:S(2)}, u32[]{:S(2)}) collective-permute-start(f32[2,64,512]{2,1,0:T(8,128)S(1)} %get-tuple-element.32), channel_id=1, source_target_pairs={{0,8},{8,16},{16,24},{1,9},{9,17},{17,25},{2,10},{10,18},{18,26},{... | collective-permute-start | bytes 786440 | tf_op jit(solution)/shard_map/ppermute | solution.py:486
  68.3 3.4 %collective-permute-start.7 = (f32[2,64,512]{2,1,0:T(8,128)S(1)}, f32[2,64,512]{2,1,0:T(8,128)S(1)}, u32[]{:S(2)}, u32[]{:S(2)}) collective-permute-start(f32[2,64,512]{2,1,0:T(8,128)S(1)} %get-tuple-element.33), channel_id=1, source_target_pairs={{8,0},{16,8},{24,16},{9,1},{17,9},{25,17},{10,2},{18,10},{26,18},{... | collective-permute-start | bytes 786440 | tf_op jit(solution)/shard_map/ppermute | solution.py:487
  69.7 25.2 %collective-permute-start.11 = (f32[2,64,512]{2,1,0:T(8,128)S(1)}, f32[2,64,512]{2,1,0:T(8,128)S(1)}, u32[]{:S(2)}, u32[]{:S(2)}) collective-permute-start(f32[2,64,512]{2,1,0:T(8,128)S(1)} %copy-done.2), channel_id=1, source_target_pairs={{0,1},{8,9},{16,17},{24,25},{1,0},{9,8},{17,16},{25,24},{2,3},{10,... | collective-permute-start | bytes 786440 | tf_op jit(solution)/shard_map/ppermute | solution.py:482
  69.8 28.9 %collective-permute-start.10 = (f32[2,64,512]{2,1,0:T(8,128)S(1)}, f32[2,64,512]{2,1,0:T(8,128)S(1)}, u32[]{:S(2)}, u32[]{:S(2)}) collective-permute-start(f32[2,64,512]{2,1,0:T(8,128)S(1)} %copy-done), channel_id=1, source_target_pairs={{0,7},{8,15},{16,17},{24,25},{1,0},{9,8},{17,18},{25,26},{2,1},{10... | collective-permute-start | bytes 786440 | tf_op jit(solution)/shard_map/ppermute | solution.py:483

commit v6 on v5

--- a/solution.py
+++ b/solution.py
@@ -13,6 +13,9 @@
 CROWDING = 0.3
 
 SUB = 8
+LANES = 128
+EARLY = 1
+SHIFT = 3
 VMEM_LIMIT = 18 * 1024 * 1024
 ANY = pl.BlockSpec(memory_space=pl.ANY)
 VMEM = pl.BlockSpec(memory_space=pltpu.VMEM)
@@ -72,19 +75,26 @@
     ]
 
 
-def value_rows_kernel(begin, end, value, sent, sems):
+def value_rows_kernel(begin, value, sent, sems):
     row = jnp.where(is_negative(), value.shape[0] - 1, 0)
-    pairs = leaving_rows(value, row, ((begin, end),), (sent,))
-    copies = [pltpu.make_async_copy(s, t, sems.at[k]) for k, (s, t) in enumerate(pairs)]
+    half = sent.shape[1]
+    copies = [
+        pltpu.make_async_copy(
+            value.at[row, (begin + k) // 2, pl.ds((begin + k) % 2 * half, half)],
+            sent.at[k],
+            sems.at[k],
+        )
+        for k in range(sent.shape[0])
+    ]
     start_all(copies)
     wait_all(copies)
 
 
 def value_rows(value, begin, end):
-    shape = (end - begin,) + value.shape[2:]
+    _, _, second, width = value.shape
     return pl.pallas_call(
-        functools.partial(value_rows_kernel, begin, end),
-        out_shape=[pltpu.VMEM(shape, value.dtype)],
+        functools.partial(value_rows_kernel, begin),
+        out_shape=[pltpu.VMEM((end - begin, second // 2, width), value.dtype)],
         in_specs=[ANY],
         out_specs=[VMEM],
         scratch_shapes=[pltpu.SemaphoreType.DMA((end - begin,))],
@@ -94,7 +104,8 @@
     )(in_hbm(value))[0]
 
 
-def edges_kernel(cuts, value, density, low, high, *rest):
+def edges_kernel(cuts, value, density, after, low, high, *rest):
+    del after
     count, rows = value.shape[:2]
     row = jnp.where(is_negative(), 0, count - 1)
     pairs = []
@@ -106,20 +117,20 @@
     relay(pairs, *rest[len(cuts) :])
 
 
-def edges(value, density, cuts):
+def edges(value, density, after, cuts):
     count, rows, second, width = value.shape
     edge = pltpu.HBM((2, count, second, width), value.dtype)
     parts = [pltpu.HBM((e - b, second, width), value.dtype) for b, e in cuts]
     return pl.pallas_call(
         functools.partial(edges_kernel, cuts),
         out_shape=[edge, edge, *parts],
-        in_specs=[ANY, ANY],
+        in_specs=[ANY, ANY, ANY],
         out_specs=[ANY] * (2 + len(cuts)),
         scratch_shapes=relay_scratch(4 * count + rows, second, width, value.dtype),
         compiler_params=pltpu.CompilerParams(vmem_limit_bytes=VMEM_LIMIT),
         cost_estimate=LIGHT,
         name="edges",
-    )(in_hbm(value), in_hbm(density))
+    )(in_hbm(value), in_hbm(density), after)
 
 
 def second_tile(ref, index, at, total):
@@ -136,6 +147,14 @@
     return here, above, below
 
 
+def steep_tiles(second, width):
+    tiles = []
+    for at in range(0, second, SUB):
+        index = at + lax.broadcasted_iota(jnp.int32, (SUB, LANES), 0)
+        tiles.append(jnp.concatenate([slant(index, second)] * (width // LANES), 1))
+    return tiles
+
+
 def value_kernel(value, low, high, crowding, *rest):
     parts = len(rest) - 9
     halos = rest[:parts]
@@ -147,6 +166,7 @@
     base = lax.axis_index("vel") * rows
     total = rows * lax.axis_size("vel")
     order = [jnp.where(negative, t, count - 1 - t) for t in range(count)]
+    half = second // 2
 
     begin = 0
     halo_copies = []
@@ -174,6 +194,7 @@
     above_far.wait()
     wait_all(halo_copies)
 
+    steep_y = steep_tiles(second, width)
     stores = []
     for t, i in enumerate(order):
         centre_copies[t].wait()
@@ -183,11 +204,10 @@
             for at in range(0, second, SUB):
                 here, up_w, dn_w = second_tile(pad, (i, a + 1), at, second)
                 if t == 0:
-                    x_near = halo[a, pl.ds(at, SUB), :]
+                    x_near = halo[2 * a + at // half, pl.ds(at % half, SUB), :]
                 else:
                     x_near = pad[order[t - 1], a + 1, pl.ds(at, SUB), :]
                 y_near = pltpu.roll(here, 1 if at < second // 2 else width - 1, 1)
-                index = at + lax.broadcasted_iota(jnp.int32, here.shape, 0)
                 up_v = pad[i, a + 2, pl.ds(at, SUB), :] - here
                 dn_v = here - pad[i, a, pl.ds(at, SUB), :]
                 up_w = up_w - here
@@ -202,7 +222,7 @@
                 fresh[i, a, pl.ds(at, SUB), :] = (
                     here
                     + steep * (x_near - here)
-                    + slant(index, second) * (y_near - here)
+                    + steep_y[at // SUB] * (y_near - here)
                     - (0.5 * CONTROL_COST) * hamilton
                     + VISCOSITY * laplace
                     + crowding[pl.ds(i, 1), :]
@@ -229,7 +249,7 @@
         out_specs=[ANY] * 3,
         scratch_shapes=[
             pltpu.VMEM((count, rows + 2, second, width), value.dtype),
-            pltpu.VMEM((rows, second, width), value.dtype),
+            pltpu.VMEM((2 * rows, second // 2, width), value.dtype),
             pltpu.VMEM(value.shape, value.dtype),
             pltpu.SemaphoreType.DMA((count + len(halos),)),
             pltpu.SemaphoreType.DMA((2,)),
@@ -274,6 +294,7 @@
             waits.append(far_copy)
     wait_all(waits)
 
+    steep_y = steep_tiles(second, width)
     stores = []
     for t, i in enumerate(order):
         wait_all(centre_copies[t])
@@ -286,26 +307,25 @@
                 up_v = pad[i, a + 2, pl.ds(at, SUB), :]
                 dn_v = pad[i, a, pl.ds(at, SUB), :]
                 y_near = pltpu.roll(here, width - 1 if at < second // 2 else 1, 1)
-                index = at + lax.broadcasted_iota(jnp.int32, here.shape, 0)
                 if t == 0:
                     along_x = -steep * here
                 else:
                     along_x = steep * (pad[order[t - 1], a + 1, pl.ds(at, SUB), :] - here)
-                speed_up = -CONTROL_COST * (ctl[i, a + 2, pl.ds(at, SUB), :] - ctl_here)
-                speed_dn = -CONTROL_COST * (ctl_here - ctl[i, a, pl.ds(at, SUB), :])
-                flux_up = jnp.maximum(speed_up, 0.0) * here + jnp.minimum(speed_up, 0.0) * up_v
-                flux_dn = jnp.maximum(speed_dn, 0.0) * dn_v + jnp.minimum(speed_dn, 0.0) * here
-                side_up = -CONTROL_COST * (ctl_up_w - ctl_here)
-                side_dn = -CONTROL_COST * (ctl_here - ctl_dn_w)
-                flux_right = jnp.maximum(side_up, 0.0) * here + jnp.minimum(side_up, 0.0) * up_w
-                flux_left = jnp.maximum(side_dn, 0.0) * dn_w + jnp.minimum(side_dn, 0.0) * here
-                spread = up_v + dn_v - 2.0 * here + up_w + dn_w - 2.0 * here
+                up = ctl[i, a + 2, pl.ds(at, SUB), :] - ctl_here
+                dn = ctl_here - ctl[i, a, pl.ds(at, SUB), :]
+                right = ctl_up_w - ctl_here
+                left = ctl_here - ctl_dn_w
+                flux_up = jnp.minimum(up, 0.0) * here + jnp.maximum(up, 0.0) * up_v
+                flux_dn = jnp.minimum(dn, 0.0) * dn_v + jnp.maximum(dn, 0.0) * here
+                flux_right = jnp.minimum(right, 0.0) * here + jnp.maximum(right, 0.0) * up_w
+                flux_left = jnp.minimum(left, 0.0) * dn_w + jnp.maximum(left, 0.0) * here
+                flux = flux_up - flux_dn + flux_right - flux_left
+                spread = up_v + dn_v + up_w + dn_w - 4.0 * here
                 fresh[i, a, pl.ds(at, SUB), :] = (
                     here
                     + along_x
-                    + slant(index, second) * (y_near - here)
-                    - (flux_up - flux_dn)
-                    - (flux_right - flux_left)
+                    + steep_y[at // SUB] * (y_near - here)
+                    + CONTROL_COST * flux
                     + VISCOSITY * spread
                 )
             return carry
@@ -465,17 +485,18 @@
     onward = [(v, v + 1) for v in range(groups - 1)]
     back = [(v + 1, v) for v in range(groups - 1)]
 
-    split = rows // 2 + 1
+    bounds = (0, 2 * EARLY, rows + 2 * EARLY + SHIFT, 2 * rows)
     value_halos = [
         lax.ppermute(value_rows(value_next, begin, end), names, value_route)
-        for begin, end in ((0, split), (split, rows))
+        for begin, end in zip(bounds, bounds[1:])
     ]
-    low, high, *parts = edges(value_next, density, cuts)
+    low, high, *parts = edges(value_next, density, value_halos[0], cuts)
     fillers = [lax.ppermute(part, names, over_route) for part in parts[1::2]]
+    mass = lax.psum(jnp.sum(density, axis=(1, 2)), "vel") / (second * second)
+    crowding = CROWDING * mass * mass
+    low, high, crowding = lax.optimization_barrier((low, high, crowding))
     low = lax.ppermute(low, "vel", onward)
     high = lax.ppermute(high, "vel", back)
-    mass = lax.psum(jnp.sum(density, axis=(1, 2)), "vel") / (second * second)
-    crowding = CROWDING * mass * mass
 
     held = (parts[::2], value_halos, crowding, low, high, fillers)
     parts, value_halos, crowding, low, high, _ = lax.optimization_barrier(held)

time: 100 us -> 100 us (level)
  blocking collectives: 9.24 us -> 6.65 us
  waiting for transfers between devices: 23.7 us -> 24.8 us
    ppermute x2, waiting for transfers between devices: 13.2 us -> 5.1 us  [body(): fillers = [lax.ppermute(part, names, over_route) for part in parts[1::2]]]
    ppermute x2 -> x3, waiting for transfers between devices: 1.6 us -> 9.09 us  [body(): lax.ppermute(value_rows(value_next, begin, end), names, value_route)]
    ppermute x2, starting transfers between devices: 9.6 us -> 5.89 us  [body(): fillers = [lax.ppermute(part, names, over_route) for part in parts[1::2]]]
    ppermute x1, waiting for transfers between devices: 0.01 us -> 2.61 us  [body(): high = lax.ppermute(high, 'vel', back)]
    psum x1, blocking collectives: 9.24 us -> 6.65 us  [body(): mass = lax.psum(jnp.sum(density, axis=(1, 2)), 'vel') / (second * second)]
    ppermute x1, starting transfers between devices: 1.31 us -> 3.63 us  [body(): low_now = lax.ppermute(low_now, 'vel', onward)]
    ppermute x2 -> x3, starting transfers between devices: 7.38 us -> 9.2 us  [body(): lax.ppermute(value_rows(value_next, begin, end), names, value_route)]
    ppermute x1, starting transfers between devices: 1.32 us -> 2.42 us  [body(): low = lax.ppermute(low, 'vel', onward)]
  transfers between devices with their start and end apart: 12 -> 13, of which waited for: 7 -> 8; matrix products, arithmetic and copies ran while one was open for 2% -> 2% of each run, Pallas kernels for 34% -> 35%
where the time goes in v6:
time: 100 us; the launch traced here: 99 us
  Pallas kernels  36.6 us (37%)
  starting transfers between devices  27.6 us (28%)
  waiting for transfers between devices  24.8 us (25%)
  blocking collectives  6.65 us (7%)
  other arithmetic  2.46 us (2%)
    pallas_call x1, Pallas kernels, density_step(): pl.pallas_call(density_kernel, out_shape=[jax.ShapeDtypeStruct(density.sh...  13.7 us
    pallas_call x1, Pallas kernels, value_step(): pl.pallas_call(value_kernel, out_shape=[jax.ShapeDtypeStruct(value.shape,...  10.5 us
    ppermute x3, starting transfers between devices, body(): lax.ppermute(value_rows(value_next, begin, end), names, value_route)  9.2 us
    ppermute x3, waiting for transfers between devices, body(): lax.ppermute(value_rows(value_next, begin, end), names, value_route)  9.09 us
    psum x1, blocking collectives, body(): mass = lax.psum(jnp.sum(density, axis=(1, 2)), 'vel') / (second * second)  6.65 us
    ppermute x2, starting transfers between devices, body(): fillers = [lax.ppermute(part, names, over_route) for part in parts[1::2]]  5.89 us
    ppermute x2, waiting for transfers between devices, body(): fillers = [lax.ppermute(part, names, over_route) for part in parts[1::2]]  5.1 us
    pallas_call x3, Pallas kernels, value_rows(): pl.pallas_call(functools.partial(value_rows_kernel, begin), out_shape=[pl...  4.46 us
  transfers between devices with their start and end apart: 13, of which 8 were waited for; matrix products, arithmetic and copies ran while one was open for 2% of the time, Pallas kernels for 35%

profile of v6, /device:TPU:0, one launch (start us, length us, event | category | flops | bytes accessed | tf_op | source)
XLA Modules:
  0.0 99.0 jit_solution(9260511622075734077)
XLA Ops:
  0.6 0.9 value_rows.3
  1.5 3.0 %collective-permute-start = (f32[2,32,512]{2,1,0:T(8,128)S(1)}, f32[2,32,512]{2,1,0:T(8,128)S(1)}, u32[]{:S(2)}, u32[]{:S(2)}) collective-permute-start(f32[2,32,512]{2,1,0:T(8,128)S(1)} %value_rows.3), channel_id=1, source_target_pairs={{0,1},{8,9},{16,23},{24,31},{1,2},{9,10},{17,16},{25,24},{2,3},{10... | collective-permute-start | bytes 393224 | tf_op jit(solution)/shard_map/ppermute | solution.py:490
  4.5 1.5 %value_rows.4 = f32[19,32,512]{2,1,0:T(8,128)S(1)} custom-call(f32[2,16,64,512]{3,2,1,0:T(8,128)} %value.9), custom_call_target="tpu_custom_call" | custom-call | tf_op jit(solution)/shard_map/value_rows/pallas_call | solution.py:95
  6.0 1.6 %collective-permute-start.1 = (f32[19,32,512]{2,1,0:T(8,128)S(1)}, f32[19,32,512]{2,1,0:T(8,128)S(1)}, u32[]{:S(2)}, u32[]{:S(2)}) collective-permute-start(f32[19,32,512]{2,1,0:T(8,128)S(1)} %value_rows.4), channel_id=1, source_target_pairs={{0,1},{8,9},{16,23},{24,31},{1,2},{9,10},{17,16},{25,24},{2,3},{10... | collective-permute-start | bytes 3735560 | tf_op jit(solution)/shard_map/ppermute | solution.py:490
  7.6 3.6 %collective-permute-done.after.rest_0_ = f32[2,32,512]{2,1,0:T(8,128)S(1)} collective-permute-done((f32[2,32,512]{2,1,0:T(8,128)S(1)}, f32[2,32,512]{2,1,0:T(8,128)S(1)}, u32[]{:S(2)}, u32[]{:S(2)}) %collective-permute-start) | collective-permute-done | bytes 131104 | tf_op jit(solution)/shard_map/ppermute | solution.py:490
  11.2 3.3 %edges.1 = (f32[2,2,64,512]{3,2,1,0:T(8,128)}, f32[2,2,64,512]{3,2,1,0:T(8,128)}, f32[5,64,512]{2,1,0:T(8,128)}, f32[7,64,512]{2,1,0:T(8,128)}, f32[2,64,512]{2,1,0:T(8,128)}, /*index=5*/f32[2,64,512]{2,1,0:T(8,128)}) custom-call(f32[2,16,64,512]{3,2,1,0:T(8,128)} %value.9, f32[2,16,64,512]{3,2,1,0:T(8,128)} %density.3, ...), custom_call_target="tpu_custom_call" | custom-call | tf_op jit(solution)/shard_map/edges/pallas_call | solution.py:124
  14.5 3.5 %collective-permute-start.5 = (f32[7,64,512]{2,1,0:T(8,128)}, f32[7,64,512]{2,1,0:T(8,128)}, u32[]{:S(2)}, u32[]{:S(2)}) collective-permute-start(f32[7,64,512]{2,1,0:T(8,128)} %get-tuple-element.31), channel_id=1, source_target_pairs={{0,6},{8,14},{16,16},{24,24},{1,1},{9,9},{17,19},{25,27},{2,0},{10... | collective-permute-start | bytes 2752520 | tf_op jit(solution)/shard_map/ppermute | solution.py:494
  18.1 2.4 %collective-permute-start.6 = (f32[2,64,512]{2,1,0:T(8,128)}, f32[2,64,512]{2,1,0:T(8,128)}, u32[]{:S(2)}, u32[]{:S(2)}) collective-permute-start(f32[2,64,512]{2,1,0:T(8,128)} %get-tuple-element.32), channel_id=1, source_target_pairs={{0,6},{8,14},{16,16},{24,24},{1,1},{9,9},{17,19},{25,27},{2,0},{10... | collective-permute-start | bytes 786440 | tf_op jit(solution)/shard_map/ppermute | solution.py:494
  20.4 2.1 %value_rows.5 = f32[11,32,512]{2,1,0:T(8,128)} custom-call(f32[2,16,64,512]{3,2,1,0:T(8,128)} %value.9), custom_call_target="tpu_custom_call" | custom-call | tf_op jit(solution)/shard_map/value_rows/pallas_call | solution.py:95
  22.5 4.6 %collective-permute-start.2 = (f32[11,32,512]{2,1,0:T(8,128)}, f32[11,32,512]{2,1,0:T(8,128)S(1)}, u32[]{:S(2)}, u32[]{:S(2)}) collective-permute-start(f32[11,32,512]{2,1,0:T(8,128)} %value_rows.5), channel_id=1, source_target_pairs={{0,1},{8,9},{16,23},{24,31},{1,2},{9,10},{17,16},{25,24},{2,3},{10... | collective-permute-start | bytes 2162696 | tf_op jit(solution)/shard_map/ppermute | solution.py:490
  27.1 2.5 %reduce_sum.9 = f32[2,512]{1,0:T(2,128)S(1)} reduce(f32[2,16,64,512]{3,2,1,0:T(8,128)} %density.3, f32[]{:T(128)} %constant.2.clone.1), dimensions={1,2}, to_apply=%region_0.0 | reduce | flops 1047552 | bytes 4198404 | tf_op jit(solution)/shard_map/reduce_sum | solution.py:495
  29.6 6.7 %psum.7 = f32[2,512]{1,0:T(2,128)S(1)} all-reduce(f32[2,512]{1,0:T(2,128)S(1)} %reduce_sum.9), channel_id=1, replica_groups=mesh['vel'=4,'pos'=8] {'vel'}, use_global_device_ids=true, to_apply=%region_1.0 | all-reduce | flops 1024 | bytes 8192 | tf_op jit(solution)/shard_map/psum | solution.py:495
  36.3 2.4 %collective-permute-start.3 = (f32[2,2,64,512]{3,2,1,0:T(8,128)}, f32[2,2,64,512]{3,2,1,0:T(8,128)S(1)}, u32[]{:S(2)}, u32[]{:S(2)}) collective-permute-start(f32[2,2,64,512]{3,2,1,0:T(8,128)} %get-tuple-element.29), channel_id=1, source_target_pairs={{0,8},{8,16},{16,24},{1,9},{9,17},{17,25},{2,10},{10,18},{18,26},{... | collective-permute-start | bytes 1572872 | tf_op jit(solution)/shard_map/ppermute | solution.py:498
  38.7 5.1 %collective-permute-done.6 = f32[2,64,512]{2,1,0:T(8,128)} collective-permute-done((f32[2,64,512]{2,1,0:T(8,128)}, f32[2,64,512]{2,1,0:T(8,128)}, u32[]{:S(2)}, u32[]{:S(2)}) %collective-permute-start.6) | collective-permute-done | bytes 262176 | tf_op jit(solution)/shard_map/ppermute | solution.py:494
  43.8 1.3 %collective-permute-start.4 = (f32[2,2,64,512]{3,2,1,0:T(8,128)}, f32[2,2,64,512]{3,2,1,0:T(8,128)S(1)}, u32[]{:S(2)}, u32[]{:S(2)}) collective-permute-start(f32[2,2,64,512]{3,2,1,0:T(8,128)} %get-tuple-element.30), channel_id=1, source_target_pairs={{8,0},{16,8},{24,16},{9,1},{17,9},{25,17},{10,2},{18,10},{26,18},{... | collective-permute-start | bytes 1572872 | tf_op jit(solution)/shard_map/ppermute | solution.py:499
  45.1 0.1 collective-permute-start.10
  45.2 0.0 collective-permute-done.3.low
  45.2 2.6 %collective-permute-done.4.high = f32[2,2,64,512]{3,2,1,0:T(8,128)S(1)} collective-permute-done((f32[2,2,64,512]{3,2,1,0:T(8,128)}, f32[2,2,64,512]{3,2,1,0:T(8,128)S(1)}, u32[]{:S(2)}, u32[]{:S(2)}) %collective-permute-start.4) | collective-permute-done | bytes 524320 | tf_op jit(solution)/shard_map/ppermute | solution.py:499
  47.8 5.5 %collective-permute-done.2.rest_2_ = f32[11,32,512]{2,1,0:T(8,128)S(1)} collective-permute-done((f32[11,32,512]{2,1,0:T(8,128)}, f32[11,32,512]{2,1,0:T(8,128)S(1)}, u32[]{:S(2)}, u32[]{:S(2)}) %collective-permute-start.2) | collective-permute-done | bytes 720928 | tf_op jit(solution)/shard_map/ppermute | solution.py:490
  53.3 2.8 %collective-permute-start.9 = (f32[5,64,512]{2,1,0:T(8,128)}, f32[5,64,512]{2,1,0:T(8,128)S(1)}, u32[]{:S(2)}, u32[]{:S(2)}) collective-permute-start(f32[5,64,512]{2,1,0:T(8,128)} %get-tuple-element.43), channel_id=1, source_target_pairs={{0,7},{8,15},{16,17},{24,25},{1,0},{9,8},{17,18},{25,26},{2,1},{10... | collective-permute-start | bytes 1966088 | tf_op jit(solution)/shard_map/ppermute | solution.py:504
  56.1 10.5 %value_step.1 = (f32[2,16,64,512]{3,2,1,0:T(8,128)}, f32[2,64,512]{2,1,0:T(8,128)S(1)}, f32[2,64,512]{2,1,0:T(8,128)S(1)}) custom-call(f32[2,16,64,512]{3,2,1,0:T(8,128)} %value.9, f32[2,2,64,512]{3,2,1,0:T(8,128)S(1)} %collective-permute-done.3.low, f32[2,2,64,512]{3,2,1,0:T(8,128)S(1)} %collective-permute-done.4.high, ...), custom_call_target="tpu_custom_call" | custom-call | tf_op jit(solution)/shard_map/value_step/pallas_call | solution.py:245
  66.6 3.6 %collective-permute-start.7 = (f32[2,64,512]{2,1,0:T(8,128)S(1)}, f32[2,64,512]{2,1,0:T(8,128)S(1)}, u32[]{:S(2)}, u32[]{:S(2)}) collective-permute-start(f32[2,64,512]{2,1,0:T(8,128)S(1)} %get-tuple-element.40), channel_id=1, source_target_pairs={{0,8},{8,16},{16,24},{1,9},{9,17},{17,25},{2,10},{10,18},{18,26},{... | collective-permute-start | bytes 786440 | tf_op jit(solution)/shard_map/ppermute | solution.py:507
  70.3 1.3 %collective-permute-start.8 = (f32[2,64,512]{2,1,0:T(8,128)S(1)}, f32[2,64,512]{2,1,0:T(8,128)S(1)}, u32[]{:S(2)}, u32[]{:S(2)}) collective-permute-start(f32[2,64,512]{2,1,0:T(8,128)S(1)} %get-tuple-element.41), channel_id=1, source_target_pairs={{8,0},{16,8},{24,16},{9,1},{17,9},{25,17},{10,2},{18,10},{26,18},{... | collective-permute-start | bytes 786440 | tf_op jit(solution)/shard_map/ppermute | solution.py:508
  71.6 0.1 collective-permute-start.12
  71.7 1.0 collective-permute-start.11
  72.7 1.1 %collective-permute-done.8.high_now = f32[2,64,512]{2,1,0:T(8,128)S(1)} collective-permute-done((f32[2,64,512]{2,1,0:T(8,128)S(1)}, f32[2,64,512]{2,1,0:T(8,128)S(1)}, u32[]{:S(2)}, u32[]{:S(2)}) %collective-permute-start.8) | collective-permute-done | bytes 262176 | tf_op jit(solution)/shard_map/ppermute | solution.py:508
  73.7 13.7 %density_step.1 = (f32[2,16,64,512]{3,2,1,0:T(8,128)}, f32[4,64,512]{2,1,0:T(8,128)S(1)}) custom-call(f32[2,16,64,512]{3,2,1,0:T(8,128)} %density.3, f32[2,16,64,512]{3,2,1,0:T(8,128)} %get-tuple-element.22.control, f32[2,2,64,512]{3,2,1,0:T(8,128)S(1)} %collective-permute-done.3.low, f32[2,2,64,512]{3,2,1,0:T(8,128)S(1)} %collective-permute-done.4.high, ...), custom_call_target="tpu_custom_call" | custom-call | tf_op jit(solution)/shard_map/density_step/pallas_call | solution.py:346
  87.4 2.9 %collective-permute-done.10.refs_1_ = f32[7,64,512]{2,1,0:T(8,128)S(1)} collective-permute-done((f32[7,64,512]{2,1,0:T(8,128)}, f32[7,64,512]{2,1,0:T(8,128)S(1)}, u32[]{:S(2)}, u32[]{:S(2)}) %collective-permute-start.10) | collective-permute-done | bytes 917536 | tf_op jit(solution)/shard_map/ppermute | solution.py:503
  90.3 3.8 %arrive.1.partial = f32[2,16,64,512]{3,2,1,0:T(8,128)} custom-call(f32[2,16,64,512]{3,2,1,0:T(8,128)} %get-tuple-element.42.partial, f32[5,64,512]{2,1,0:T(8,128)S(1)} %collective-permute-done.9.refs_0_, f32[7,64,512]{2,1,0:T(8,128)S(1)} %collective-permute-done.10.refs_1_), custom_call_target="tpu_custom_call", output_to_operand_aliasing={{}: (0, {})} | custom-call | tf_op jit(solution)/shard_map/arrive/pallas_call | solution.py:396
  94.1 0.4 collective-permute-done.12.refs_1_
  94.5 3.7 %collective-permute-done.11.refs_0_ = f32[2,64,512]{2,1,0:T(8,128)S(1)} collective-permute-done((f32[2,64,512]{2,1,0:T(8,128)S(1)}, f32[2,64,512]{2,1,0:T(8,128)S(1)}, u32[]{:S(2)}, u32[]{:S(2)}) %collective-permute-start.11) | collective-permute-done | bytes 262176 | tf_op jit(solution)/shard_map/ppermute | solution.py:504
  98.1 0.8 arrive_last.1
  (7 shorter events, 0.0 us)
Async XLA Ops:
  1.5 9.6 %collective-permute-start = (f32[2,32,512]{2,1,0:T(8,128)S(1)}, f32[2,32,512]{2,1,0:T(8,128)S(1)}, u32[]{:S(2)}, u32[]{:S(2)}) collective-permute-start(f32[2,32,512]{2,1,0:T(8,128)S(1)} %value_rows.3), channel_id=1, source_target_pairs={{0,1},{8,9},{16,23},{24,31},{1,2},{9,10},{17,16},{25,24},{2,3},{10... | collective-permute-start | bytes 393224 | tf_op jit(solution)/shard_map/ppermute | solution.py:490
  6.0 47.3 %collective-permute-start.1 = (f32[19,32,512]{2,1,0:T(8,128)S(1)}, f32[19,32,512]{2,1,0:T(8,128)S(1)}, u32[]{:S(2)}, u32[]{:S(2)}) collective-permute-start(f32[19,32,512]{2,1,0:T(8,128)S(1)} %value_rows.4), channel_id=1, source_target_pairs={{0,1},{8,9},{16,23},{24,31},{1,2},{9,10},{17,16},{25,24},{2,3},{10... | collective-permute-start | bytes 3735560 | tf_op jit(solution)/shard_map/ppermute | solution.py:490
  14.5 30.6 %collective-permute-start.5 = (f32[7,64,512]{2,1,0:T(8,128)}, f32[7,64,512]{2,1,0:T(8,128)}, u32[]{:S(2)}, u32[]{:S(2)}) collective-permute-start(f32[7,64,512]{2,1,0:T(8,128)} %get-tuple-element.31), channel_id=1, source_target_pairs={{0,6},{8,14},{16,16},{24,24},{1,1},{9,9},{17,19},{25,27},{2,0},{10... | collective-permute-start | bytes 2752520 | tf_op jit(solution)/shard_map/ppermute | solution.py:494
  18.1 25.7 %collective-permute-start.6 = (f32[2,64,512]{2,1,0:T(8,128)}, f32[2,64,512]{2,1,0:T(8,128)}, u32[]{:S(2)}, u32[]{:S(2)}) collective-permute-start(f32[2,64,512]{2,1,0:T(8,128)} %get-tuple-element.32), channel_id=1, source_target_pairs={{0,6},{8,14},{16,16},{24,24},{1,1},{9,9},{17,19},{25,27},{2,0},{10... | collective-permute-start | bytes 786440 | tf_op jit(solution)/shard_map/ppermute | solution.py:494
  22.5 30.8 %collective-permute-start.2 = (f32[11,32,512]{2,1,0:T(8,128)}, f32[11,32,512]{2,1,0:T(8,128)S(1)}, u32[]{:S(2)}, u32[]{:S(2)}) collective-permute-start(f32[11,32,512]{2,1,0:T(8,128)} %value_rows.5), channel_id=1, source_target_pairs={{0,1},{8,9},{16,23},{24,31},{1,2},{9,10},{17,16},{25,24},{2,3},{10... | collective-permute-start | bytes 2162696 | tf_op jit(solution)/shard_map/ppermute | solution.py:490
  36.2 35.4 %copy-start = (f32[2,64,512]{2,1,0:T(8,128)S(1)}, f32[2,64,512]{2,1,0:T(8,128)}, u32[]{:S(2)}) copy-start(f32[2,64,512]{2,1,0:T(8,128)} %get-tuple-element.45) | copy-start | bytes 786436
  36.3 8.9 %collective-permute-start.3 = (f32[2,2,64,512]{3,2,1,0:T(8,128)}, f32[2,2,64,512]{3,2,1,0:T(8,128)S(1)}, u32[]{:S(2)}, u32[]{:S(2)}) collective-permute-start(f32[2,2,64,512]{3,2,1,0:T(8,128)} %get-tuple-element.29), channel_id=1, source_target_pairs={{0,8},{8,16},{16,24},{1,9},{9,17},{17,25},{2,10},{10,18},{18,26},{... | collective-permute-start | bytes 1572872 | tf_op jit(solution)/shard_map/ppermute | solution.py:498
  43.8 4.0 %collective-permute-start.4 = (f32[2,2,64,512]{3,2,1,0:T(8,128)}, f32[2,2,64,512]{3,2,1,0:T(8,128)S(1)}, u32[]{:S(2)}, u32[]{:S(2)}) collective-permute-start(f32[2,2,64,512]{3,2,1,0:T(8,128)} %get-tuple-element.30), channel_id=1, source_target_pairs={{8,0},{16,8},{24,16},{9,1},{17,9},{25,17},{10,2},{18,10},{26,18},{... | collective-permute-start | bytes 1572872 | tf_op jit(solution)/shard_map/ppermute | solution.py:499
  45.1 45.2 %collective-permute-start.10 = (f32[7,64,512]{2,1,0:T(8,128)}, f32[7,64,512]{2,1,0:T(8,128)S(1)}, u32[]{:S(2)}, u32[]{:S(2)}) collective-permute-start(f32[7,64,512]{2,1,0:T(8,128)} %collective-permute-done.5), channel_id=1, source_target_pairs={{0,1},{8,9},{16,17},{24,25},{1,0},{9,8},{17,16},{25,24},{2,3},{10,... | collective-permute-start | bytes 2752520 | tf_op jit(solution)/shard_map/ppermute | solution.py:503
  53.3 34.1 %collective-permute-start.9 = (f32[5,64,512]{2,1,0:T(8,128)}, f32[5,64,512]{2,1,0:T(8,128)S(1)}, u32[]{:S(2)}, u32[]{:S(2)}) collective-permute-start(f32[5,64,512]{2,1,0:T(8,128)} %get-tuple-element.43), channel_id=1, source_target_pairs={{0,7},{8,15},{16,17},{24,25},{1,0},{9,8},{17,18},{25,26},{2,1},{10... | collective-permute-start | bytes 1966088 | tf_op jit(solution)/shard_map/ppermute | solution.py:504
  66.6 5.0 %collective-permute-start.7 = (f32[2,64,512]{2,1,0:T(8,128)S(1)}, f32[2,64,512]{2,1,0:T(8,128)S(1)}, u32[]{:S(2)}, u32[]{:S(2)}) collective-permute-start(f32[2,64,512]{2,1,0:T(8,128)S(1)} %get-tuple-element.40), channel_id=1, source_target_pairs={{0,8},{8,16},{16,24},{1,9},{9,17},{17,25},{2,10},{10,18},{18,26},{... | collective-permute-start | bytes 786440 | tf_op jit(solution)/shard_map/ppermute | solution.py:507
  70.3 3.4 %collective-permute-start.8 = (f32[2,64,512]{2,1,0:T(8,128)S(1)}, f32[2,64,512]{2,1,0:T(8,128)S(1)}, u32[]{:S(2)}, u32[]{:S(2)}) collective-permute-start(f32[2,64,512]{2,1,0:T(8,128)S(1)} %get-tuple-element.41), channel_id=1, source_target_pairs={{8,0},{16,8},{24,16},{9,1},{17,9},{25,17},{10,2},{18,10},{26,18},{... | collective-permute-start | bytes 786440 | tf_op jit(solution)/shard_map/ppermute | solution.py:508
  71.6 22.9 %collective-permute-start.12 = (f32[2,64,512]{2,1,0:T(8,128)}, f32[2,64,512]{2,1,0:T(8,128)S(1)}, u32[]{:S(2)}, u32[]{:S(2)}) collective-permute-start(f32[2,64,512]{2,1,0:T(8,128)} %collective-permute-done.6), channel_id=1, source_target_pairs={{0,1},{8,9},{16,17},{24,25},{1,0},{9,8},{17,16},{25,24},{2,3},{10,... | collective-permute-start | bytes 786440 | tf_op jit(solution)/shard_map/ppermute | solution.py:503
  71.7 26.5 %collective-permute-start.11 = (f32[2,64,512]{2,1,0:T(8,128)S(1)}, f32[2,64,512]{2,1,0:T(8,128)S(1)}, u32[]{:S(2)}, u32[]{:S(2)}) collective-permute-start(f32[2,64,512]{2,1,0:T(8,128)S(1)} %copy-done), channel_id=1, source_target_pairs={{0,7},{8,15},{16,17},{24,25},{1,0},{9,8},{17,18},{25,26},{2,1},{10... | collective-permute-start | bytes 786440 | tf_op jit(solution)/shard_map/ppermute | solution.py:504

commit v7 on v6

--- a/solution.py
+++ b/solution.py
@@ -15,7 +15,7 @@
 SUB = 8
 LANES = 128
 EARLY = 1
-SHIFT = 3
+SHIFT = 1
 VMEM_LIMIT = 18 * 1024 * 1024
 ANY = pl.BlockSpec(memory_space=pl.ANY)
 VMEM = pl.BlockSpec(memory_space=pltpu.VMEM)
@@ -411,39 +411,36 @@
     )(in_hbm(partial), *halos)
 
 
-def arrive_last_kernel(partial, rest, *refs):
-    halos, (out, held, sems) = refs[:-3], refs[-3:]
+def arrive_rest_kernel(begin, partial, rest, halo, out, held, sems):
     count, rows = partial.shape[:2]
-    extent = rest.shape[0]
+    extent = halo.shape[0]
+    skipped = begin - (rows - rest.shape[0])
     row = jnp.where(is_negative(), count - 1, 0)
-    base = lax.axis_index("vel") * rows + rows - extent
+    base = lax.axis_index("vel") * rows + begin
     total = rows * lax.axis_size("vel")
     copies = []
-    for halo in halos:
-        for k in range(halo.shape[0]):
-            a = len(copies)
-            held[a] = rest[a] + slant(base + a, total) * halo[k]
-            target = out.at[row, rows - extent + a]
-            copies.append(pltpu.make_async_copy(held.at[a], target, sems.at[a]))
-            copies[-1].start()
+    for a in range(extent):
+        held[a] = rest[skipped + a] + slant(base + a, total) * halo[a]
+        copies.append(pltpu.make_async_copy(held.at[a], out.at[row, begin + a], sems.at[a]))
+        copies[-1].start()
     wait_all(copies)
 
 
-def arrive_last(partial, rest, halos):
+def arrive_rest(partial, rest, halo, begin):
     return pl.pallas_call(
-        arrive_last_kernel,
+        functools.partial(arrive_rest_kernel, begin),
         out_shape=jax.ShapeDtypeStruct(partial.shape, partial.dtype),
-        in_specs=[ANY] + [VMEM] * (1 + len(halos)),
+        in_specs=[ANY, VMEM, VMEM],
         out_specs=ANY,
         scratch_shapes=[
-            pltpu.VMEM(rest.shape, rest.dtype),
-            pltpu.SemaphoreType.DMA((rest.shape[0],)),
+            pltpu.VMEM(halo.shape, halo.dtype),
+            pltpu.SemaphoreType.DMA((halo.shape[0],)),
         ],
         input_output_aliases={0: 0},
         compiler_params=pltpu.CompilerParams(vmem_limit_bytes=VMEM_LIMIT),
         cost_estimate=LIGHT,
-        name="arrive_last",
-    )(in_hbm(partial), in_vmem(rest), *[in_vmem(halo) for halo in halos])
+        name="arrive_rest",
+    )(in_hbm(partial), in_vmem(rest), in_vmem(halo))
 
 
 def routes(mesh):
@@ -474,13 +471,13 @@
     names, value_route, density_route, over_route, swap_route = routes(mesh)
     groups = mesh.shape["vel"]
     count, rows, second, width = value_next.shape
-    tail = max(1, rows // 8)
-    near = rows // 2 - tail - 1
+    last, filler = max(1, rows // 16), max(1, rows // 8)
+    near = rows // 2 - 2 * last
     cuts = (
         (0, near),
-        (near, rows - 2 * tail),
-        (rows - 2 * tail, rows - tail),
-        (rows - tail, rows),
+        (near, rows - last - filler),
+        (rows - last - filler, rows - filler),
+        (rows - filler, rows),
     )
     onward = [(v, v + 1) for v in range(groups - 1)]
     back = [(v + 1, v) for v in range(groups - 1)]
@@ -507,10 +504,11 @@
     low_now = lax.ppermute(low_now, "vel", onward)
     high_now = lax.ppermute(high_now, "vel", back)
     density_next, rest = density_step(
-        density, value_now, low, high, low_now, high_now, 2 * tail
+        density, value_now, low, high, low_now, high_now, last + filler
     )
     density_next = arrive(density_next, (parts[0], fillers[0]))
-    density_next = arrive_last(density_next, rest, (parts[1], fillers[1]))
+    density_next = arrive_rest(density_next, rest, fillers[1], cuts[3][0])
+    density_next = arrive_rest(density_next, rest, parts[1], cuts[2][0])
     return value_now, density_next
 
 

time: 100 us -> 99.8 us (level)
  starting transfers between devices: 27.6 us -> 30.1 us
  waiting for transfers between devices: 24.8 us -> 22.3 us
    ppermute x2, starting transfers between devices: 5.89 us -> 10.2 us  [body(): fillers = [lax.ppermute(part, names, over_route) for part in parts[1::2]]]
    ppermute x2, waiting for transfers between devices: 5.1 us -> 3.28 us  [body(): fillers = [lax.ppermute(part, names, over_route) for part in parts[1::2]]]
    ppermute x2, waiting for transfers between devices: 3.3 us -> 1.63 us  [body(): fillers = [lax.ppermute(part, names, swap_route) for part in fillers]]
    ppermute x3, starting transfers between devices: 9.2 us -> 7.95 us  [body(): lax.ppermute(value_rows(value_next, begin, end), names, value_route)]
  transfers between devices with their start and end apart: 13 -> 13, of which waited for: 8 -> 9; matrix products, arithmetic and copies ran while one was open for 2% -> 2% of each run, Pallas kernels for 35% -> 36%
where the time goes in v7:
time: 99.8 us; the launch traced here: 98.8 us
  Pallas kernels  37.2 us (37%)
  starting transfers between devices  30.1 us (30%)
  waiting for transfers between devices  22.3 us (22%)
  blocking collectives  5.96 us (6%)
  other arithmetic  2.46 us (2%)
    pallas_call x1, Pallas kernels, density_step(): pl.pallas_call(density_kernel, out_shape=[jax.ShapeDtypeStruct(density.sh...  13.6 us
    pallas_call x1, Pallas kernels, value_step(): pl.pallas_call(value_kernel, out_shape=[jax.ShapeDtypeStruct(value.shape,...  10.2 us
    ppermute x2, starting transfers between devices, body(): fillers = [lax.ppermute(part, names, over_route) for part in parts[1::2]]  10.2 us
    ppermute x3, waiting for transfers between devices, body(): lax.ppermute(value_rows(value_next, begin, end), names, value_route)  9.19 us
    ppermute x3, starting transfers between devices, body(): lax.ppermute(value_rows(value_next, begin, end), names, value_route)  7.95 us
    psum x1, blocking collectives, body(): mass = lax.psum(jnp.sum(density, axis=(1, 2)), 'vel') / (second * second)  5.96 us
    ppermute x2, waiting for transfers between devices, body(): parts = [lax.ppermute(part, names, density_route) for part in parts]  4.65 us
    pallas_call x3, Pallas kernels, value_rows(): pl.pallas_call(functools.partial(value_rows_kernel, begin), out_shape=[pl...  4.5 us
  transfers between devices with their start and end apart: 13, of which 9 were waited for; matrix products, arithmetic and copies ran while one was open for 2% of the time, Pallas kernels for 36%

profile of v7, /device:TPU:0, one launch (start us, length us, event | category | flops | bytes accessed | tf_op | source)
XLA Modules:
  0.0 98.8 jit_solution(6385958672490745154)
XLA Ops:
  0.6 0.9 value_rows.3
  1.5 3.0 %collective-permute-start = (f32[2,32,512]{2,1,0:T(8,128)S(1)}, f32[2,32,512]{2,1,0:T(8,128)S(1)}, u32[]{:S(2)}, u32[]{:S(2)}) collective-permute-start(f32[2,32,512]{2,1,0:T(8,128)S(1)} %value_rows.3), channel_id=1, source_target_pairs={{0,1},{8,9},{16,23},{24,31},{1,2},{9,10},{17,16},{25,24},{2,3},{10... | collective-permute-start | bytes 393224 | tf_op jit(solution)/shard_map/ppermute | solution.py:487
  4.5 1.4 %value_rows.4 = f32[17,32,512]{2,1,0:T(8,128)S(1)} custom-call(f32[2,16,64,512]{3,2,1,0:T(8,128)} %value.9), custom_call_target="tpu_custom_call" | custom-call | tf_op jit(solution)/shard_map/value_rows/pallas_call | solution.py:95
  5.9 1.6 %collective-permute-start.1 = (f32[17,32,512]{2,1,0:T(8,128)S(1)}, f32[17,32,512]{2,1,0:T(8,128)S(1)}, u32[]{:S(2)}, u32[]{:S(2)}) collective-permute-start(f32[17,32,512]{2,1,0:T(8,128)S(1)} %value_rows.4), channel_id=1, source_target_pairs={{0,1},{8,9},{16,23},{24,31},{1,2},{9,10},{17,16},{25,24},{2,3},{10... | collective-permute-start | bytes 3342344 | tf_op jit(solution)/shard_map/ppermute | solution.py:487
  7.5 3.7 %collective-permute-done.after.rest_0_ = f32[2,32,512]{2,1,0:T(8,128)S(1)} collective-permute-done((f32[2,32,512]{2,1,0:T(8,128)S(1)}, f32[2,32,512]{2,1,0:T(8,128)S(1)}, u32[]{:S(2)}, u32[]{:S(2)}) %collective-permute-start) | collective-permute-done | bytes 131104 | tf_op jit(solution)/shard_map/ppermute | solution.py:487
  11.2 3.5 %edges.1 = (f32[2,2,64,512]{3,2,1,0:T(8,128)}, f32[2,2,64,512]{3,2,1,0:T(8,128)}, f32[6,64,512]{2,1,0:T(8,128)}, f32[7,64,512]{2,1,0:T(8,128)}, f32[1,64,512]{2,1,0:T(8,128)}, /*index=5*/f32[2,64,512]{2,1,0:T(8,128)}) custom-call(f32[2,16,64,512]{3,2,1,0:T(8,128)} %value.9, f32[2,16,64,512]{3,2,1,0:T(8,128)} %density.3, ...), custom_call_target="tpu_custom_call" | custom-call | tf_op jit(solution)/shard_map/edges/pallas_call | solution.py:124
  14.7 3.5 %collective-permute-start.5 = (f32[7,64,512]{2,1,0:T(8,128)}, f32[7,64,512]{2,1,0:T(8,128)}, u32[]{:S(2)}, u32[]{:S(2)}) collective-permute-start(f32[7,64,512]{2,1,0:T(8,128)} %get-tuple-element.31), channel_id=1, source_target_pairs={{0,6},{8,14},{16,16},{24,24},{1,1},{9,9},{17,19},{25,27},{2,0},{10... | collective-permute-start | bytes 2752520 | tf_op jit(solution)/shard_map/ppermute | solution.py:491
  18.2 2.2 %value_rows.5 = f32[13,32,512]{2,1,0:T(8,128)} custom-call(f32[2,16,64,512]{3,2,1,0:T(8,128)} %value.9), custom_call_target="tpu_custom_call" | custom-call | tf_op jit(solution)/shard_map/value_rows/pallas_call | solution.py:95
  20.4 3.4 %collective-permute-start.2 = (f32[13,32,512]{2,1,0:T(8,128)}, f32[13,32,512]{2,1,0:T(8,128)S(1)}, u32[]{:S(2)}, u32[]{:S(2)}) collective-permute-start(f32[13,32,512]{2,1,0:T(8,128)} %value_rows.5), channel_id=1, source_target_pairs={{0,1},{8,9},{16,23},{24,31},{1,2},{9,10},{17,16},{25,24},{2,3},{10... | collective-permute-start | bytes 2555912 | tf_op jit(solution)/shard_map/ppermute | solution.py:487
  23.8 6.6 %collective-permute-start.6 = (f32[2,64,512]{2,1,0:T(8,128)}, f32[2,64,512]{2,1,0:T(8,128)S(1)}, u32[]{:S(2)}, u32[]{:S(2)}) collective-permute-start(f32[2,64,512]{2,1,0:T(8,128)} %get-tuple-element.32), channel_id=1, source_target_pairs={{0,6},{8,14},{16,16},{24,24},{1,1},{9,9},{17,19},{25,27},{2,0},{10... | collective-permute-start | bytes 786440 | tf_op jit(solution)/shard_map/ppermute | solution.py:491
  30.4 2.5 %reduce_sum.9 = f32[2,512]{1,0:T(2,128)S(1)} reduce(f32[2,16,64,512]{3,2,1,0:T(8,128)} %density.3, f32[]{:T(128)} %constant.2.clone.1), dimensions={1,2}, to_apply=%region_0.0 | reduce | flops 1047552 | bytes 4198404 | tf_op jit(solution)/shard_map/reduce_sum | solution.py:492
  32.9 6.0 %psum.7 = f32[2,512]{1,0:T(2,128)S(1)} all-reduce(f32[2,512]{1,0:T(2,128)S(1)} %reduce_sum.9), channel_id=1, replica_groups=mesh['vel'=4,'pos'=8] {'vel'}, use_global_device_ids=true, to_apply=%region_1.0 | all-reduce | flops 1024 | bytes 8192 | tf_op jit(solution)/shard_map/psum | solution.py:492
  38.9 1.6 %collective-permute-start.3 = (f32[2,2,64,512]{3,2,1,0:T(8,128)}, f32[2,2,64,512]{3,2,1,0:T(8,128)S(1)}, u32[]{:S(2)}, u32[]{:S(2)}) collective-permute-start(f32[2,2,64,512]{3,2,1,0:T(8,128)} %get-tuple-element.29), channel_id=1, source_target_pairs={{0,8},{8,16},{16,24},{1,9},{9,17},{17,25},{2,10},{10,18},{18,26},{... | collective-permute-start | bytes 1572872 | tf_op jit(solution)/shard_map/ppermute | solution.py:495
  40.5 3.3 %collective-permute-done.6 = f32[2,64,512]{2,1,0:T(8,128)S(1)} collective-permute-done((f32[2,64,512]{2,1,0:T(8,128)}, f32[2,64,512]{2,1,0:T(8,128)S(1)}, u32[]{:S(2)}, u32[]{:S(2)}) %collective-permute-start.6) | collective-permute-done | bytes 262176 | tf_op jit(solution)/shard_map/ppermute | solution.py:491
  43.8 1.3 %collective-permute-start.4 = (f32[2,2,64,512]{3,2,1,0:T(8,128)}, f32[2,2,64,512]{3,2,1,0:T(8,128)S(1)}, u32[]{:S(2)}, u32[]{:S(2)}) collective-permute-start(f32[2,2,64,512]{3,2,1,0:T(8,128)} %get-tuple-element.30), channel_id=1, source_target_pairs={{8,0},{16,8},{24,16},{9,1},{17,9},{25,17},{10,2},{18,10},{26,18},{... | collective-permute-start | bytes 1572872 | tf_op jit(solution)/shard_map/ppermute | solution.py:496
  45.2 2.6 %collective-permute-done.4.high = f32[2,2,64,512]{3,2,1,0:T(8,128)S(1)} collective-permute-done((f32[2,2,64,512]{3,2,1,0:T(8,128)}, f32[2,2,64,512]{3,2,1,0:T(8,128)S(1)}, u32[]{:S(2)}, u32[]{:S(2)}) %collective-permute-start.4) | collective-permute-done | bytes 524320 | tf_op jit(solution)/shard_map/ppermute | solution.py:496
  47.8 5.5 %collective-permute-done.2.rest_2_ = f32[13,32,512]{2,1,0:T(8,128)S(1)} collective-permute-done((f32[13,32,512]{2,1,0:T(8,128)}, f32[13,32,512]{2,1,0:T(8,128)S(1)}, u32[]{:S(2)}, u32[]{:S(2)}) %collective-permute-start.2) | collective-permute-done | bytes 852000 | tf_op jit(solution)/shard_map/ppermute | solution.py:487
  53.3 2.8 %collective-permute-start.9 = (f32[6,64,512]{2,1,0:T(8,128)}, f32[6,64,512]{2,1,0:T(8,128)S(1)}, u32[]{:S(2)}, u32[]{:S(2)}) collective-permute-start(f32[6,64,512]{2,1,0:T(8,128)} %get-tuple-element.43), channel_id=1, source_target_pairs={{0,7},{8,15},{16,17},{24,25},{1,0},{9,8},{17,18},{25,26},{2,1},{10... | collective-permute-start | bytes 2359304 | tf_op jit(solution)/shard_map/ppermute | solution.py:501
  56.1 10.2 %value_step.1 = (f32[2,16,64,512]{3,2,1,0:T(8,128)}, f32[2,64,512]{2,1,0:T(8,128)S(1)}, f32[2,64,512]{2,1,0:T(8,128)S(1)}) custom-call(f32[2,16,64,512]{3,2,1,0:T(8,128)} %value.9, f32[2,2,64,512]{3,2,1,0:T(8,128)S(1)} %collective-permute-done.3.low, f32[2,2,64,512]{3,2,1,0:T(8,128)S(1)} %collective-permute-done.4.high, ...), custom_call_target="tpu_custom_call" | custom-call | tf_op jit(solution)/shard_map/value_step/pallas_call | solution.py:245
  66.3 3.8 %collective-permute-start.7 = (f32[2,64,512]{2,1,0:T(8,128)S(1)}, f32[2,64,512]{2,1,0:T(8,128)S(1)}, u32[]{:S(2)}, u32[]{:S(2)}) collective-permute-start(f32[2,64,512]{2,1,0:T(8,128)S(1)} %get-tuple-element.40), channel_id=1, source_target_pairs={{0,8},{8,16},{16,24},{1,9},{9,17},{17,25},{2,10},{10,18},{18,26},{... | collective-permute-start | bytes 786440 | tf_op jit(solution)/shard_map/ppermute | solution.py:504
  70.1 1.3 %collective-permute-start.8 = (f32[2,64,512]{2,1,0:T(8,128)S(1)}, f32[2,64,512]{2,1,0:T(8,128)S(1)}, u32[]{:S(2)}, u32[]{:S(2)}) collective-permute-start(f32[2,64,512]{2,1,0:T(8,128)S(1)} %get-tuple-element.41), channel_id=1, source_target_pairs={{8,0},{16,8},{24,16},{9,1},{17,9},{25,17},{10,2},{18,10},{26,18},{... | collective-permute-start | bytes 786440 | tf_op jit(solution)/shard_map/ppermute | solution.py:505
  71.4 0.1 collective-permute-start.11
  71.5 1.1 %collective-permute-start.12 = (f32[1,64,512]{2,1,0:T(8,128)S(1)}, f32[1,64,512]{2,1,0:T(8,128)S(1)}, u32[]{:S(2)}, u32[]{:S(2)}) collective-permute-start(f32[1,64,512]{2,1,0:T(8,128)S(1)} %copy-done), channel_id=1, source_target_pairs={{0,7},{8,15},{16,17},{24,25},{1,0},{9,8},{17,18},{25,26},{2,1},{10... | collective-permute-start | bytes 393224 | tf_op jit(solution)/shard_map/ppermute | solution.py:501
  72.6 0.9 collective-permute-done.8.high_now
  73.5 13.6 %density_step.1 = (f32[2,16,64,512]{3,2,1,0:T(8,128)}, f32[3,64,512]{2,1,0:T(8,128)S(1)}) custom-call(f32[2,16,64,512]{3,2,1,0:T(8,128)} %density.3, f32[2,16,64,512]{3,2,1,0:T(8,128)} %get-tuple-element.22.control, f32[2,2,64,512]{3,2,1,0:T(8,128)S(1)} %collective-permute-done.3.low, f32[2,2,64,512]{3,2,1,0:T(8,128)S(1)} %collective-permute-done.4.high, ...), custom_call_target="tpu_custom_call" | custom-call | tf_op jit(solution)/shard_map/density_step/pallas_call | solution.py:346
  87.1 2.6 %collective-permute-done.9.refs_0_ = f32[6,64,512]{2,1,0:T(8,128)S(1)} collective-permute-done((f32[6,64,512]{2,1,0:T(8,128)}, f32[6,64,512]{2,1,0:T(8,128)S(1)}, u32[]{:S(2)}, u32[]{:S(2)}) %collective-permute-start.9) | collective-permute-done | bytes 786464 | tf_op jit(solution)/shard_map/ppermute | solution.py:501
  89.7 0.5 collective-permute-done.10.refs_1_
  90.2 4.0 %arrive.1.partial = f32[2,16,64,512]{3,2,1,0:T(8,128)} custom-call(f32[2,16,64,512]{3,2,1,0:T(8,128)} %get-tuple-element.42.partial, f32[6,64,512]{2,1,0:T(8,128)S(1)} %collective-permute-done.9.refs_0_, f32[7,64,512]{2,1,0:T(8,128)S(1)} %collective-permute-done.10.refs_1_), custom_call_target="tpu_custom_call", output_to_operand_aliasing={{}: (0, {})} | custom-call | tf_op jit(solution)/shard_map/arrive/pallas_call | solution.py:396
  94.2 1.1 %collective-permute-done.11.halo = f32[2,64,512]{2,1,0:T(8,128)S(1)} collective-permute-done((f32[2,64,512]{2,1,0:T(8,128)S(1)}, f32[2,64,512]{2,1,0:T(8,128)S(1)}, u32[]{:S(2)}, u32[]{:S(2)}) %collective-permute-start.11) | collective-permute-done | bytes 262176 | tf_op jit(solution)/shard_map/ppermute | solution.py:500
  95.3 0.7 arrive_rest.2.partial
  96.1 2.1 %collective-permute-done.12.halo = f32[1,64,512]{2,1,0:T(8,128)S(1)} collective-permute-done((f32[1,64,512]{2,1,0:T(8,128)S(1)}, f32[1,64,512]{2,1,0:T(8,128)S(1)}, u32[]{:S(2)}, u32[]{:S(2)}) %collective-permute-start.12) | collective-permute-done | bytes 131104 | tf_op jit(solution)/shard_map/ppermute | solution.py:501
  98.1 0.7 arrive_rest.3
  (8 shorter events, 0.1 us)
Async XLA Ops:
  1.5 9.7 %collective-permute-start = (f32[2,32,512]{2,1,0:T(8,128)S(1)}, f32[2,32,512]{2,1,0:T(8,128)S(1)}, u32[]{:S(2)}, u32[]{:S(2)}) collective-permute-start(f32[2,32,512]{2,1,0:T(8,128)S(1)} %value_rows.3), channel_id=1, source_target_pairs={{0,1},{8,9},{16,23},{24,31},{1,2},{9,10},{17,16},{25,24},{2,3},{10... | collective-permute-start | bytes 393224 | tf_op jit(solution)/shard_map/ppermute | solution.py:487
  5.9 47.4 %collective-permute-start.1 = (f32[17,32,512]{2,1,0:T(8,128)S(1)}, f32[17,32,512]{2,1,0:T(8,128)S(1)}, u32[]{:S(2)}, u32[]{:S(2)}) collective-permute-start(f32[17,32,512]{2,1,0:T(8,128)S(1)} %value_rows.4), channel_id=1, source_target_pairs={{0,1},{8,9},{16,23},{24,31},{1,2},{9,10},{17,16},{25,24},{2,3},{10... | collective-permute-start | bytes 3342344 | tf_op jit(solution)/shard_map/ppermute | solution.py:487
  14.7 30.4 %collective-permute-start.5 = (f32[7,64,512]{2,1,0:T(8,128)}, f32[7,64,512]{2,1,0:T(8,128)}, u32[]{:S(2)}, u32[]{:S(2)}) collective-permute-start(f32[7,64,512]{2,1,0:T(8,128)} %get-tuple-element.31), channel_id=1, source_target_pairs={{0,6},{8,14},{16,16},{24,24},{1,1},{9,9},{17,19},{25,27},{2,0},{10... | collective-permute-start | bytes 2752520 | tf_op jit(solution)/shard_map/ppermute | solution.py:491
  20.4 32.9 %collective-permute-start.2 = (f32[13,32,512]{2,1,0:T(8,128)}, f32[13,32,512]{2,1,0:T(8,128)S(1)}, u32[]{:S(2)}, u32[]{:S(2)}) collective-permute-start(f32[13,32,512]{2,1,0:T(8,128)} %value_rows.5), channel_id=1, source_target_pairs={{0,1},{8,9},{16,23},{24,31},{1,2},{9,10},{17,16},{25,24},{2,3},{10... | collective-permute-start | bytes 2555912 | tf_op jit(solution)/shard_map/ppermute | solution.py:487
  23.8 20.0 %collective-permute-start.6 = (f32[2,64,512]{2,1,0:T(8,128)}, f32[2,64,512]{2,1,0:T(8,128)S(1)}, u32[]{:S(2)}, u32[]{:S(2)}) collective-permute-start(f32[2,64,512]{2,1,0:T(8,128)} %get-tuple-element.32), channel_id=1, source_target_pairs={{0,6},{8,14},{16,16},{24,24},{1,1},{9,9},{17,19},{25,27},{2,0},{10... | collective-permute-start | bytes 786440 | tf_op jit(solution)/shard_map/ppermute | solution.py:491
  38.9 32.6 %copy-start = (f32[1,64,512]{2,1,0:T(8,128)S(1)}, f32[1,64,512]{2,1,0:T(8,128)}, u32[]{:S(2)}) copy-start(f32[1,64,512]{2,1,0:T(8,128)} %get-tuple-element.45) | copy-start | bytes 393220
  38.9 6.3 %collective-permute-start.3 = (f32[2,2,64,512]{3,2,1,0:T(8,128)}, f32[2,2,64,512]{3,2,1,0:T(8,128)S(1)}, u32[]{:S(2)}, u32[]{:S(2)}) collective-permute-start(f32[2,2,64,512]{3,2,1,0:T(8,128)} %get-tuple-element.29), channel_id=1, source_target_pairs={{0,8},{8,16},{16,24},{1,9},{9,17},{17,25},{2,10},{10,18},{18,26},{... | collective-permute-start | bytes 1572872 | tf_op jit(solution)/shard_map/ppermute | solution.py:495
  43.8 4.0 %collective-permute-start.4 = (f32[2,2,64,512]{3,2,1,0:T(8,128)}, f32[2,2,64,512]{3,2,1,0:T(8,128)S(1)}, u32[]{:S(2)}, u32[]{:S(2)}) collective-permute-start(f32[2,2,64,512]{3,2,1,0:T(8,128)} %get-tuple-element.30), channel_id=1, source_target_pairs={{8,0},{16,8},{24,16},{9,1},{17,9},{25,17},{10,2},{18,10},{26,18},{... | collective-permute-start | bytes 1572872 | tf_op jit(solution)/shard_map/ppermute | solution.py:496
  45.1 45.1 %collective-permute-start.10 = (f32[7,64,512]{2,1,0:T(8,128)}, f32[7,64,512]{2,1,0:T(8,128)S(1)}, u32[]{:S(2)}, u32[]{:S(2)}) collective-permute-start(f32[7,64,512]{2,1,0:T(8,128)} %collective-permute-done.5), channel_id=1, source_target_pairs={{0,1},{8,9},{16,17},{24,25},{1,0},{9,8},{17,16},{25,24},{2,3},{10,... | collective-permute-start | bytes 2752520 | tf_op jit(solution)/shard_map/ppermute | solution.py:500
  53.3 36.4 %collective-permute-start.9 = (f32[6,64,512]{2,1,0:T(8,128)}, f32[6,64,512]{2,1,0:T(8,128)S(1)}, u32[]{:S(2)}, u32[]{:S(2)}) collective-permute-start(f32[6,64,512]{2,1,0:T(8,128)} %get-tuple-element.43), channel_id=1, source_target_pairs={{0,7},{8,15},{16,17},{24,25},{1,0},{9,8},{17,18},{25,26},{2,1},{10... | collective-permute-start | bytes 2359304 | tf_op jit(solution)/shard_map/ppermute | solution.py:501
  66.3 5.1 %collective-permute-start.7 = (f32[2,64,512]{2,1,0:T(8,128)S(1)}, f32[2,64,512]{2,1,0:T(8,128)S(1)}, u32[]{:S(2)}, u32[]{:S(2)}) collective-permute-start(f32[2,64,512]{2,1,0:T(8,128)S(1)} %get-tuple-element.40), channel_id=1, source_target_pairs={{0,8},{8,16},{16,24},{1,9},{9,17},{17,25},{2,10},{10,18},{18,26},{... | collective-permute-start | bytes 786440 | tf_op jit(solution)/shard_map/ppermute | solution.py:504
  70.1 3.4 %collective-permute-start.8 = (f32[2,64,512]{2,1,0:T(8,128)S(1)}, f32[2,64,512]{2,1,0:T(8,128)S(1)}, u32[]{:S(2)}, u32[]{:S(2)}) collective-permute-start(f32[2,64,512]{2,1,0:T(8,128)S(1)} %get-tuple-element.41), channel_id=1, source_target_pairs={{8,0},{16,8},{24,16},{9,1},{17,9},{25,17},{10,2},{18,10},{26,18},{... | collective-permute-start | bytes 786440 | tf_op jit(solution)/shard_map/ppermute | solution.py:505
  71.4 23.9 %collective-permute-start.11 = (f32[2,64,512]{2,1,0:T(8,128)S(1)}, f32[2,64,512]{2,1,0:T(8,128)S(1)}, u32[]{:S(2)}, u32[]{:S(2)}) collective-permute-start(f32[2,64,512]{2,1,0:T(8,128)S(1)} %collective-permute-done.6), channel_id=1, source_target_pairs={{0,1},{8,9},{16,17},{24,25},{1,0},{9,8},{17,16},{25,24},{2,3},{10,... | collective-permute-start | bytes 786440 | tf_op jit(solution)/shard_map/ppermute | solution.py:500
  71.5 26.6 %collective-permute-start.12 = (f32[1,64,512]{2,1,0:T(8,128)S(1)}, f32[1,64,512]{2,1,0:T(8,128)S(1)}, u32[]{:S(2)}, u32[]{:S(2)}) collective-permute-start(f32[1,64,512]{2,1,0:T(8,128)S(1)} %copy-done), channel_id=1, source_target_pairs={{0,7},{8,15},{16,17},{24,25},{1,0},{9,8},{17,18},{25,26},{2,1},{10... | collective-permute-start | bytes 393224 | tf_op jit(solution)/shard_map/ppermute | solution.py:501

commit v8 on v7

--- a/solution.py
+++ b/solution.py
@@ -14,7 +14,7 @@
 
 SUB = 8
 LANES = 128
-EARLY = 1
+EARLY = 3
 SHIFT = 1
 VMEM_LIMIT = 18 * 1024 * 1024
 ANY = pl.BlockSpec(memory_space=pl.ANY)
@@ -482,7 +482,7 @@
     onward = [(v, v + 1) for v in range(groups - 1)]
     back = [(v + 1, v) for v in range(groups - 1)]
 
-    bounds = (0, 2 * EARLY, rows + 2 * EARLY + SHIFT, 2 * rows)
+    bounds = (0, EARLY, rows + EARLY + SHIFT, 2 * rows)
     value_halos = [
         lax.ppermute(value_rows(value_next, begin, end), names, value_route)
         for begin, end in zip(bounds, bounds[1:])

time: 99.8 us -> 99.9 us (level)
  starting transfers between devices: 30.1 us -> 27.4 us
  waiting for transfers between devices: 22.3 us -> 25 us
    ppermute x2, starting transfers between devices: 10.2 us -> 6.3 us  [body(): fillers = [lax.ppermute(part, names, over_route) for part in parts[1::2]]]
    ppermute x2, waiting for transfers between devices: 3.28 us -> 6.74 us  [body(): fillers = [lax.ppermute(part, names, over_route) for part in parts[1::2]]]
    ppermute x1, starting transfers between devices: 3.75 us -> 5.16 us  [body(): low_now = lax.ppermute(low_now, 'vel', onward)]
    ppermute x2, waiting for transfers between devices: 4.65 us -> 3.24 us  [body(): parts = [lax.ppermute(part, names, density_route) for part in parts]]
where the time goes in v8:
time: 99.9 us; the launch traced here: 98.8 us
  Pallas kernels  37.2 us (37%)
  starting transfers between devices  27.4 us (27%)
  waiting for transfers between devices  25 us (25%)
  blocking collectives  5.96 us (6%)
  other arithmetic  2.46 us (2%)
    pallas_call x1, Pallas kernels, density_step(): pl.pallas_call(density_kernel, out_shape=[jax.ShapeDtypeStruct(density.sh...  13.6 us
    pallas_call x1, Pallas kernels, value_step(): pl.pallas_call(value_kernel, out_shape=[jax.ShapeDtypeStruct(value.shape,...  10.2 us
    ppermute x3, waiting for transfers between devices, body(): lax.ppermute(value_rows(value_next, begin, end), names, value_route)  9.86 us
    ppermute x3, starting transfers between devices, body(): lax.ppermute(value_rows(value_next, begin, end), names, value_route)  7.24 us
    ppermute x2, waiting for transfers between devices, body(): fillers = [lax.ppermute(part, names, over_route) for part in parts[1::2]]  6.74 us
    ppermute x2, starting transfers between devices, body(): fillers = [lax.ppermute(part, names, over_route) for part in parts[1::2]]  6.3 us
    psum x1, blocking collectives, body(): mass = lax.psum(jnp.sum(density, axis=(1, 2)), 'vel') / (second * second)  5.96 us
    ppermute x1, starting transfers between devices, body(): low_now = lax.ppermute(low_now, 'vel', onward)  5.16 us
  transfers between devices with their start and end apart: 13, of which 9 were waited for; matrix products, arithmetic and copies ran while one was open for 2% of the time, Pallas kernels for 36%

profile of v8, /device:TPU:0, one launch (start us, length us, event | category | flops | bytes accessed | tf_op | source)
XLA Modules:
  0.0 98.8 jit_solution(4842129381797066033)
XLA Ops:
  0.6 0.9 value_rows.3
  1.6 3.0 %collective-permute-start = (f32[3,32,512]{2,1,0:T(8,128)S(1)}, f32[3,32,512]{2,1,0:T(8,128)S(1)}, u32[]{:S(2)}, u32[]{:S(2)}) collective-permute-start(f32[3,32,512]{2,1,0:T(8,128)S(1)} %value_rows.3), channel_id=1, source_target_pairs={{0,1},{8,9},{16,23},{24,31},{1,2},{9,10},{17,16},{25,24},{2,3},{10... | collective-permute-start | bytes 589832 | tf_op jit(solution)/shard_map/ppermute | solution.py:487
  4.6 1.4 %value_rows.4 = f32[17,32,512]{2,1,0:T(8,128)S(1)} custom-call(f32[2,16,64,512]{3,2,1,0:T(8,128)} %value.9), custom_call_target="tpu_custom_call" | custom-call | tf_op jit(solution)/shard_map/value_rows/pallas_call | solution.py:95
  6.0 1.6 %collective-permute-start.1 = (f32[17,32,512]{2,1,0:T(8,128)S(1)}, f32[17,32,512]{2,1,0:T(8,128)S(1)}, u32[]{:S(2)}, u32[]{:S(2)}) collective-permute-start(f32[17,32,512]{2,1,0:T(8,128)S(1)} %value_rows.4), channel_id=1, source_target_pairs={{0,1},{8,9},{16,23},{24,31},{1,2},{9,10},{17,16},{25,24},{2,3},{10... | collective-permute-start | bytes 3342344 | tf_op jit(solution)/shard_map/ppermute | solution.py:487
  7.6 5.8 %collective-permute-done.after.rest_0_ = f32[3,32,512]{2,1,0:T(8,128)S(1)} collective-permute-done((f32[3,32,512]{2,1,0:T(8,128)S(1)}, f32[3,32,512]{2,1,0:T(8,128)S(1)}, u32[]{:S(2)}, u32[]{:S(2)}) %collective-permute-start) | collective-permute-done | bytes 196640 | tf_op jit(solution)/shard_map/ppermute | solution.py:487
  13.3 3.5 %edges.1 = (f32[2,2,64,512]{3,2,1,0:T(8,128)}, f32[2,2,64,512]{3,2,1,0:T(8,128)}, f32[6,64,512]{2,1,0:T(8,128)}, f32[7,64,512]{2,1,0:T(8,128)}, f32[1,64,512]{2,1,0:T(8,128)}, /*index=5*/f32[2,64,512]{2,1,0:T(8,128)}) custom-call(f32[2,16,64,512]{3,2,1,0:T(8,128)} %value.9, f32[2,16,64,512]{3,2,1,0:T(8,128)} %density.3, ...), custom_call_target="tpu_custom_call" | custom-call | tf_op jit(solution)/shard_map/edges/pallas_call | solution.py:124
  16.8 3.9 %collective-permute-start.5 = (f32[7,64,512]{2,1,0:T(8,128)}, f32[7,64,512]{2,1,0:T(8,128)}, u32[]{:S(2)}, u32[]{:S(2)}) collective-permute-start(f32[7,64,512]{2,1,0:T(8,128)} %get-tuple-element.31), channel_id=1, source_target_pairs={{0,6},{8,14},{16,16},{24,24},{1,1},{9,9},{17,19},{25,27},{2,0},{10... | collective-permute-start | bytes 2752520 | tf_op jit(solution)/shard_map/ppermute | solution.py:491
  20.8 2.4 %collective-permute-start.6 = (f32[2,64,512]{2,1,0:T(8,128)}, f32[2,64,512]{2,1,0:T(8,128)S(1)}, u32[]{:S(2)}, u32[]{:S(2)}) collective-permute-start(f32[2,64,512]{2,1,0:T(8,128)} %get-tuple-element.32), channel_id=1, source_target_pairs={{0,6},{8,14},{16,16},{24,24},{1,1},{9,9},{17,19},{25,27},{2,0},{10... | collective-permute-start | bytes 786440 | tf_op jit(solution)/shard_map/ppermute | solution.py:491
  23.1 2.1 %value_rows.5 = f32[12,32,512]{2,1,0:T(8,128)} custom-call(f32[2,16,64,512]{3,2,1,0:T(8,128)} %value.9), custom_call_target="tpu_custom_call" | custom-call | tf_op jit(solution)/shard_map/value_rows/pallas_call | solution.py:95
  25.3 2.6 %collective-permute-start.2 = (f32[12,32,512]{2,1,0:T(8,128)}, f32[12,32,512]{2,1,0:T(8,128)S(1)}, u32[]{:S(2)}, u32[]{:S(2)}) collective-permute-start(f32[12,32,512]{2,1,0:T(8,128)} %value_rows.5), channel_id=1, source_target_pairs={{0,1},{8,9},{16,23},{24,31},{1,2},{9,10},{17,16},{25,24},{2,3},{10... | collective-permute-start | bytes 2359304 | tf_op jit(solution)/shard_map/ppermute | solution.py:487
  27.9 2.5 %reduce_sum.9 = f32[2,512]{1,0:T(2,128)S(1)} reduce(f32[2,16,64,512]{3,2,1,0:T(8,128)} %density.3, f32[]{:T(128)} %constant.2.clone.1), dimensions={1,2}, to_apply=%region_0.0 | reduce | flops 1047552 | bytes 4198404 | tf_op jit(solution)/shard_map/reduce_sum | solution.py:492
  30.4 6.0 %psum.7 = f32[2,512]{1,0:T(2,128)S(1)} all-reduce(f32[2,512]{1,0:T(2,128)S(1)} %reduce_sum.9), channel_id=1, replica_groups=mesh['vel'=4,'pos'=8] {'vel'}, use_global_device_ids=true, to_apply=%region_1.0 | all-reduce | flops 1024 | bytes 8192 | tf_op jit(solution)/shard_map/psum | solution.py:492
  36.4 2.1 %collective-permute-start.3 = (f32[2,2,64,512]{3,2,1,0:T(8,128)}, f32[2,2,64,512]{3,2,1,0:T(8,128)S(1)}, u32[]{:S(2)}, u32[]{:S(2)}) collective-permute-start(f32[2,2,64,512]{3,2,1,0:T(8,128)} %get-tuple-element.29), channel_id=1, source_target_pairs={{0,8},{8,16},{16,24},{1,9},{9,17},{17,25},{2,10},{10,18},{18,26},{... | collective-permute-start | bytes 1572872 | tf_op jit(solution)/shard_map/ppermute | solution.py:495
  38.5 6.7 %collective-permute-done.6 = f32[2,64,512]{2,1,0:T(8,128)S(1)} collective-permute-done((f32[2,64,512]{2,1,0:T(8,128)}, f32[2,64,512]{2,1,0:T(8,128)S(1)}, u32[]{:S(2)}, u32[]{:S(2)}) %collective-permute-start.6) | collective-permute-done | bytes 262176 | tf_op jit(solution)/shard_map/ppermute | solution.py:491
  45.2 1.3 %collective-permute-start.4 = (f32[2,2,64,512]{3,2,1,0:T(8,128)}, f32[2,2,64,512]{3,2,1,0:T(8,128)S(1)}, u32[]{:S(2)}, u32[]{:S(2)}) collective-permute-start(f32[2,2,64,512]{3,2,1,0:T(8,128)} %get-tuple-element.30), channel_id=1, source_target_pairs={{8,0},{16,8},{24,16},{9,1},{17,9},{25,17},{10,2},{18,10},{26,18},{... | collective-permute-start | bytes 1572872 | tf_op jit(solution)/shard_map/ppermute | solution.py:496
  46.6 2.6 %collective-permute-done.4.high = f32[2,2,64,512]{3,2,1,0:T(8,128)S(1)} collective-permute-done((f32[2,2,64,512]{3,2,1,0:T(8,128)}, f32[2,2,64,512]{3,2,1,0:T(8,128)S(1)}, u32[]{:S(2)}, u32[]{:S(2)}) %collective-permute-start.4) | collective-permute-done | bytes 524320 | tf_op jit(solution)/shard_map/ppermute | solution.py:496
  49.2 4.1 %collective-permute-done.2.rest_2_ = f32[12,32,512]{2,1,0:T(8,128)S(1)} collective-permute-done((f32[12,32,512]{2,1,0:T(8,128)}, f32[12,32,512]{2,1,0:T(8,128)S(1)}, u32[]{:S(2)}, u32[]{:S(2)}) %collective-permute-start.2) | collective-permute-done | bytes 786464 | tf_op jit(solution)/shard_map/ppermute | solution.py:487
  53.3 2.8 %collective-permute-start.9 = (f32[6,64,512]{2,1,0:T(8,128)}, f32[6,64,512]{2,1,0:T(8,128)S(1)}, u32[]{:S(2)}, u32[]{:S(2)}) collective-permute-start(f32[6,64,512]{2,1,0:T(8,128)} %get-tuple-element.43), channel_id=1, source_target_pairs={{0,7},{8,15},{16,17},{24,25},{1,0},{9,8},{17,18},{25,26},{2,1},{10... | collective-permute-start | bytes 2359304 | tf_op jit(solution)/shard_map/ppermute | solution.py:501
  56.1 10.2 %value_step.1 = (f32[2,16,64,512]{3,2,1,0:T(8,128)}, f32[2,64,512]{2,1,0:T(8,128)S(1)}, f32[2,64,512]{2,1,0:T(8,128)S(1)}) custom-call(f32[2,16,64,512]{3,2,1,0:T(8,128)} %value.9, f32[2,2,64,512]{3,2,1,0:T(8,128)S(1)} %collective-permute-done.3.low, f32[2,2,64,512]{3,2,1,0:T(8,128)S(1)} %collective-permute-done.4.high, ...), custom_call_target="tpu_custom_call" | custom-call | tf_op jit(solution)/shard_map/value_step/pallas_call | solution.py:245
  66.4 5.2 %collective-permute-start.7 = (f32[2,64,512]{2,1,0:T(8,128)S(1)}, f32[2,64,512]{2,1,0:T(8,128)S(1)}, u32[]{:S(2)}, u32[]{:S(2)}) collective-permute-start(f32[2,64,512]{2,1,0:T(8,128)S(1)} %get-tuple-element.40), channel_id=1, source_target_pairs={{0,8},{8,16},{16,24},{1,9},{9,17},{17,25},{2,10},{10,18},{18,26},{... | collective-permute-start | bytes 786440 | tf_op jit(solution)/shard_map/ppermute | solution.py:504
  71.5 1.3 %collective-permute-start.8 = (f32[2,64,512]{2,1,0:T(8,128)S(1)}, f32[2,64,512]{2,1,0:T(8,128)S(1)}, u32[]{:S(2)}, u32[]{:S(2)}) collective-permute-start(f32[2,64,512]{2,1,0:T(8,128)S(1)} %get-tuple-element.41), channel_id=1, source_target_pairs={{8,0},{16,8},{24,16},{9,1},{17,9},{25,17},{10,2},{18,10},{26,18},{... | collective-permute-start | bytes 786440 | tf_op jit(solution)/shard_map/ppermute | solution.py:505
  72.8 0.1 collective-permute-start.11
  72.9 1.1 %collective-permute-start.12 = (f32[1,64,512]{2,1,0:T(8,128)S(1)}, f32[1,64,512]{2,1,0:T(8,128)S(1)}, u32[]{:S(2)}, u32[]{:S(2)}) collective-permute-start(f32[1,64,512]{2,1,0:T(8,128)S(1)} %copy-done), channel_id=1, source_target_pairs={{0,7},{8,15},{16,17},{24,25},{1,0},{9,8},{17,18},{25,26},{2,1},{10... | collective-permute-start | bytes 393224 | tf_op jit(solution)/shard_map/ppermute | solution.py:501
  74.0 0.9 collective-permute-done.8.high_now
  75.0 13.6 %density_step.1 = (f32[2,16,64,512]{3,2,1,0:T(8,128)}, f32[3,64,512]{2,1,0:T(8,128)S(1)}) custom-call(f32[2,16,64,512]{3,2,1,0:T(8,128)} %density.3, f32[2,16,64,512]{3,2,1,0:T(8,128)} %get-tuple-element.22.control, f32[2,2,64,512]{3,2,1,0:T(8,128)S(1)} %collective-permute-done.3.low, f32[2,2,64,512]{3,2,1,0:T(8,128)S(1)} %collective-permute-done.4.high, ...), custom_call_target="tpu_custom_call" | custom-call | tf_op jit(solution)/shard_map/density_step/pallas_call | solution.py:346
  88.6 1.2 %collective-permute-done.9.refs_0_ = f32[6,64,512]{2,1,0:T(8,128)S(1)} collective-permute-done((f32[6,64,512]{2,1,0:T(8,128)}, f32[6,64,512]{2,1,0:T(8,128)S(1)}, u32[]{:S(2)}, u32[]{:S(2)}) %collective-permute-start.9) | collective-permute-done | bytes 786464 | tf_op jit(solution)/shard_map/ppermute | solution.py:501
  89.7 0.2 collective-permute-done.10.refs_1_
  89.9 4.0 %arrive.1.partial = f32[2,16,64,512]{3,2,1,0:T(8,128)} custom-call(f32[2,16,64,512]{3,2,1,0:T(8,128)} %get-tuple-element.42.partial, f32[6,64,512]{2,1,0:T(8,128)S(1)} %collective-permute-done.9.refs_0_, f32[7,64,512]{2,1,0:T(8,128)S(1)} %collective-permute-done.10.refs_1_), custom_call_target="tpu_custom_call", output_to_operand_aliasing={{}: (0, {})} | custom-call | tf_op jit(solution)/shard_map/arrive/pallas_call | solution.py:396
  93.9 1.4 %collective-permute-done.11.halo = f32[2,64,512]{2,1,0:T(8,128)S(1)} collective-permute-done((f32[2,64,512]{2,1,0:T(8,128)S(1)}, f32[2,64,512]{2,1,0:T(8,128)S(1)}, u32[]{:S(2)}, u32[]{:S(2)}) %collective-permute-start.11) | collective-permute-done | bytes 262176 | tf_op jit(solution)/shard_map/ppermute | solution.py:500
  95.4 0.7 arrive_rest.2.partial
  96.1 2.1 %collective-permute-done.12.halo = f32[1,64,512]{2,1,0:T(8,128)S(1)} collective-permute-done((f32[1,64,512]{2,1,0:T(8,128)S(1)}, f32[1,64,512]{2,1,0:T(8,128)S(1)}, u32[]{:S(2)}, u32[]{:S(2)}) %collective-permute-start.12) | collective-permute-done | bytes 131104 | tf_op jit(solution)/shard_map/ppermute | solution.py:501
  98.2 0.7 arrive_rest.3
  (8 shorter events, 0.1 us)
Async XLA Ops:
  1.6 11.8 %collective-permute-start = (f32[3,32,512]{2,1,0:T(8,128)S(1)}, f32[3,32,512]{2,1,0:T(8,128)S(1)}, u32[]{:S(2)}, u32[]{:S(2)}) collective-permute-start(f32[3,32,512]{2,1,0:T(8,128)S(1)} %value_rows.3), channel_id=1, source_target_pairs={{0,1},{8,9},{16,23},{24,31},{1,2},{9,10},{17,16},{25,24},{2,3},{10... | collective-permute-start | bytes 589832 | tf_op jit(solution)/shard_map/ppermute | solution.py:487
  6.0 47.4 %collective-permute-start.1 = (f32[17,32,512]{2,1,0:T(8,128)S(1)}, f32[17,32,512]{2,1,0:T(8,128)S(1)}, u32[]{:S(2)}, u32[]{:S(2)}) collective-permute-start(f32[17,32,512]{2,1,0:T(8,128)S(1)} %value_rows.4), channel_id=1, source_target_pairs={{0,1},{8,9},{16,23},{24,31},{1,2},{9,10},{17,16},{25,24},{2,3},{10... | collective-permute-start | bytes 3342344 | tf_op jit(solution)/shard_map/ppermute | solution.py:487
  16.8 29.7 %collective-permute-start.5 = (f32[7,64,512]{2,1,0:T(8,128)}, f32[7,64,512]{2,1,0:T(8,128)}, u32[]{:S(2)}, u32[]{:S(2)}) collective-permute-start(f32[7,64,512]{2,1,0:T(8,128)} %get-tuple-element.31), channel_id=1, source_target_pairs={{0,6},{8,14},{16,16},{24,24},{1,1},{9,9},{17,19},{25,27},{2,0},{10... | collective-permute-start | bytes 2752520 | tf_op jit(solution)/shard_map/ppermute | solution.py:491
  20.8 24.5 %collective-permute-start.6 = (f32[2,64,512]{2,1,0:T(8,128)}, f32[2,64,512]{2,1,0:T(8,128)S(1)}, u32[]{:S(2)}, u32[]{:S(2)}) collective-permute-start(f32[2,64,512]{2,1,0:T(8,128)} %get-tuple-element.32), channel_id=1, source_target_pairs={{0,6},{8,14},{16,16},{24,24},{1,1},{9,9},{17,19},{25,27},{2,0},{10... | collective-permute-start | bytes 786440 | tf_op jit(solution)/shard_map/ppermute | solution.py:491
  25.3 28.1 %collective-permute-start.2 = (f32[12,32,512]{2,1,0:T(8,128)}, f32[12,32,512]{2,1,0:T(8,128)S(1)}, u32[]{:S(2)}, u32[]{:S(2)}) collective-permute-start(f32[12,32,512]{2,1,0:T(8,128)} %value_rows.5), channel_id=1, source_target_pairs={{0,1},{8,9},{16,23},{24,31},{1,2},{9,10},{17,16},{25,24},{2,3},{10... | collective-permute-start | bytes 2359304 | tf_op jit(solution)/shard_map/ppermute | solution.py:487
  36.3 36.6 %copy-start = (f32[1,64,512]{2,1,0:T(8,128)S(1)}, f32[1,64,512]{2,1,0:T(8,128)}, u32[]{:S(2)}) copy-start(f32[1,64,512]{2,1,0:T(8,128)} %get-tuple-element.45) | copy-start | bytes 393220
  36.4 10.3 %collective-permute-start.3 = (f32[2,2,64,512]{3,2,1,0:T(8,128)}, f32[2,2,64,512]{3,2,1,0:T(8,128)S(1)}, u32[]{:S(2)}, u32[]{:S(2)}) collective-permute-start(f32[2,2,64,512]{3,2,1,0:T(8,128)} %get-tuple-element.29), channel_id=1, source_target_pairs={{0,8},{8,16},{16,24},{1,9},{9,17},{17,25},{2,10},{10,18},{18,26},{... | collective-permute-start | bytes 1572872 | tf_op jit(solution)/shard_map/ppermute | solution.py:495
  45.2 4.0 %collective-permute-start.4 = (f32[2,2,64,512]{3,2,1,0:T(8,128)}, f32[2,2,64,512]{3,2,1,0:T(8,128)S(1)}, u32[]{:S(2)}, u32[]{:S(2)}) collective-permute-start(f32[2,2,64,512]{3,2,1,0:T(8,128)} %get-tuple-element.30), channel_id=1, source_target_pairs={{8,0},{16,8},{24,16},{9,1},{17,9},{25,17},{10,2},{18,10},{26,18},{... | collective-permute-start | bytes 1572872 | tf_op jit(solution)/shard_map/ppermute | solution.py:496
  46.5 43.4 %collective-permute-start.10 = (f32[7,64,512]{2,1,0:T(8,128)}, f32[7,64,512]{2,1,0:T(8,128)S(1)}, u32[]{:S(2)}, u32[]{:S(2)}) collective-permute-start(f32[7,64,512]{2,1,0:T(8,128)} %collective-permute-done.5), channel_id=1, source_target_pairs={{0,1},{8,9},{16,17},{24,25},{1,0},{9,8},{17,16},{25,24},{2,3},{10,... | collective-permute-start | bytes 2752520 | tf_op jit(solution)/shard_map/ppermute | solution.py:500
  53.3 36.4 %collective-permute-start.9 = (f32[6,64,512]{2,1,0:T(8,128)}, f32[6,64,512]{2,1,0:T(8,128)S(1)}, u32[]{:S(2)}, u32[]{:S(2)}) collective-permute-start(f32[6,64,512]{2,1,0:T(8,128)} %get-tuple-element.43), channel_id=1, source_target_pairs={{0,7},{8,15},{16,17},{24,25},{1,0},{9,8},{17,18},{25,26},{2,1},{10... | collective-permute-start | bytes 2359304 | tf_op jit(solution)/shard_map/ppermute | solution.py:501
  66.4 6.5 %collective-permute-start.7 = (f32[2,64,512]{2,1,0:T(8,128)S(1)}, f32[2,64,512]{2,1,0:T(8,128)S(1)}, u32[]{:S(2)}, u32[]{:S(2)}) collective-permute-start(f32[2,64,512]{2,1,0:T(8,128)S(1)} %get-tuple-element.40), channel_id=1, source_target_pairs={{0,8},{8,16},{16,24},{1,9},{9,17},{17,25},{2,10},{10,18},{18,26},{... | collective-permute-start | bytes 786440 | tf_op jit(solution)/shard_map/ppermute | solution.py:504
  71.5 3.4 %collective-permute-start.8 = (f32[2,64,512]{2,1,0:T(8,128)S(1)}, f32[2,64,512]{2,1,0:T(8,128)S(1)}, u32[]{:S(2)}, u32[]{:S(2)}) collective-permute-start(f32[2,64,512]{2,1,0:T(8,128)S(1)} %get-tuple-element.41), channel_id=1, source_target_pairs={{8,0},{16,8},{24,16},{9,1},{17,9},{25,17},{10,2},{18,10},{26,18},{... | collective-permute-start | bytes 786440 | tf_op jit(solution)/shard_map/ppermute | solution.py:505
  72.8 22.5 %collective-permute-start.11 = (f32[2,64,512]{2,1,0:T(8,128)S(1)}, f32[2,64,512]{2,1,0:T(8,128)S(1)}, u32[]{:S(2)}, u32[]{:S(2)}) collective-permute-start(f32[2,64,512]{2,1,0:T(8,128)S(1)} %collective-permute-done.6), channel_id=1, source_target_pairs={{0,1},{8,9},{16,17},{24,25},{1,0},{9,8},{17,16},{25,24},{2,3},{10,... | collective-permute-start | bytes 786440 | tf_op jit(solution)/shard_map/ppermute | solution.py:500
  72.9 25.2 %collective-permute-start.12 = (f32[1,64,512]{2,1,0:T(8,128)S(1)}, f32[1,64,512]{2,1,0:T(8,128)S(1)}, u32[]{:S(2)}, u32[]{:S(2)}) collective-permute-start(f32[1,64,512]{2,1,0:T(8,128)S(1)} %copy-done), channel_id=1, source_target_pairs={{0,7},{8,15},{16,17},{24,25},{1,0},{9,8},{17,18},{25,26},{2,1},{10... | collective-permute-start | bytes 393224 | tf_op jit(solution)/shard_map/ppermute | solution.py:501

commit v9 on v7

--- a/solution.py
+++ b/solution.py
@@ -16,7 +16,7 @@
 LANES = 128
 EARLY = 1
 SHIFT = 1
-VMEM_LIMIT = 18 * 1024 * 1024
+VMEM_LIMIT = 15 * 1024 * 1024
 ANY = pl.BlockSpec(memory_space=pl.ANY)
 VMEM = pl.BlockSpec(memory_space=pltpu.VMEM)
 LIGHT = pl.CostEstimate(flops=0, transcendentals=0, bytes_accessed=0)

time: 99.8 us -> 99.8 us (level)
  no operation moved by 1% of the time
where the time goes in v9:
time: 99.8 us; the launch traced here: 98.8 us
  Pallas kernels  37.2 us (37%)
  starting transfers between devices  30.1 us (30%)
  waiting for transfers between devices  22.3 us (22%)
  blocking collectives  5.96 us (6%)
  other arithmetic  2.46 us (2%)
    pallas_call x1, Pallas kernels, density_step(): pl.pallas_call(density_kernel, out_shape=[jax.ShapeDtypeStruct(density.sh...  13.6 us
    pallas_call x1, Pallas kernels, value_step(): pl.pallas_call(value_kernel, out_shape=[jax.ShapeDtypeStruct(value.shape,...  10.2 us
    ppermute x2, starting transfers between devices, body(): fillers = [lax.ppermute(part, names, over_route) for part in parts[1::2]]  10.2 us
    ppermute x3, waiting for transfers between devices, body(): lax.ppermute(value_rows(value_next, begin, end), names, value_route)  9.19 us
    ppermute x3, starting transfers between devices, body(): lax.ppermute(value_rows(value_next, begin, end), names, value_route)  7.95 us
    psum x1, blocking collectives, body(): mass = lax.psum(jnp.sum(density, axis=(1, 2)), 'vel') / (second * second)  5.96 us
    ppermute x2, waiting for transfers between devices, body(): parts = [lax.ppermute(part, names, density_route) for part in parts]  4.65 us
    pallas_call x3, Pallas kernels, value_rows(): pl.pallas_call(functools.partial(value_rows_kernel, begin), out_shape=[pl...  4.5 us
  transfers between devices with their start and end apart: 13, of which 9 were waited for; matrix products, arithmetic and copies ran while one was open for 2% of the time, Pallas kernels for 36%

profile of v9, /device:TPU:0, one launch (start us, length us, event | category | flops | bytes accessed | tf_op | source)
XLA Modules:
  0.0 98.8 jit_solution(14790888463986194206)
XLA Ops:
  0.6 0.9 value_rows.3
  1.5 3.0 %collective-permute-start = (f32[2,32,512]{2,1,0:T(8,128)S(1)}, f32[2,32,512]{2,1,0:T(8,128)S(1)}, u32[]{:S(2)}, u32[]{:S(2)}) collective-permute-start(f32[2,32,512]{2,1,0:T(8,128)S(1)} %value_rows.3), channel_id=1, source_target_pairs={{0,1},{8,9},{16,23},{24,31},{1,2},{9,10},{17,16},{25,24},{2,3},{10... | collective-permute-start | bytes 393224 | tf_op jit(solution)/shard_map/ppermute | solution.py:487
  4.5 1.4 %value_rows.4 = f32[17,32,512]{2,1,0:T(8,128)S(1)} custom-call(f32[2,16,64,512]{3,2,1,0:T(8,128)} %value.9), custom_call_target="tpu_custom_call" | custom-call | tf_op jit(solution)/shard_map/value_rows/pallas_call | solution.py:95
  5.9 1.6 %collective-permute-start.1 = (f32[17,32,512]{2,1,0:T(8,128)S(1)}, f32[17,32,512]{2,1,0:T(8,128)S(1)}, u32[]{:S(2)}, u32[]{:S(2)}) collective-permute-start(f32[17,32,512]{2,1,0:T(8,128)S(1)} %value_rows.4), channel_id=1, source_target_pairs={{0,1},{8,9},{16,23},{24,31},{1,2},{9,10},{17,16},{25,24},{2,3},{10... | collective-permute-start | bytes 3342344 | tf_op jit(solution)/shard_map/ppermute | solution.py:487
  7.5 3.7 %collective-permute-done.after.rest_0_ = f32[2,32,512]{2,1,0:T(8,128)S(1)} collective-permute-done((f32[2,32,512]{2,1,0:T(8,128)S(1)}, f32[2,32,512]{2,1,0:T(8,128)S(1)}, u32[]{:S(2)}, u32[]{:S(2)}) %collective-permute-start) | collective-permute-done | bytes 131104 | tf_op jit(solution)/shard_map/ppermute | solution.py:487
  11.2 3.5 %edges.1 = (f32[2,2,64,512]{3,2,1,0:T(8,128)}, f32[2,2,64,512]{3,2,1,0:T(8,128)}, f32[6,64,512]{2,1,0:T(8,128)}, f32[7,64,512]{2,1,0:T(8,128)}, f32[1,64,512]{2,1,0:T(8,128)}, /*index=5*/f32[2,64,512]{2,1,0:T(8,128)}) custom-call(f32[2,16,64,512]{3,2,1,0:T(8,128)} %value.9, f32[2,16,64,512]{3,2,1,0:T(8,128)} %density.3, ...), custom_call_target="tpu_custom_call" | custom-call | tf_op jit(solution)/shard_map/edges/pallas_call | solution.py:124
  14.7 3.5 %collective-permute-start.5 = (f32[7,64,512]{2,1,0:T(8,128)}, f32[7,64,512]{2,1,0:T(8,128)}, u32[]{:S(2)}, u32[]{:S(2)}) collective-permute-start(f32[7,64,512]{2,1,0:T(8,128)} %get-tuple-element.31), channel_id=1, source_target_pairs={{0,6},{8,14},{16,16},{24,24},{1,1},{9,9},{17,19},{25,27},{2,0},{10... | collective-permute-start | bytes 2752520 | tf_op jit(solution)/shard_map/ppermute | solution.py:491
  18.2 2.2 %value_rows.5 = f32[13,32,512]{2,1,0:T(8,128)} custom-call(f32[2,16,64,512]{3,2,1,0:T(8,128)} %value.9), custom_call_target="tpu_custom_call" | custom-call | tf_op jit(solution)/shard_map/value_rows/pallas_call | solution.py:95
  20.4 3.4 %collective-permute-start.2 = (f32[13,32,512]{2,1,0:T(8,128)}, f32[13,32,512]{2,1,0:T(8,128)S(1)}, u32[]{:S(2)}, u32[]{:S(2)}) collective-permute-start(f32[13,32,512]{2,1,0:T(8,128)} %value_rows.5), channel_id=1, source_target_pairs={{0,1},{8,9},{16,23},{24,31},{1,2},{9,10},{17,16},{25,24},{2,3},{10... | collective-permute-start | bytes 2555912 | tf_op jit(solution)/shard_map/ppermute | solution.py:487
  23.8 6.6 %collective-permute-start.6 = (f32[2,64,512]{2,1,0:T(8,128)}, f32[2,64,512]{2,1,0:T(8,128)S(1)}, u32[]{:S(2)}, u32[]{:S(2)}) collective-permute-start(f32[2,64,512]{2,1,0:T(8,128)} %get-tuple-element.32), channel_id=1, source_target_pairs={{0,6},{8,14},{16,16},{24,24},{1,1},{9,9},{17,19},{25,27},{2,0},{10... | collective-permute-start | bytes 786440 | tf_op jit(solution)/shard_map/ppermute | solution.py:491
  30.4 2.5 %reduce_sum.9 = f32[2,512]{1,0:T(2,128)S(1)} reduce(f32[2,16,64,512]{3,2,1,0:T(8,128)} %density.3, f32[]{:T(128)} %constant.2.clone.1), dimensions={1,2}, to_apply=%region_0.0 | reduce | flops 1047552 | bytes 4198404 | tf_op jit(solution)/shard_map/reduce_sum | solution.py:492
  32.9 6.0 %psum.7 = f32[2,512]{1,0:T(2,128)S(1)} all-reduce(f32[2,512]{1,0:T(2,128)S(1)} %reduce_sum.9), channel_id=1, replica_groups=mesh['vel'=4,'pos'=8] {'vel'}, use_global_device_ids=true, to_apply=%region_1.0 | all-reduce | flops 1024 | bytes 8192 | tf_op jit(solution)/shard_map/psum | solution.py:492
  38.9 1.6 %collective-permute-start.3 = (f32[2,2,64,512]{3,2,1,0:T(8,128)}, f32[2,2,64,512]{3,2,1,0:T(8,128)S(1)}, u32[]{:S(2)}, u32[]{:S(2)}) collective-permute-start(f32[2,2,64,512]{3,2,1,0:T(8,128)} %get-tuple-element.29), channel_id=1, source_target_pairs={{0,8},{8,16},{16,24},{1,9},{9,17},{17,25},{2,10},{10,18},{18,26},{... | collective-permute-start | bytes 1572872 | tf_op jit(solution)/shard_map/ppermute | solution.py:495
  40.5 3.3 %collective-permute-done.6 = f32[2,64,512]{2,1,0:T(8,128)S(1)} collective-permute-done((f32[2,64,512]{2,1,0:T(8,128)}, f32[2,64,512]{2,1,0:T(8,128)S(1)}, u32[]{:S(2)}, u32[]{:S(2)}) %collective-permute-start.6) | collective-permute-done | bytes 262176 | tf_op jit(solution)/shard_map/ppermute | solution.py:491
  43.8 1.3 %collective-permute-start.4 = (f32[2,2,64,512]{3,2,1,0:T(8,128)}, f32[2,2,64,512]{3,2,1,0:T(8,128)S(1)}, u32[]{:S(2)}, u32[]{:S(2)}) collective-permute-start(f32[2,2,64,512]{3,2,1,0:T(8,128)} %get-tuple-element.30), channel_id=1, source_target_pairs={{8,0},{16,8},{24,16},{9,1},{17,9},{25,17},{10,2},{18,10},{26,18},{... | collective-permute-start | bytes 1572872 | tf_op jit(solution)/shard_map/ppermute | solution.py:496
  45.2 2.6 %collective-permute-done.4.high = f32[2,2,64,512]{3,2,1,0:T(8,128)S(1)} collective-permute-done((f32[2,2,64,512]{3,2,1,0:T(8,128)}, f32[2,2,64,512]{3,2,1,0:T(8,128)S(1)}, u32[]{:S(2)}, u32[]{:S(2)}) %collective-permute-start.4) | collective-permute-done | bytes 524320 | tf_op jit(solution)/shard_map/ppermute | solution.py:496
  47.8 5.5 %collective-permute-done.2.rest_2_ = f32[13,32,512]{2,1,0:T(8,128)S(1)} collective-permute-done((f32[13,32,512]{2,1,0:T(8,128)}, f32[13,32,512]{2,1,0:T(8,128)S(1)}, u32[]{:S(2)}, u32[]{:S(2)}) %collective-permute-start.2) | collective-permute-done | bytes 852000 | tf_op jit(solution)/shard_map/ppermute | solution.py:487
  53.3 2.8 %collective-permute-start.9 = (f32[6,64,512]{2,1,0:T(8,128)}, f32[6,64,512]{2,1,0:T(8,128)S(1)}, u32[]{:S(2)}, u32[]{:S(2)}) collective-permute-start(f32[6,64,512]{2,1,0:T(8,128)} %get-tuple-element.43), channel_id=1, source_target_pairs={{0,7},{8,15},{16,17},{24,25},{1,0},{9,8},{17,18},{25,26},{2,1},{10... | collective-permute-start | bytes 2359304 | tf_op jit(solution)/shard_map/ppermute | solution.py:501
  56.1 10.2 %value_step.1 = (f32[2,16,64,512]{3,2,1,0:T(8,128)}, f32[2,64,512]{2,1,0:T(8,128)S(1)}, f32[2,64,512]{2,1,0:T(8,128)S(1)}) custom-call(f32[2,16,64,512]{3,2,1,0:T(8,128)} %value.9, f32[2,2,64,512]{3,2,1,0:T(8,128)S(1)} %collective-permute-done.3.low, f32[2,2,64,512]{3,2,1,0:T(8,128)S(1)} %collective-permute-done.4.high, ...), custom_call_target="tpu_custom_call" | custom-call | tf_op jit(solution)/shard_map/value_step/pallas_call | solution.py:245
  66.3 3.8 %collective-permute-start.7 = (f32[2,64,512]{2,1,0:T(8,128)S(1)}, f32[2,64,512]{2,1,0:T(8,128)S(1)}, u32[]{:S(2)}, u32[]{:S(2)}) collective-permute-start(f32[2,64,512]{2,1,0:T(8,128)S(1)} %get-tuple-element.40), channel_id=1, source_target_pairs={{0,8},{8,16},{16,24},{1,9},{9,17},{17,25},{2,10},{10,18},{18,26},{... | collective-permute-start | bytes 786440 | tf_op jit(solution)/shard_map/ppermute | solution.py:504
  70.1 1.3 %collective-permute-start.8 = (f32[2,64,512]{2,1,0:T(8,128)S(1)}, f32[2,64,512]{2,1,0:T(8,128)S(1)}, u32[]{:S(2)}, u32[]{:S(2)}) collective-permute-start(f32[2,64,512]{2,1,0:T(8,128)S(1)} %get-tuple-element.41), channel_id=1, source_target_pairs={{8,0},{16,8},{24,16},{9,1},{17,9},{25,17},{10,2},{18,10},{26,18},{... | collective-permute-start | bytes 786440 | tf_op jit(solution)/shard_map/ppermute | solution.py:505
  71.4 0.1 collective-permute-start.11
  71.5 1.1 %collective-permute-start.12 = (f32[1,64,512]{2,1,0:T(8,128)S(1)}, f32[1,64,512]{2,1,0:T(8,128)S(1)}, u32[]{:S(2)}, u32[]{:S(2)}) collective-permute-start(f32[1,64,512]{2,1,0:T(8,128)S(1)} %copy-done), channel_id=1, source_target_pairs={{0,7},{8,15},{16,17},{24,25},{1,0},{9,8},{17,18},{25,26},{2,1},{10... | collective-permute-start | bytes 393224 | tf_op jit(solution)/shard_map/ppermute | solution.py:501
  72.6 0.9 collective-permute-done.8.high_now
  73.5 13.6 %density_step.1 = (f32[2,16,64,512]{3,2,1,0:T(8,128)}, f32[3,64,512]{2,1,0:T(8,128)S(1)}) custom-call(f32[2,16,64,512]{3,2,1,0:T(8,128)} %density.3, f32[2,16,64,512]{3,2,1,0:T(8,128)} %get-tuple-element.22.control, f32[2,2,64,512]{3,2,1,0:T(8,128)S(1)} %collective-permute-done.3.low, f32[2,2,64,512]{3,2,1,0:T(8,128)S(1)} %collective-permute-done.4.high, ...), custom_call_target="tpu_custom_call" | custom-call | tf_op jit(solution)/shard_map/density_step/pallas_call | solution.py:346
  87.1 2.6 %collective-permute-done.9.refs_0_ = f32[6,64,512]{2,1,0:T(8,128)S(1)} collective-permute-done((f32[6,64,512]{2,1,0:T(8,128)}, f32[6,64,512]{2,1,0:T(8,128)S(1)}, u32[]{:S(2)}, u32[]{:S(2)}) %collective-permute-start.9) | collective-permute-done | bytes 786464 | tf_op jit(solution)/shard_map/ppermute | solution.py:501
  89.7 0.5 collective-permute-done.10.refs_1_
  90.2 4.0 %arrive.1.partial = f32[2,16,64,512]{3,2,1,0:T(8,128)} custom-call(f32[2,16,64,512]{3,2,1,0:T(8,128)} %get-tuple-element.42.partial, f32[6,64,512]{2,1,0:T(8,128)S(1)} %collective-permute-done.9.refs_0_, f32[7,64,512]{2,1,0:T(8,128)S(1)} %collective-permute-done.10.refs_1_), custom_call_target="tpu_custom_call", output_to_operand_aliasing={{}: (0, {})} | custom-call | tf_op jit(solution)/shard_map/arrive/pallas_call | solution.py:396
  94.2 1.1 %collective-permute-done.11.halo = f32[2,64,512]{2,1,0:T(8,128)S(1)} collective-permute-done((f32[2,64,512]{2,1,0:T(8,128)S(1)}, f32[2,64,512]{2,1,0:T(8,128)S(1)}, u32[]{:S(2)}, u32[]{:S(2)}) %collective-permute-start.11) | collective-permute-done | bytes 262176 | tf_op jit(solution)/shard_map/ppermute | solution.py:500
  95.3 0.7 arrive_rest.2.partial
  96.1 2.1 %collective-permute-done.12.halo = f32[1,64,512]{2,1,0:T(8,128)S(1)} collective-permute-done((f32[1,64,512]{2,1,0:T(8,128)S(1)}, f32[1,64,512]{2,1,0:T(8,128)S(1)}, u32[]{:S(2)}, u32[]{:S(2)}) %collective-permute-start.12) | collective-permute-done | bytes 131104 | tf_op jit(solution)/shard_map/ppermute | solution.py:501
  98.1 0.7 arrive_rest.3
  (8 shorter events, 0.1 us)
Async XLA Ops:
  1.5 9.7 %collective-permute-start = (f32[2,32,512]{2,1,0:T(8,128)S(1)}, f32[2,32,512]{2,1,0:T(8,128)S(1)}, u32[]{:S(2)}, u32[]{:S(2)}) collective-permute-start(f32[2,32,512]{2,1,0:T(8,128)S(1)} %value_rows.3), channel_id=1, source_target_pairs={{0,1},{8,9},{16,23},{24,31},{1,2},{9,10},{17,16},{25,24},{2,3},{10... | collective-permute-start | bytes 393224 | tf_op jit(solution)/shard_map/ppermute | solution.py:487
  5.9 47.4 %collective-permute-start.1 = (f32[17,32,512]{2,1,0:T(8,128)S(1)}, f32[17,32,512]{2,1,0:T(8,128)S(1)}, u32[]{:S(2)}, u32[]{:S(2)}) collective-permute-start(f32[17,32,512]{2,1,0:T(8,128)S(1)} %value_rows.4), channel_id=1, source_target_pairs={{0,1},{8,9},{16,23},{24,31},{1,2},{9,10},{17,16},{25,24},{2,3},{10... | collective-permute-start | bytes 3342344 | tf_op jit(solution)/shard_map/ppermute | solution.py:487
  14.7 30.4 %collective-permute-start.5 = (f32[7,64,512]{2,1,0:T(8,128)}, f32[7,64,512]{2,1,0:T(8,128)}, u32[]{:S(2)}, u32[]{:S(2)}) collective-permute-start(f32[7,64,512]{2,1,0:T(8,128)} %get-tuple-element.31), channel_id=1, source_target_pairs={{0,6},{8,14},{16,16},{24,24},{1,1},{9,9},{17,19},{25,27},{2,0},{10... | collective-permute-start | bytes 2752520 | tf_op jit(solution)/shard_map/ppermute | solution.py:491
  20.4 32.9 %collective-permute-start.2 = (f32[13,32,512]{2,1,0:T(8,128)}, f32[13,32,512]{2,1,0:T(8,128)S(1)}, u32[]{:S(2)}, u32[]{:S(2)}) collective-permute-start(f32[13,32,512]{2,1,0:T(8,128)} %value_rows.5), channel_id=1, source_target_pairs={{0,1},{8,9},{16,23},{24,31},{1,2},{9,10},{17,16},{25,24},{2,3},{10... | collective-permute-start | bytes 2555912 | tf_op jit(solution)/shard_map/ppermute | solution.py:487
  23.8 20.0 %collective-permute-start.6 = (f32[2,64,512]{2,1,0:T(8,128)}, f32[2,64,512]{2,1,0:T(8,128)S(1)}, u32[]{:S(2)}, u32[]{:S(2)}) collective-permute-start(f32[2,64,512]{2,1,0:T(8,128)} %get-tuple-element.32), channel_id=1, source_target_pairs={{0,6},{8,14},{16,16},{24,24},{1,1},{9,9},{17,19},{25,27},{2,0},{10... | collective-permute-start | bytes 786440 | tf_op jit(solution)/shard_map/ppermute | solution.py:491
  38.9 32.6 %copy-start = (f32[1,64,512]{2,1,0:T(8,128)S(1)}, f32[1,64,512]{2,1,0:T(8,128)}, u32[]{:S(2)}) copy-start(f32[1,64,512]{2,1,0:T(8,128)} %get-tuple-element.45) | copy-start | bytes 393220
  38.9 6.3 %collective-permute-start.3 = (f32[2,2,64,512]{3,2,1,0:T(8,128)}, f32[2,2,64,512]{3,2,1,0:T(8,128)S(1)}, u32[]{:S(2)}, u32[]{:S(2)}) collective-permute-start(f32[2,2,64,512]{3,2,1,0:T(8,128)} %get-tuple-element.29), channel_id=1, source_target_pairs={{0,8},{8,16},{16,24},{1,9},{9,17},{17,25},{2,10},{10,18},{18,26},{... | collective-permute-start | bytes 1572872 | tf_op jit(solution)/shard_map/ppermute | solution.py:495
  43.8 4.0 %collective-permute-start.4 = (f32[2,2,64,512]{3,2,1,0:T(8,128)}, f32[2,2,64,512]{3,2,1,0:T(8,128)S(1)}, u32[]{:S(2)}, u32[]{:S(2)}) collective-permute-start(f32[2,2,64,512]{3,2,1,0:T(8,128)} %get-tuple-element.30), channel_id=1, source_target_pairs={{8,0},{16,8},{24,16},{9,1},{17,9},{25,17},{10,2},{18,10},{26,18},{... | collective-permute-start | bytes 1572872 | tf_op jit(solution)/shard_map/ppermute | solution.py:496
  45.1 45.1 %collective-permute-start.10 = (f32[7,64,512]{2,1,0:T(8,128)}, f32[7,64,512]{2,1,0:T(8,128)S(1)}, u32[]{:S(2)}, u32[]{:S(2)}) collective-permute-start(f32[7,64,512]{2,1,0:T(8,128)} %collective-permute-done.5), channel_id=1, source_target_pairs={{0,1},{8,9},{16,17},{24,25},{1,0},{9,8},{17,16},{25,24},{2,3},{10,... | collective-permute-start | bytes 2752520 | tf_op jit(solution)/shard_map/ppermute | solution.py:500
  53.3 36.4 %collective-permute-start.9 = (f32[6,64,512]{2,1,0:T(8,128)}, f32[6,64,512]{2,1,0:T(8,128)S(1)}, u32[]{:S(2)}, u32[]{:S(2)}) collective-permute-start(f32[6,64,512]{2,1,0:T(8,128)} %get-tuple-element.43), channel_id=1, source_target_pairs={{0,7},{8,15},{16,17},{24,25},{1,0},{9,8},{17,18},{25,26},{2,1},{10... | collective-permute-start | bytes 2359304 | tf_op jit(solution)/shard_map/ppermute | solution.py:501
  66.3 5.1 %collective-permute-start.7 = (f32[2,64,512]{2,1,0:T(8,128)S(1)}, f32[2,64,512]{2,1,0:T(8,128)S(1)}, u32[]{:S(2)}, u32[]{:S(2)}) collective-permute-start(f32[2,64,512]{2,1,0:T(8,128)S(1)} %get-tuple-element.40), channel_id=1, source_target_pairs={{0,8},{8,16},{16,24},{1,9},{9,17},{17,25},{2,10},{10,18},{18,26},{... | collective-permute-start | bytes 786440 | tf_op jit(solution)/shard_map/ppermute | solution.py:504
  70.1 3.4 %collective-permute-start.8 = (f32[2,64,512]{2,1,0:T(8,128)S(1)}, f32[2,64,512]{2,1,0:T(8,128)S(1)}, u32[]{:S(2)}, u32[]{:S(2)}) collective-permute-start(f32[2,64,512]{2,1,0:T(8,128)S(1)} %get-tuple-element.41), channel_id=1, source_target_pairs={{8,0},{16,8},{24,16},{9,1},{17,9},{25,17},{10,2},{18,10},{26,18},{... | collective-permute-start | bytes 786440 | tf_op jit(solution)/shard_map/ppermute | solution.py:505
  71.4 23.9 %collective-permute-start.11 = (f32[2,64,512]{2,1,0:T(8,128)S(1)}, f32[2,64,512]{2,1,0:T(8,128)S(1)}, u32[]{:S(2)}, u32[]{:S(2)}) collective-permute-start(f32[2,64,512]{2,1,0:T(8,128)S(1)} %collective-permute-done.6), channel_id=1, source_target_pairs={{0,1},{8,9},{16,17},{24,25},{1,0},{9,8},{17,16},{25,24},{2,3},{10,... | collective-permute-start | bytes 786440 | tf_op jit(solution)/shard_map/ppermute | solution.py:500
  71.5 26.6 %collective-permute-start.12 = (f32[1,64,512]{2,1,0:T(8,128)S(1)}, f32[1,64,512]{2,1,0:T(8,128)S(1)}, u32[]{:S(2)}, u32[]{:S(2)}) collective-permute-start(f32[1,64,512]{2,1,0:T(8,128)S(1)} %copy-done), channel_id=1, source_target_pairs={{0,7},{8,15},{16,17},{24,25},{1,0},{9,8},{17,18},{25,26},{2,1},{10... | collective-permute-start | bytes 393224 | tf_op jit(solution)/shard_map/ppermute | solution.py:501

commit v10 on v7

--- a/solution.py
+++ b/solution.py
@@ -365,18 +365,18 @@
     )(in_hbm(density), in_hbm(control), low, high, low_now, high_now)
 
 
-def arrive_kernel(partial, *refs):
+def arrive_kernel(begin, partial, *refs):
     halos, (out, held, near, load, store) = refs[:-5], refs[-5:]
     count, rows = partial.shape[:2]
     row = jnp.where(is_negative(), count - 1, 0)
-    base = lax.axis_index("vel") * rows
+    base = lax.axis_index("vel") * rows + begin
     total = rows * lax.axis_size("vel")
     loads = []
     for halo in halos:
         for k in range(halo.shape[0]):
             a = len(loads)
             pair = [
-                pltpu.make_async_copy(partial.at[row, a], held.at[a], load.at[2 * a]),
+                pltpu.make_async_copy(partial.at[row, begin + a], held.at[a], load.at[2 * a]),
                 pltpu.make_async_copy(halo.at[k], near.at[a], load.at[2 * a + 1]),
             ]
             start_all(pair)
@@ -385,16 +385,16 @@
     for a, pair in enumerate(loads):
         wait_all(pair)
         held[a] = held[a] + slant(base + a, total) * near[a]
-        stores.append(pltpu.make_async_copy(held.at[a], out.at[row, a], store.at[a]))
+        stores.append(pltpu.make_async_copy(held.at[a], out.at[row, begin + a], store.at[a]))
         stores[-1].start()
     wait_all(stores)
 
 
-def arrive(partial, halos):
+def arrive(partial, halos, begin):
     extent = sum(halo.shape[0] for halo in halos)
     block = pltpu.VMEM((extent,) + partial.shape[2:], partial.dtype)
     return pl.pallas_call(
-        arrive_kernel,
+        functools.partial(arrive_kernel, begin),
         out_shape=jax.ShapeDtypeStruct(partial.shape, partial.dtype),
         in_specs=[ANY] * (1 + len(halos)),
         out_specs=ANY,
@@ -506,7 +506,8 @@
     density_next, rest = density_step(
         density, value_now, low, high, low_now, high_now, last + filler
     )
-    density_next = arrive(density_next, (parts[0], fillers[0]))
+    density_next = arrive(density_next, (parts[0],), cuts[0][0])
+    density_next = arrive(density_next, (fillers[0],), cuts[1][0])
     density_next = arrive_rest(density_next, rest, fillers[1], cuts[3][0])
     density_next = arrive_rest(density_next, rest, parts[1], cuts[2][0])
     return value_now, density_next

time: 99.8 us -> 99.9 us (level)
  Pallas kernels: 37.2 us -> 38.7 us
  waiting for transfers between devices: 22.3 us -> 20.8 us
    ppermute x2, waiting for transfers between devices: 1.63 us -> 0.1 us  [body(): fillers = [lax.ppermute(part, names, swap_route) for part in fillers]]
    pallas_call x1 -> x2, Pallas kernels: 3.98 us -> 5.49 us  [arrive(): pl.pallas_call(functools.partial(arrive_kernel, begin), out_shape=jax.Sha...]
  transfers between devices with their start and end apart: 13 -> 13, of which waited for: 9 -> 8; matrix products, arithmetic and copies ran while one was open for 2% -> 2% of each run, Pallas kernels for 36% -> 38%
where the time goes in v10:
time: 99.9 us; the launch traced here: 98.8 us
  Pallas kernels  38.7 us (39%)
  starting transfers between devices  30.1 us (30%)
  waiting for transfers between devices  20.8 us (21%)
  blocking collectives  5.96 us (6%)
  other arithmetic  2.46 us (2%)
    pallas_call x1, Pallas kernels, density_step(): pl.pallas_call(density_kernel, out_shape=[jax.ShapeDtypeStruct(density.sh...  13.6 us
    pallas_call x1, Pallas kernels, value_step(): pl.pallas_call(value_kernel, out_shape=[jax.ShapeDtypeStruct(value.shape,...  10.2 us
    ppermute x2, starting transfers between devices, body(): fillers = [lax.ppermute(part, names, over_route) for part in parts[1::2]]  10.2 us
    ppermute x3, waiting for transfers between devices, body(): lax.ppermute(value_rows(value_next, begin, end), names, value_route)  9.19 us
    ppermute x3, starting transfers between devices, body(): lax.ppermute(value_rows(value_next, begin, end), names, value_route)  7.95 us
    psum x1, blocking collectives, body(): mass = lax.psum(jnp.sum(density, axis=(1, 2)), 'vel') / (second * second)  5.96 us
    pallas_call x2, Pallas kernels, arrive(): pl.pallas_call(functools.partial(arrive_kernel, begin), out_shape=jax.Sha...  5.49 us
    ppermute x2, waiting for transfers between devices, body(): parts = [lax.ppermute(part, names, density_route) for part in parts]  4.65 us
  transfers between devices with their start and end apart: 13, of which 8 were waited for; matrix products, arithmetic and copies ran while one was open for 2% of the time, Pallas kernels for 38%

profile of v10, /device:TPU:0, one launch (start us, length us, event | category | flops | bytes accessed | tf_op | source)
XLA Modules:
  0.0 98.8 jit_solution(12843914831774226700)
XLA Ops:
  0.6 0.9 value_rows.3
  1.5 3.0 %collective-permute-start = (f32[2,32,512]{2,1,0:T(8,128)S(1)}, f32[2,32,512]{2,1,0:T(8,128)S(1)}, u32[]{:S(2)}, u32[]{:S(2)}) collective-permute-start(f32[2,32,512]{2,1,0:T(8,128)S(1)} %value_rows.3), channel_id=1, source_target_pairs={{0,1},{8,9},{16,23},{24,31},{1,2},{9,10},{17,16},{25,24},{2,3},{10... | collective-permute-start | bytes 393224 | tf_op jit(solution)/shard_map/ppermute | solution.py:487
  4.5 1.4 %value_rows.4 = f32[17,32,512]{2,1,0:T(8,128)S(1)} custom-call(f32[2,16,64,512]{3,2,1,0:T(8,128)} %value.9), custom_call_target="tpu_custom_call" | custom-call | tf_op jit(solution)/shard_map/value_rows/pallas_call | solution.py:95
  5.9 1.6 %collective-permute-start.1 = (f32[17,32,512]{2,1,0:T(8,128)S(1)}, f32[17,32,512]{2,1,0:T(8,128)S(1)}, u32[]{:S(2)}, u32[]{:S(2)}) collective-permute-start(f32[17,32,512]{2,1,0:T(8,128)S(1)} %value_rows.4), channel_id=1, source_target_pairs={{0,1},{8,9},{16,23},{24,31},{1,2},{9,10},{17,16},{25,24},{2,3},{10... | collective-permute-start | bytes 3342344 | tf_op jit(solution)/shard_map/ppermute | solution.py:487
  7.5 3.7 %collective-permute-done.after.rest_0_ = f32[2,32,512]{2,1,0:T(8,128)S(1)} collective-permute-done((f32[2,32,512]{2,1,0:T(8,128)S(1)}, f32[2,32,512]{2,1,0:T(8,128)S(1)}, u32[]{:S(2)}, u32[]{:S(2)}) %collective-permute-start) | collective-permute-done | bytes 131104 | tf_op jit(solution)/shard_map/ppermute | solution.py:487
  11.2 3.5 %edges.1 = (f32[2,2,64,512]{3,2,1,0:T(8,128)}, f32[2,2,64,512]{3,2,1,0:T(8,128)}, f32[6,64,512]{2,1,0:T(8,128)}, f32[7,64,512]{2,1,0:T(8,128)}, f32[1,64,512]{2,1,0:T(8,128)}, /*index=5*/f32[2,64,512]{2,1,0:T(8,128)}) custom-call(f32[2,16,64,512]{3,2,1,0:T(8,128)} %value.9, f32[2,16,64,512]{3,2,1,0:T(8,128)} %density.3, ...), custom_call_target="tpu_custom_call" | custom-call | tf_op jit(solution)/shard_map/edges/pallas_call | solution.py:124
  14.7 3.5 %collective-permute-start.5 = (f32[7,64,512]{2,1,0:T(8,128)}, f32[7,64,512]{2,1,0:T(8,128)}, u32[]{:S(2)}, u32[]{:S(2)}) collective-permute-start(f32[7,64,512]{2,1,0:T(8,128)} %get-tuple-element.31), channel_id=1, source_target_pairs={{0,6},{8,14},{16,16},{24,24},{1,1},{9,9},{17,19},{25,27},{2,0},{10... | collective-permute-start | bytes 2752520 | tf_op jit(solution)/shard_map/ppermute | solution.py:491
  18.2 2.2 %value_rows.5 = f32[13,32,512]{2,1,0:T(8,128)} custom-call(f32[2,16,64,512]{3,2,1,0:T(8,128)} %value.9), custom_call_target="tpu_custom_call" | custom-call | tf_op jit(solution)/shard_map/value_rows/pallas_call | solution.py:95
  20.4 3.4 %collective-permute-start.2 = (f32[13,32,512]{2,1,0:T(8,128)}, f32[13,32,512]{2,1,0:T(8,128)S(1)}, u32[]{:S(2)}, u32[]{:S(2)}) collective-permute-start(f32[13,32,512]{2,1,0:T(8,128)} %value_rows.5), channel_id=1, source_target_pairs={{0,1},{8,9},{16,23},{24,31},{1,2},{9,10},{17,16},{25,24},{2,3},{10... | collective-permute-start | bytes 2555912 | tf_op jit(solution)/shard_map/ppermute | solution.py:487
  23.8 6.6 %collective-permute-start.6 = (f32[2,64,512]{2,1,0:T(8,128)}, f32[2,64,512]{2,1,0:T(8,128)S(1)}, u32[]{:S(2)}, u32[]{:S(2)}) collective-permute-start(f32[2,64,512]{2,1,0:T(8,128)} %get-tuple-element.32), channel_id=1, source_target_pairs={{0,6},{8,14},{16,16},{24,24},{1,1},{9,9},{17,19},{25,27},{2,0},{10... | collective-permute-start | bytes 786440 | tf_op jit(solution)/shard_map/ppermute | solution.py:491
  30.4 2.5 %reduce_sum.9 = f32[2,512]{1,0:T(2,128)S(1)} reduce(f32[2,16,64,512]{3,2,1,0:T(8,128)} %density.3, f32[]{:T(128)} %constant.2.clone.1), dimensions={1,2}, to_apply=%region_0.0 | reduce | flops 1047552 | bytes 4198404 | tf_op jit(solution)/shard_map/reduce_sum | solution.py:492
  32.9 6.0 %psum.7 = f32[2,512]{1,0:T(2,128)S(1)} all-reduce(f32[2,512]{1,0:T(2,128)S(1)} %reduce_sum.9), channel_id=1, replica_groups=mesh['vel'=4,'pos'=8] {'vel'}, use_global_device_ids=true, to_apply=%region_1.0 | all-reduce | flops 1024 | bytes 8192 | tf_op jit(solution)/shard_map/psum | solution.py:492
  38.9 1.6 %collective-permute-start.3 = (f32[2,2,64,512]{3,2,1,0:T(8,128)}, f32[2,2,64,512]{3,2,1,0:T(8,128)S(1)}, u32[]{:S(2)}, u32[]{:S(2)}) collective-permute-start(f32[2,2,64,512]{3,2,1,0:T(8,128)} %get-tuple-element.29), channel_id=1, source_target_pairs={{0,8},{8,16},{16,24},{1,9},{9,17},{17,25},{2,10},{10,18},{18,26},{... | collective-permute-start | bytes 1572872 | tf_op jit(solution)/shard_map/ppermute | solution.py:495
  40.5 3.3 %collective-permute-done.6 = f32[2,64,512]{2,1,0:T(8,128)S(1)} collective-permute-done((f32[2,64,512]{2,1,0:T(8,128)}, f32[2,64,512]{2,1,0:T(8,128)S(1)}, u32[]{:S(2)}, u32[]{:S(2)}) %collective-permute-start.6) | collective-permute-done | bytes 262176 | tf_op jit(solution)/shard_map/ppermute | solution.py:491
  43.8 1.3 %collective-permute-start.4 = (f32[2,2,64,512]{3,2,1,0:T(8,128)}, f32[2,2,64,512]{3,2,1,0:T(8,128)S(1)}, u32[]{:S(2)}, u32[]{:S(2)}) collective-permute-start(f32[2,2,64,512]{3,2,1,0:T(8,128)} %get-tuple-element.30), channel_id=1, source_target_pairs={{8,0},{16,8},{24,16},{9,1},{17,9},{25,17},{10,2},{18,10},{26,18},{... | collective-permute-start | bytes 1572872 | tf_op jit(solution)/shard_map/ppermute | solution.py:496
  45.2 2.6 %collective-permute-done.4.high = f32[2,2,64,512]{3,2,1,0:T(8,128)S(1)} collective-permute-done((f32[2,2,64,512]{3,2,1,0:T(8,128)}, f32[2,2,64,512]{3,2,1,0:T(8,128)S(1)}, u32[]{:S(2)}, u32[]{:S(2)}) %collective-permute-start.4) | collective-permute-done | bytes 524320 | tf_op jit(solution)/shard_map/ppermute | solution.py:496
  47.8 5.5 %collective-permute-done.2.rest_2_ = f32[13,32,512]{2,1,0:T(8,128)S(1)} collective-permute-done((f32[13,32,512]{2,1,0:T(8,128)}, f32[13,32,512]{2,1,0:T(8,128)S(1)}, u32[]{:S(2)}, u32[]{:S(2)}) %collective-permute-start.2) | collective-permute-done | bytes 852000 | tf_op jit(solution)/shard_map/ppermute | solution.py:487
  53.3 2.8 %collective-permute-start.9 = (f32[6,64,512]{2,1,0:T(8,128)}, f32[6,64,512]{2,1,0:T(8,128)S(1)}, u32[]{:S(2)}, u32[]{:S(2)}) collective-permute-start(f32[6,64,512]{2,1,0:T(8,128)} %get-tuple-element.43), channel_id=1, source_target_pairs={{0,7},{8,15},{16,17},{24,25},{1,0},{9,8},{17,18},{25,26},{2,1},{10... | collective-permute-start | bytes 2359304 | tf_op jit(solution)/shard_map/ppermute | solution.py:501
  56.1 10.2 %value_step.1 = (f32[2,16,64,512]{3,2,1,0:T(8,128)}, f32[2,64,512]{2,1,0:T(8,128)S(1)}, f32[2,64,512]{2,1,0:T(8,128)S(1)}) custom-call(f32[2,16,64,512]{3,2,1,0:T(8,128)} %value.9, f32[2,2,64,512]{3,2,1,0:T(8,128)S(1)} %collective-permute-done.3.low, f32[2,2,64,512]{3,2,1,0:T(8,128)S(1)} %collective-permute-done.4.high, ...), custom_call_target="tpu_custom_call" | custom-call | tf_op jit(solution)/shard_map/value_step/pallas_call | solution.py:245
  66.3 3.8 %collective-permute-start.7 = (f32[2,64,512]{2,1,0:T(8,128)S(1)}, f32[2,64,512]{2,1,0:T(8,128)S(1)}, u32[]{:S(2)}, u32[]{:S(2)}) collective-permute-start(f32[2,64,512]{2,1,0:T(8,128)S(1)} %get-tuple-element.40), channel_id=1, source_target_pairs={{0,8},{8,16},{16,24},{1,9},{9,17},{17,25},{2,10},{10,18},{18,26},{... | collective-permute-start | bytes 786440 | tf_op jit(solution)/shard_map/ppermute | solution.py:504
  70.1 1.3 %collective-permute-start.8 = (f32[2,64,512]{2,1,0:T(8,128)S(1)}, f32[2,64,512]{2,1,0:T(8,128)S(1)}, u32[]{:S(2)}, u32[]{:S(2)}) collective-permute-start(f32[2,64,512]{2,1,0:T(8,128)S(1)} %get-tuple-element.41), channel_id=1, source_target_pairs={{8,0},{16,8},{24,16},{9,1},{17,9},{25,17},{10,2},{18,10},{26,18},{... | collective-permute-start | bytes 786440 | tf_op jit(solution)/shard_map/ppermute | solution.py:505
  71.4 0.1 collective-permute-start.11
  71.5 1.1 %collective-permute-start.12 = (f32[1,64,512]{2,1,0:T(8,128)S(1)}, f32[1,64,512]{2,1,0:T(8,128)S(1)}, u32[]{:S(2)}, u32[]{:S(2)}) collective-permute-start(f32[1,64,512]{2,1,0:T(8,128)S(1)} %copy-done), channel_id=1, source_target_pairs={{0,7},{8,15},{16,17},{24,25},{1,0},{9,8},{17,18},{25,26},{2,1},{10... | collective-permute-start | bytes 393224 | tf_op jit(solution)/shard_map/ppermute | solution.py:501
  72.6 0.9 collective-permute-done.8.high_now
  73.5 13.6 %density_step.1 = (f32[2,16,64,512]{3,2,1,0:T(8,128)}, f32[3,64,512]{2,1,0:T(8,128)S(1)}) custom-call(f32[2,16,64,512]{3,2,1,0:T(8,128)} %density.3, f32[2,16,64,512]{3,2,1,0:T(8,128)} %get-tuple-element.22.control, f32[2,2,64,512]{3,2,1,0:T(8,128)S(1)} %collective-permute-done.3.low, f32[2,2,64,512]{3,2,1,0:T(8,128)S(1)} %collective-permute-done.4.high, ...), custom_call_target="tpu_custom_call" | custom-call | tf_op jit(solution)/shard_map/density_step/pallas_call | solution.py:346
  87.1 2.6 %collective-permute-done.9.refs_0_ = f32[6,64,512]{2,1,0:T(8,128)S(1)} collective-permute-done((f32[6,64,512]{2,1,0:T(8,128)}, f32[6,64,512]{2,1,0:T(8,128)S(1)}, u32[]{:S(2)}, u32[]{:S(2)}) %collective-permute-start.9) | collective-permute-done | bytes 786464 | tf_op jit(solution)/shard_map/ppermute | solution.py:501
  89.7 2.6 %arrive.2.partial = f32[2,16,64,512]{3,2,1,0:T(8,128)} custom-call(f32[2,16,64,512]{3,2,1,0:T(8,128)} %get-tuple-element.42.partial, f32[6,64,512]{2,1,0:T(8,128)S(1)} %collective-permute-done.9.refs_0_), custom_call_target="tpu_custom_call", output_to_operand_aliasing={{}: (0, {})} | custom-call | tf_op jit(solution)/shard_map/arrive/pallas_call | solution.py:396
  92.3 2.9 %arrive.3.partial = f32[2,16,64,512]{3,2,1,0:T(8,128)} custom-call(f32[2,16,64,512]{3,2,1,0:T(8,128)} %arrive.2.partial, f32[7,64,512]{2,1,0:T(8,128)S(1)} %collective-permute-done.10.refs_0_), custom_call_target="tpu_custom_call", output_to_operand_aliasing={{}: (0, {})} | custom-call | tf_op jit(solution)/shard_map/arrive/pallas_call | solution.py:396
  95.2 0.1 collective-permute-done.11.halo
  95.3 0.7 arrive_rest.2.partial
  96.1 2.1 %collective-permute-done.12.halo = f32[1,64,512]{2,1,0:T(8,128)S(1)} collective-permute-done((f32[1,64,512]{2,1,0:T(8,128)S(1)}, f32[1,64,512]{2,1,0:T(8,128)S(1)}, u32[]{:S(2)}, u32[]{:S(2)}) %collective-permute-start.12) | collective-permute-done | bytes 131104 | tf_op jit(solution)/shard_map/ppermute | solution.py:501
  98.1 0.7 arrive_rest.3
  (9 shorter events, 0.1 us)
Async XLA Ops:
  1.5 9.7 %collective-permute-start = (f32[2,32,512]{2,1,0:T(8,128)S(1)}, f32[2,32,512]{2,1,0:T(8,128)S(1)}, u32[]{:S(2)}, u32[]{:S(2)}) collective-permute-start(f32[2,32,512]{2,1,0:T(8,128)S(1)} %value_rows.3), channel_id=1, source_target_pairs={{0,1},{8,9},{16,23},{24,31},{1,2},{9,10},{17,16},{25,24},{2,3},{10... | collective-permute-start | bytes 393224 | tf_op jit(solution)/shard_map/ppermute | solution.py:487
  5.9 47.4 %collective-permute-start.1 = (f32[17,32,512]{2,1,0:T(8,128)S(1)}, f32[17,32,512]{2,1,0:T(8,128)S(1)}, u32[]{:S(2)}, u32[]{:S(2)}) collective-permute-start(f32[17,32,512]{2,1,0:T(8,128)S(1)} %value_rows.4), channel_id=1, source_target_pairs={{0,1},{8,9},{16,23},{24,31},{1,2},{9,10},{17,16},{25,24},{2,3},{10... | collective-permute-start | bytes 3342344 | tf_op jit(solution)/shard_map/ppermute | solution.py:487
  14.7 30.4 %collective-permute-start.5 = (f32[7,64,512]{2,1,0:T(8,128)}, f32[7,64,512]{2,1,0:T(8,128)}, u32[]{:S(2)}, u32[]{:S(2)}) collective-permute-start(f32[7,64,512]{2,1,0:T(8,128)} %get-tuple-element.31), channel_id=1, source_target_pairs={{0,6},{8,14},{16,16},{24,24},{1,1},{9,9},{17,19},{25,27},{2,0},{10... | collective-permute-start | bytes 2752520 | tf_op jit(solution)/shard_map/ppermute | solution.py:491
  20.4 32.9 %collective-permute-start.2 = (f32[13,32,512]{2,1,0:T(8,128)}, f32[13,32,512]{2,1,0:T(8,128)S(1)}, u32[]{:S(2)}, u32[]{:S(2)}) collective-permute-start(f32[13,32,512]{2,1,0:T(8,128)} %value_rows.5), channel_id=1, source_target_pairs={{0,1},{8,9},{16,23},{24,31},{1,2},{9,10},{17,16},{25,24},{2,3},{10... | collective-permute-start | bytes 2555912 | tf_op jit(solution)/shard_map/ppermute | solution.py:487
  23.8 20.0 %collective-permute-start.6 = (f32[2,64,512]{2,1,0:T(8,128)}, f32[2,64,512]{2,1,0:T(8,128)S(1)}, u32[]{:S(2)}, u32[]{:S(2)}) collective-permute-start(f32[2,64,512]{2,1,0:T(8,128)} %get-tuple-element.32), channel_id=1, source_target_pairs={{0,6},{8,14},{16,16},{24,24},{1,1},{9,9},{17,19},{25,27},{2,0},{10... | collective-permute-start | bytes 786440 | tf_op jit(solution)/shard_map/ppermute | solution.py:491
  38.9 32.6 %copy-start = (f32[1,64,512]{2,1,0:T(8,128)S(1)}, f32[1,64,512]{2,1,0:T(8,128)}, u32[]{:S(2)}) copy-start(f32[1,64,512]{2,1,0:T(8,128)} %get-tuple-element.45) | copy-start | bytes 393220
  38.9 6.3 %collective-permute-start.3 = (f32[2,2,64,512]{3,2,1,0:T(8,128)}, f32[2,2,64,512]{3,2,1,0:T(8,128)S(1)}, u32[]{:S(2)}, u32[]{:S(2)}) collective-permute-start(f32[2,2,64,512]{3,2,1,0:T(8,128)} %get-tuple-element.29), channel_id=1, source_target_pairs={{0,8},{8,16},{16,24},{1,9},{9,17},{17,25},{2,10},{10,18},{18,26},{... | collective-permute-start | bytes 1572872 | tf_op jit(solution)/shard_map/ppermute | solution.py:495
  43.8 4.0 %collective-permute-start.4 = (f32[2,2,64,512]{3,2,1,0:T(8,128)}, f32[2,2,64,512]{3,2,1,0:T(8,128)S(1)}, u32[]{:S(2)}, u32[]{:S(2)}) collective-permute-start(f32[2,2,64,512]{3,2,1,0:T(8,128)} %get-tuple-element.30), channel_id=1, source_target_pairs={{8,0},{16,8},{24,16},{9,1},{17,9},{25,17},{10,2},{18,10},{26,18},{... | collective-permute-start | bytes 1572872 | tf_op jit(solution)/shard_map/ppermute | solution.py:496
  45.1 47.2 %collective-permute-start.10 = (f32[7,64,512]{2,1,0:T(8,128)}, f32[7,64,512]{2,1,0:T(8,128)S(1)}, u32[]{:S(2)}, u32[]{:S(2)}) collective-permute-start(f32[7,64,512]{2,1,0:T(8,128)} %collective-permute-done.5), channel_id=1, source_target_pairs={{0,1},{8,9},{16,17},{24,25},{1,0},{9,8},{17,16},{25,24},{2,3},{10,... | collective-permute-start | bytes 2752520 | tf_op jit(solution)/shard_map/ppermute | solution.py:500
  53.3 36.4 %collective-permute-start.9 = (f32[6,64,512]{2,1,0:T(8,128)}, f32[6,64,512]{2,1,0:T(8,128)S(1)}, u32[]{:S(2)}, u32[]{:S(2)}) collective-permute-start(f32[6,64,512]{2,1,0:T(8,128)} %get-tuple-element.43), channel_id=1, source_target_pairs={{0,7},{8,15},{16,17},{24,25},{1,0},{9,8},{17,18},{25,26},{2,1},{10... | collective-permute-start | bytes 2359304 | tf_op jit(solution)/shard_map/ppermute | solution.py:501
  66.3 5.1 %collective-permute-start.7 = (f32[2,64,512]{2,1,0:T(8,128)S(1)}, f32[2,64,512]{2,1,0:T(8,128)S(1)}, u32[]{:S(2)}, u32[]{:S(2)}) collective-permute-start(f32[2,64,512]{2,1,0:T(8,128)S(1)} %get-tuple-element.40), channel_id=1, source_target_pairs={{0,8},{8,16},{16,24},{1,9},{9,17},{17,25},{2,10},{10,18},{18,26},{... | collective-permute-start | bytes 786440 | tf_op jit(solution)/shard_map/ppermute | solution.py:504
  70.1 3.4 %collective-permute-start.8 = (f32[2,64,512]{2,1,0:T(8,128)S(1)}, f32[2,64,512]{2,1,0:T(8,128)S(1)}, u32[]{:S(2)}, u32[]{:S(2)}) collective-permute-start(f32[2,64,512]{2,1,0:T(8,128)S(1)} %get-tuple-element.41), channel_id=1, source_target_pairs={{8,0},{16,8},{24,16},{9,1},{17,9},{25,17},{10,2},{18,10},{26,18},{... | collective-permute-start | bytes 786440 | tf_op jit(solution)/shard_map/ppermute | solution.py:505
  71.4 23.9 %collective-permute-start.11 = (f32[2,64,512]{2,1,0:T(8,128)S(1)}, f32[2,64,512]{2,1,0:T(8,128)S(1)}, u32[]{:S(2)}, u32[]{:S(2)}) collective-permute-start(f32[2,64,512]{2,1,0:T(8,128)S(1)} %collective-permute-done.6), channel_id=1, source_target_pairs={{0,1},{8,9},{16,17},{24,25},{1,0},{9,8},{17,16},{25,24},{2,3},{10,... | collective-permute-start | bytes 786440 | tf_op jit(solution)/shard_map/ppermute | solution.py:500
  71.5 26.6 %collective-permute-start.12 = (f32[1,64,512]{2,1,0:T(8,128)S(1)}, f32[1,64,512]{2,1,0:T(8,128)S(1)}, u32[]{:S(2)}, u32[]{:S(2)}) collective-permute-start(f32[1,64,512]{2,1,0:T(8,128)S(1)} %copy-done), channel_id=1, source_target_pairs={{0,7},{8,15},{16,17},{24,25},{1,0},{9,8},{17,18},{25,26},{2,1},{10... | collective-permute-start | bytes 393224 | tf_op jit(solution)/shard_map/ppermute | solution.py:501

commit v11 on v7

--- a/solution.py
+++ b/solution.py
@@ -415,14 +415,18 @@
     count, rows = partial.shape[:2]
     extent = halo.shape[0]
     skipped = begin - (rows - rest.shape[0])
+    step = halo.shape[1] // 2
     row = jnp.where(is_negative(), count - 1, 0)
     base = lax.axis_index("vel") * rows + begin
     total = rows * lax.axis_size("vel")
     copies = []
     for a in range(extent):
-        held[a] = rest[skipped + a] + slant(base + a, total) * halo[a]
-        copies.append(pltpu.make_async_copy(held.at[a], out.at[row, begin + a], sems.at[a]))
-        copies[-1].start()
+        for u in range(2):
+            part = pl.ds(u * step, step)
+            held[a, part] = rest[skipped + a, part] + slant(base + a, total) * halo[a, part]
+            target = out.at[row, begin + a, part]
+            copies.append(pltpu.make_async_copy(held.at[a, part], target, sems.at[2 * a + u]))
+            copies[-1].start()
     wait_all(copies)
 
 
@@ -434,7 +438,7 @@
         out_specs=ANY,
         scratch_shapes=[
             pltpu.VMEM(halo.shape, halo.dtype),
-            pltpu.SemaphoreType.DMA((halo.shape[0],)),
+            pltpu.SemaphoreType.DMA((2 * halo.shape[0],)),
         ],
         input_output_aliases={0: 0},
         compiler_params=pltpu.CompilerParams(vmem_limit_bytes=VMEM_LIMIT),

time: 99.8 us -> 99.8 us (level)
  no operation moved by 1% of the time
where the time goes in v11:
time: 99.8 us; the launch traced here: 98.8 us
  Pallas kernels  37.2 us (37%)
  starting transfers between devices  30.1 us (30%)
  waiting for transfers between devices  22.3 us (22%)
  blocking collectives  5.96 us (6%)
  other arithmetic  2.46 us (2%)
    pallas_call x1, Pallas kernels, density_step(): pl.pallas_call(density_kernel, out_shape=[jax.ShapeDtypeStruct(density.sh...  13.6 us
    pallas_call x1, Pallas kernels, value_step(): pl.pallas_call(value_kernel, out_shape=[jax.ShapeDtypeStruct(value.shape,...  10.2 us
    ppermute x2, starting transfers between devices, body(): fillers = [lax.ppermute(part, names, over_route) for part in parts[1::2]]  10.2 us
    ppermute x3, waiting for transfers between devices, body(): lax.ppermute(value_rows(value_next, begin, end), names, value_route)  9.19 us
    ppermute x3, starting transfers between devices, body(): lax.ppermute(value_rows(value_next, begin, end), names, value_route)  7.95 us
    psum x1, blocking collectives, body(): mass = lax.psum(jnp.sum(density, axis=(1, 2)), 'vel') / (second * second)  5.96 us
    ppermute x2, waiting for transfers between devices, body(): parts = [lax.ppermute(part, names, density_route) for part in parts]  4.64 us
    pallas_call x3, Pallas kernels, value_rows(): pl.pallas_call(functools.partial(value_rows_kernel, begin), out_shape=[pl...  4.5 us
  transfers between devices with their start and end apart: 13, of which 9 were waited for; matrix products, arithmetic and copies ran while one was open for 2% of the time, Pallas kernels for 36%

profile of v11, /device:TPU:0, one launch (start us, length us, event | category | flops | bytes accessed | tf_op | source)
XLA Modules:
  0.0 98.8 jit_solution(2130599204367717295)
XLA Ops:
  0.6 0.9 value_rows.3
  1.5 3.0 %collective-permute-start = (f32[2,32,512]{2,1,0:T(8,128)S(1)}, f32[2,32,512]{2,1,0:T(8,128)S(1)}, u32[]{:S(2)}, u32[]{:S(2)}) collective-permute-start(f32[2,32,512]{2,1,0:T(8,128)S(1)} %value_rows.3), channel_id=1, source_target_pairs={{0,1},{8,9},{16,23},{24,31},{1,2},{9,10},{17,16},{25,24},{2,3},{10... | collective-permute-start | bytes 393224 | tf_op jit(solution)/shard_map/ppermute | solution.py:491
  4.5 1.4 %value_rows.4 = f32[17,32,512]{2,1,0:T(8,128)S(1)} custom-call(f32[2,16,64,512]{3,2,1,0:T(8,128)} %value.9), custom_call_target="tpu_custom_call" | custom-call | tf_op jit(solution)/shard_map/value_rows/pallas_call | solution.py:95
  5.9 1.6 %collective-permute-start.1 = (f32[17,32,512]{2,1,0:T(8,128)S(1)}, f32[17,32,512]{2,1,0:T(8,128)S(1)}, u32[]{:S(2)}, u32[]{:S(2)}) collective-permute-start(f32[17,32,512]{2,1,0:T(8,128)S(1)} %value_rows.4), channel_id=1, source_target_pairs={{0,1},{8,9},{16,23},{24,31},{1,2},{9,10},{17,16},{25,24},{2,3},{10... | collective-permute-start | bytes 3342344 | tf_op jit(solution)/shard_map/ppermute | solution.py:491
  7.5 3.7 %collective-permute-done.after.rest_0_ = f32[2,32,512]{2,1,0:T(8,128)S(1)} collective-permute-done((f32[2,32,512]{2,1,0:T(8,128)S(1)}, f32[2,32,512]{2,1,0:T(8,128)S(1)}, u32[]{:S(2)}, u32[]{:S(2)}) %collective-permute-start) | collective-permute-done | bytes 131104 | tf_op jit(solution)/shard_map/ppermute | solution.py:491
  11.2 3.5 %edges.1 = (f32[2,2,64,512]{3,2,1,0:T(8,128)}, f32[2,2,64,512]{3,2,1,0:T(8,128)}, f32[6,64,512]{2,1,0:T(8,128)}, f32[7,64,512]{2,1,0:T(8,128)}, f32[1,64,512]{2,1,0:T(8,128)}, /*index=5*/f32[2,64,512]{2,1,0:T(8,128)}) custom-call(f32[2,16,64,512]{3,2,1,0:T(8,128)} %value.9, f32[2,16,64,512]{3,2,1,0:T(8,128)} %density.3, ...), custom_call_target="tpu_custom_call" | custom-call | tf_op jit(solution)/shard_map/edges/pallas_call | solution.py:124
  14.7 3.5 %collective-permute-start.5 = (f32[7,64,512]{2,1,0:T(8,128)}, f32[7,64,512]{2,1,0:T(8,128)}, u32[]{:S(2)}, u32[]{:S(2)}) collective-permute-start(f32[7,64,512]{2,1,0:T(8,128)} %get-tuple-element.31), channel_id=1, source_target_pairs={{0,6},{8,14},{16,16},{24,24},{1,1},{9,9},{17,19},{25,27},{2,0},{10... | collective-permute-start | bytes 2752520 | tf_op jit(solution)/shard_map/ppermute | solution.py:495
  18.2 2.2 %value_rows.5 = f32[13,32,512]{2,1,0:T(8,128)} custom-call(f32[2,16,64,512]{3,2,1,0:T(8,128)} %value.9), custom_call_target="tpu_custom_call" | custom-call | tf_op jit(solution)/shard_map/value_rows/pallas_call | solution.py:95
  20.4 3.4 %collective-permute-start.2 = (f32[13,32,512]{2,1,0:T(8,128)}, f32[13,32,512]{2,1,0:T(8,128)S(1)}, u32[]{:S(2)}, u32[]{:S(2)}) collective-permute-start(f32[13,32,512]{2,1,0:T(8,128)} %value_rows.5), channel_id=1, source_target_pairs={{0,1},{8,9},{16,23},{24,31},{1,2},{9,10},{17,16},{25,24},{2,3},{10... | collective-permute-start | bytes 2555912 | tf_op jit(solution)/shard_map/ppermute | solution.py:491
  23.8 6.6 %collective-permute-start.6 = (f32[2,64,512]{2,1,0:T(8,128)}, f32[2,64,512]{2,1,0:T(8,128)S(1)}, u32[]{:S(2)}, u32[]{:S(2)}) collective-permute-start(f32[2,64,512]{2,1,0:T(8,128)} %get-tuple-element.32), channel_id=1, source_target_pairs={{0,6},{8,14},{16,16},{24,24},{1,1},{9,9},{17,19},{25,27},{2,0},{10... | collective-permute-start | bytes 786440 | tf_op jit(solution)/shard_map/ppermute | solution.py:495
  30.4 2.5 %reduce_sum.9 = f32[2,512]{1,0:T(2,128)S(1)} reduce(f32[2,16,64,512]{3,2,1,0:T(8,128)} %density.3, f32[]{:T(128)} %constant.2.clone.1), dimensions={1,2}, to_apply=%region_0.0 | reduce | flops 1047552 | bytes 4198404 | tf_op jit(solution)/shard_map/reduce_sum | solution.py:496
  32.9 6.0 %psum.7 = f32[2,512]{1,0:T(2,128)S(1)} all-reduce(f32[2,512]{1,0:T(2,128)S(1)} %reduce_sum.9), channel_id=1, replica_groups=mesh['vel'=4,'pos'=8] {'vel'}, use_global_device_ids=true, to_apply=%region_1.0 | all-reduce | flops 1024 | bytes 8192 | tf_op jit(solution)/shard_map/psum | solution.py:496
  38.9 1.6 %collective-permute-start.3 = (f32[2,2,64,512]{3,2,1,0:T(8,128)}, f32[2,2,64,512]{3,2,1,0:T(8,128)S(1)}, u32[]{:S(2)}, u32[]{:S(2)}) collective-permute-start(f32[2,2,64,512]{3,2,1,0:T(8,128)} %get-tuple-element.29), channel_id=1, source_target_pairs={{0,8},{8,16},{16,24},{1,9},{9,17},{17,25},{2,10},{10,18},{18,26},{... | collective-permute-start | bytes 1572872 | tf_op jit(solution)/shard_map/ppermute | solution.py:499
  40.5 3.3 %collective-permute-done.6 = f32[2,64,512]{2,1,0:T(8,128)S(1)} collective-permute-done((f32[2,64,512]{2,1,0:T(8,128)}, f32[2,64,512]{2,1,0:T(8,128)S(1)}, u32[]{:S(2)}, u32[]{:S(2)}) %collective-permute-start.6) | collective-permute-done | bytes 262176 | tf_op jit(solution)/shard_map/ppermute | solution.py:495
  43.8 1.3 %collective-permute-start.4 = (f32[2,2,64,512]{3,2,1,0:T(8,128)}, f32[2,2,64,512]{3,2,1,0:T(8,128)S(1)}, u32[]{:S(2)}, u32[]{:S(2)}) collective-permute-start(f32[2,2,64,512]{3,2,1,0:T(8,128)} %get-tuple-element.30), channel_id=1, source_target_pairs={{8,0},{16,8},{24,16},{9,1},{17,9},{25,17},{10,2},{18,10},{26,18},{... | collective-permute-start | bytes 1572872 | tf_op jit(solution)/shard_map/ppermute | solution.py:500
  45.2 2.6 %collective-permute-done.4.high = f32[2,2,64,512]{3,2,1,0:T(8,128)S(1)} collective-permute-done((f32[2,2,64,512]{3,2,1,0:T(8,128)}, f32[2,2,64,512]{3,2,1,0:T(8,128)S(1)}, u32[]{:S(2)}, u32[]{:S(2)}) %collective-permute-start.4) | collective-permute-done | bytes 524320 | tf_op jit(solution)/shard_map/ppermute | solution.py:500
  47.8 5.5 %collective-permute-done.2.rest_2_ = f32[13,32,512]{2,1,0:T(8,128)S(1)} collective-permute-done((f32[13,32,512]{2,1,0:T(8,128)}, f32[13,32,512]{2,1,0:T(8,128)S(1)}, u32[]{:S(2)}, u32[]{:S(2)}) %collective-permute-start.2) | collective-permute-done | bytes 852000 | tf_op jit(solution)/shard_map/ppermute | solution.py:491
  53.3 2.8 %collective-permute-start.9 = (f32[6,64,512]{2,1,0:T(8,128)}, f32[6,64,512]{2,1,0:T(8,128)S(1)}, u32[]{:S(2)}, u32[]{:S(2)}) collective-permute-start(f32[6,64,512]{2,1,0:T(8,128)} %get-tuple-element.43), channel_id=1, source_target_pairs={{0,7},{8,15},{16,17},{24,25},{1,0},{9,8},{17,18},{25,26},{2,1},{10... | collective-permute-start | bytes 2359304 | tf_op jit(solution)/shard_map/ppermute | solution.py:505
  56.1 10.2 %value_step.1 = (f32[2,16,64,512]{3,2,1,0:T(8,128)}, f32[2,64,512]{2,1,0:T(8,128)S(1)}, f32[2,64,512]{2,1,0:T(8,128)S(1)}) custom-call(f32[2,16,64,512]{3,2,1,0:T(8,128)} %value.9, f32[2,2,64,512]{3,2,1,0:T(8,128)S(1)} %collective-permute-done.3.low, f32[2,2,64,512]{3,2,1,0:T(8,128)S(1)} %collective-permute-done.4.high, ...), custom_call_target="tpu_custom_call" | custom-call | tf_op jit(solution)/shard_map/value_step/pallas_call | solution.py:245
  66.3 3.8 %collective-permute-start.7 = (f32[2,64,512]{2,1,0:T(8,128)S(1)}, f32[2,64,512]{2,1,0:T(8,128)S(1)}, u32[]{:S(2)}, u32[]{:S(2)}) collective-permute-start(f32[2,64,512]{2,1,0:T(8,128)S(1)} %get-tuple-element.40), channel_id=1, source_target_pairs={{0,8},{8,16},{16,24},{1,9},{9,17},{17,25},{2,10},{10,18},{18,26},{... | collective-permute-start | bytes 786440 | tf_op jit(solution)/shard_map/ppermute | solution.py:508
  70.1 1.3 %collective-permute-start.8 = (f32[2,64,512]{2,1,0:T(8,128)S(1)}, f32[2,64,512]{2,1,0:T(8,128)S(1)}, u32[]{:S(2)}, u32[]{:S(2)}) collective-permute-start(f32[2,64,512]{2,1,0:T(8,128)S(1)} %get-tuple-element.41), channel_id=1, source_target_pairs={{8,0},{16,8},{24,16},{9,1},{17,9},{25,17},{10,2},{18,10},{26,18},{... | collective-permute-start | bytes 786440 | tf_op jit(solution)/shard_map/ppermute | solution.py:509
  71.4 0.1 collective-permute-start.11
  71.5 1.1 %collective-permute-start.12 = (f32[1,64,512]{2,1,0:T(8,128)S(1)}, f32[1,64,512]{2,1,0:T(8,128)S(1)}, u32[]{:S(2)}, u32[]{:S(2)}) collective-permute-start(f32[1,64,512]{2,1,0:T(8,128)S(1)} %copy-done), channel_id=1, source_target_pairs={{0,7},{8,15},{16,17},{24,25},{1,0},{9,8},{17,18},{25,26},{2,1},{10... | collective-permute-start | bytes 393224 | tf_op jit(solution)/shard_map/ppermute | solution.py:505
  72.6 0.9 collective-permute-done.8.high_now
  73.5 13.6 %density_step.1 = (f32[2,16,64,512]{3,2,1,0:T(8,128)}, f32[3,64,512]{2,1,0:T(8,128)S(1)}) custom-call(f32[2,16,64,512]{3,2,1,0:T(8,128)} %density.3, f32[2,16,64,512]{3,2,1,0:T(8,128)} %get-tuple-element.22.control, f32[2,2,64,512]{3,2,1,0:T(8,128)S(1)} %collective-permute-done.3.low, f32[2,2,64,512]{3,2,1,0:T(8,128)S(1)} %collective-permute-done.4.high, ...), custom_call_target="tpu_custom_call" | custom-call | tf_op jit(solution)/shard_map/density_step/pallas_call | solution.py:346
  87.1 2.6 %collective-permute-done.9.refs_0_ = f32[6,64,512]{2,1,0:T(8,128)S(1)} collective-permute-done((f32[6,64,512]{2,1,0:T(8,128)}, f32[6,64,512]{2,1,0:T(8,128)S(1)}, u32[]{:S(2)}, u32[]{:S(2)}) %collective-permute-start.9) | collective-permute-done | bytes 786464 | tf_op jit(solution)/shard_map/ppermute | solution.py:505
  89.7 0.5 collective-permute-done.10.refs_1_
  90.2 4.0 %arrive.1.partial = f32[2,16,64,512]{3,2,1,0:T(8,128)} custom-call(f32[2,16,64,512]{3,2,1,0:T(8,128)} %get-tuple-element.42.partial, f32[6,64,512]{2,1,0:T(8,128)S(1)} %collective-permute-done.9.refs_0_, f32[7,64,512]{2,1,0:T(8,128)S(1)} %collective-permute-done.10.refs_1_), custom_call_target="tpu_custom_call", output_to_operand_aliasing={{}: (0, {})} | custom-call | tf_op jit(solution)/shard_map/arrive/pallas_call | solution.py:396
  94.2 1.1 %collective-permute-done.11.halo = f32[2,64,512]{2,1,0:T(8,128)S(1)} collective-permute-done((f32[2,64,512]{2,1,0:T(8,128)S(1)}, f32[2,64,512]{2,1,0:T(8,128)S(1)}, u32[]{:S(2)}, u32[]{:S(2)}) %collective-permute-start.11) | collective-permute-done | bytes 262176 | tf_op jit(solution)/shard_map/ppermute | solution.py:504
  95.3 0.7 arrive_rest.2.partial
  96.1 2.1 %collective-permute-done.12.halo = f32[1,64,512]{2,1,0:T(8,128)S(1)} collective-permute-done((f32[1,64,512]{2,1,0:T(8,128)S(1)}, f32[1,64,512]{2,1,0:T(8,128)S(1)}, u32[]{:S(2)}, u32[]{:S(2)}) %collective-permute-start.12) | collective-permute-done | bytes 131104 | tf_op jit(solution)/shard_map/ppermute | solution.py:505
  98.1 0.7 arrive_rest.3
  (8 shorter events, 0.1 us)
Async XLA Ops:
  1.5 9.7 %collective-permute-start = (f32[2,32,512]{2,1,0:T(8,128)S(1)}, f32[2,32,512]{2,1,0:T(8,128)S(1)}, u32[]{:S(2)}, u32[]{:S(2)}) collective-permute-start(f32[2,32,512]{2,1,0:T(8,128)S(1)} %value_rows.3), channel_id=1, source_target_pairs={{0,1},{8,9},{16,23},{24,31},{1,2},{9,10},{17,16},{25,24},{2,3},{10... | collective-permute-start | bytes 393224 | tf_op jit(solution)/shard_map/ppermute | solution.py:491
  5.9 47.4 %collective-permute-start.1 = (f32[17,32,512]{2,1,0:T(8,128)S(1)}, f32[17,32,512]{2,1,0:T(8,128)S(1)}, u32[]{:S(2)}, u32[]{:S(2)}) collective-permute-start(f32[17,32,512]{2,1,0:T(8,128)S(1)} %value_rows.4), channel_id=1, source_target_pairs={{0,1},{8,9},{16,23},{24,31},{1,2},{9,10},{17,16},{25,24},{2,3},{10... | collective-permute-start | bytes 3342344 | tf_op jit(solution)/shard_map/ppermute | solution.py:491
  14.7 30.4 %collective-permute-start.5 = (f32[7,64,512]{2,1,0:T(8,128)}, f32[7,64,512]{2,1,0:T(8,128)}, u32[]{:S(2)}, u32[]{:S(2)}) collective-permute-start(f32[7,64,512]{2,1,0:T(8,128)} %get-tuple-element.31), channel_id=1, source_target_pairs={{0,6},{8,14},{16,16},{24,24},{1,1},{9,9},{17,19},{25,27},{2,0},{10... | collective-permute-start | bytes 2752520 | tf_op jit(solution)/shard_map/ppermute | solution.py:495
  20.4 32.9 %collective-permute-start.2 = (f32[13,32,512]{2,1,0:T(8,128)}, f32[13,32,512]{2,1,0:T(8,128)S(1)}, u32[]{:S(2)}, u32[]{:S(2)}) collective-permute-start(f32[13,32,512]{2,1,0:T(8,128)} %value_rows.5), channel_id=1, source_target_pairs={{0,1},{8,9},{16,23},{24,31},{1,2},{9,10},{17,16},{25,24},{2,3},{10... | collective-permute-start | bytes 2555912 | tf_op jit(solution)/shard_map/ppermute | solution.py:491
  23.8 20.0 %collective-permute-start.6 = (f32[2,64,512]{2,1,0:T(8,128)}, f32[2,64,512]{2,1,0:T(8,128)S(1)}, u32[]{:S(2)}, u32[]{:S(2)}) collective-permute-start(f32[2,64,512]{2,1,0:T(8,128)} %get-tuple-element.32), channel_id=1, source_target_pairs={{0,6},{8,14},{16,16},{24,24},{1,1},{9,9},{17,19},{25,27},{2,0},{10... | collective-permute-start | bytes 786440 | tf_op jit(solution)/shard_map/ppermute | solution.py:495
  38.9 32.6 %copy-start = (f32[1,64,512]{2,1,0:T(8,128)S(1)}, f32[1,64,512]{2,1,0:T(8,128)}, u32[]{:S(2)}) copy-start(f32[1,64,512]{2,1,0:T(8,128)} %get-tuple-element.45) | copy-start | bytes 393220
  38.9 6.3 %collective-permute-start.3 = (f32[2,2,64,512]{3,2,1,0:T(8,128)}, f32[2,2,64,512]{3,2,1,0:T(8,128)S(1)}, u32[]{:S(2)}, u32[]{:S(2)}) collective-permute-start(f32[2,2,64,512]{3,2,1,0:T(8,128)} %get-tuple-element.29), channel_id=1, source_target_pairs={{0,8},{8,16},{16,24},{1,9},{9,17},{17,25},{2,10},{10,18},{18,26},{... | collective-permute-start | bytes 1572872 | tf_op jit(solution)/shard_map/ppermute | solution.py:499
  43.8 4.0 %collective-permute-start.4 = (f32[2,2,64,512]{3,2,1,0:T(8,128)}, f32[2,2,64,512]{3,2,1,0:T(8,128)S(1)}, u32[]{:S(2)}, u32[]{:S(2)}) collective-permute-start(f32[2,2,64,512]{3,2,1,0:T(8,128)} %get-tuple-element.30), channel_id=1, source_target_pairs={{8,0},{16,8},{24,16},{9,1},{17,9},{25,17},{10,2},{18,10},{26,18},{... | collective-permute-start | bytes 1572872 | tf_op jit(solution)/shard_map/ppermute | solution.py:500
  45.1 45.1 %collective-permute-start.10 = (f32[7,64,512]{2,1,0:T(8,128)}, f32[7,64,512]{2,1,0:T(8,128)S(1)}, u32[]{:S(2)}, u32[]{:S(2)}) collective-permute-start(f32[7,64,512]{2,1,0:T(8,128)} %collective-permute-done.5), channel_id=1, source_target_pairs={{0,1},{8,9},{16,17},{24,25},{1,0},{9,8},{17,16},{25,24},{2,3},{10,... | collective-permute-start | bytes 2752520 | tf_op jit(solution)/shard_map/ppermute | solution.py:504
  53.3 36.4 %collective-permute-start.9 = (f32[6,64,512]{2,1,0:T(8,128)}, f32[6,64,512]{2,1,0:T(8,128)S(1)}, u32[]{:S(2)}, u32[]{:S(2)}) collective-permute-start(f32[6,64,512]{2,1,0:T(8,128)} %get-tuple-element.43), channel_id=1, source_target_pairs={{0,7},{8,15},{16,17},{24,25},{1,0},{9,8},{17,18},{25,26},{2,1},{10... | collective-permute-start | bytes 2359304 | tf_op jit(solution)/shard_map/ppermute | solution.py:505
  66.3 5.1 %collective-permute-start.7 = (f32[2,64,512]{2,1,0:T(8,128)S(1)}, f32[2,64,512]{2,1,0:T(8,128)S(1)}, u32[]{:S(2)}, u32[]{:S(2)}) collective-permute-start(f32[2,64,512]{2,1,0:T(8,128)S(1)} %get-tuple-element.40), channel_id=1, source_target_pairs={{0,8},{8,16},{16,24},{1,9},{9,17},{17,25},{2,10},{10,18},{18,26},{... | collective-permute-start | bytes 786440 | tf_op jit(solution)/shard_map/ppermute | solution.py:508
  70.1 3.4 %collective-permute-start.8 = (f32[2,64,512]{2,1,0:T(8,128)S(1)}, f32[2,64,512]{2,1,0:T(8,128)S(1)}, u32[]{:S(2)}, u32[]{:S(2)}) collective-permute-start(f32[2,64,512]{2,1,0:T(8,128)S(1)} %get-tuple-element.41), channel_id=1, source_target_pairs={{8,0},{16,8},{24,16},{9,1},{17,9},{25,17},{10,2},{18,10},{26,18},{... | collective-permute-start | bytes 786440 | tf_op jit(solution)/shard_map/ppermute | solution.py:509
  71.4 23.9 %collective-permute-start.11 = (f32[2,64,512]{2,1,0:T(8,128)S(1)}, f32[2,64,512]{2,1,0:T(8,128)S(1)}, u32[]{:S(2)}, u32[]{:S(2)}) collective-permute-start(f32[2,64,512]{2,1,0:T(8,128)S(1)} %collective-permute-done.6), channel_id=1, source_target_pairs={{0,1},{8,9},{16,17},{24,25},{1,0},{9,8},{17,16},{25,24},{2,3},{10,... | collective-permute-start | bytes 786440 | tf_op jit(solution)/shard_map/ppermute | solution.py:504
  71.5 26.6 %collective-permute-start.12 = (f32[1,64,512]{2,1,0:T(8,128)S(1)}, f32[1,64,512]{2,1,0:T(8,128)S(1)}, u32[]{:S(2)}, u32[]{:S(2)}) collective-permute-start(f32[1,64,512]{2,1,0:T(8,128)S(1)} %copy-done), channel_id=1, source_target_pairs={{0,7},{8,15},{16,17},{24,25},{1,0},{9,8},{17,18},{25,26},{2,1},{10... | collective-permute-start | bytes 393224 | tf_op jit(solution)/shard_map/ppermute | solution.py:505

commit v12 on v7

--- a/solution.py
+++ b/solution.py
@@ -15,7 +15,7 @@
 SUB = 8
 LANES = 128
 EARLY = 1
-SHIFT = 1
+SHIFT = 2
 VMEM_LIMIT = 18 * 1024 * 1024
 ANY = pl.BlockSpec(memory_space=pl.ANY)
 VMEM = pl.BlockSpec(memory_space=pltpu.VMEM)

time: 99.8 us -> 122 us (1.22)
  waiting for transfers between devices: 22.3 us -> 42.6 us
    ppermute x3, waiting for transfers between devices: 9.19 us -> 29.3 us  [body(): lax.ppermute(value_rows(value_next, begin, end), names, value_route)]
    ppermute x1, starting transfers between devices: 3.75 us -> 9.96 us  [body(): low_now = lax.ppermute(low_now, 'vel', onward)]
    ppermute x2, waiting for transfers between devices: 3.28 us -> 7.89 us  [body(): fillers = [lax.ppermute(part, names, over_route) for part in parts[1::2]]]
    ppermute x2, starting transfers between devices: 10.2 us -> 5.98 us  [body(): fillers = [lax.ppermute(part, names, over_route) for part in parts[1::2]]]
    ppermute x2, waiting for transfers between devices: 4.65 us -> 1.77 us  [body(): parts = [lax.ppermute(part, names, density_route) for part in parts]]
    ppermute x2, waiting for transfers between devices: 1.63 us -> 0.01 us  [body(): fillers = [lax.ppermute(part, names, swap_route) for part in fillers]]
  transfers between devices with their start and end apart: 13 -> 13, of which waited for: 9 -> 5; matrix products, arithmetic and copies ran while one was open for 2% -> 2% of each run, Pallas kernels for 36% -> 29%
where the time goes in v12:
time: 122 us; the launch traced here: 120 us
  waiting for transfers between devices  42.6 us (35%)
  Pallas kernels  37.2 us (30%)
  starting transfers between devices  30.5 us (25%)
  blocking collectives  6.64 us (5%)
  other arithmetic  2.46 us (2%)
    ppermute x3, waiting for transfers between devices, body(): lax.ppermute(value_rows(value_next, begin, end), names, value_route)  29.3 us
    pallas_call x1, Pallas kernels, density_step(): pl.pallas_call(density_kernel, out_shape=[jax.ShapeDtypeStruct(density.sh...  13.6 us
    pallas_call x1, Pallas kernels, value_step(): pl.pallas_call(value_kernel, out_shape=[jax.ShapeDtypeStruct(value.shape,...  10.2 us
    ppermute x1, starting transfers between devices, body(): low_now = lax.ppermute(low_now, 'vel', onward)  9.96 us
    ppermute x2, waiting for transfers between devices, body(): fillers = [lax.ppermute(part, names, over_route) for part in parts[1::2]]  7.89 us
    ppermute x3, starting transfers between devices, body(): lax.ppermute(value_rows(value_next, begin, end), names, value_route)  7.24 us
    psum x1, blocking collectives, body(): mass = lax.psum(jnp.sum(density, axis=(1, 2)), 'vel') / (second * second)  6.64 us
    ppermute x2, starting transfers between devices, body(): fillers = [lax.ppermute(part, names, over_route) for part in parts[1::2]]  5.98 us
  transfers between devices with their start and end apart: 13, of which 5 were waited for; matrix products, arithmetic and copies ran while one was open for 2% of the time, Pallas kernels for 29%

profile of v12, /device:TPU:0, one launch (start us, length us, event | category | flops | bytes accessed | tf_op | source)
XLA Modules:
  0.0 120.2 jit_solution(10698039177779358699)
XLA Ops:
  0.6 1.4 %value_rows.4 = f32[18,32,512]{2,1,0:T(8,128)S(1)} custom-call(f32[2,16,64,512]{3,2,1,0:T(8,128)} %value.9), custom_call_target="tpu_custom_call" | custom-call | tf_op jit(solution)/shard_map/value_rows/pallas_call | solution.py:95
  2.1 3.0 %collective-permute-start.1 = (f32[18,32,512]{2,1,0:T(8,128)S(1)}, f32[18,32,512]{2,1,0:T(8,128)S(1)}, u32[]{:S(2)}, u32[]{:S(2)}) collective-permute-start(f32[18,32,512]{2,1,0:T(8,128)S(1)} %value_rows.4), channel_id=1, source_target_pairs={{0,1},{8,9},{16,23},{24,31},{1,2},{9,10},{17,16},{25,24},{2,3},{10... | collective-permute-start | bytes 3538952 | tf_op jit(solution)/shard_map/ppermute | solution.py:487
  5.1 0.9 value_rows.3
  6.0 1.6 %collective-permute-start = (f32[2,32,512]{2,1,0:T(8,128)S(1)}, f32[2,32,512]{2,1,0:T(8,128)S(1)}, u32[]{:S(2)}, u32[]{:S(2)}) collective-permute-start(f32[2,32,512]{2,1,0:T(8,128)S(1)} %value_rows.3), channel_id=1, source_target_pairs={{0,1},{8,9},{16,23},{24,31},{1,2},{9,10},{17,16},{25,24},{2,3},{10... | collective-permute-start | bytes 393224 | tf_op jit(solution)/shard_map/ppermute | solution.py:487
  7.6 29.3 %collective-permute-done.after.rest_0_ = f32[2,32,512]{2,1,0:T(8,128)S(1)} collective-permute-done((f32[2,32,512]{2,1,0:T(8,128)S(1)}, f32[2,32,512]{2,1,0:T(8,128)S(1)}, u32[]{:S(2)}, u32[]{:S(2)}) %collective-permute-start) | collective-permute-done | bytes 131104 | tf_op jit(solution)/shard_map/ppermute | solution.py:487
  36.9 3.5 %edges.1 = (f32[2,2,64,512]{3,2,1,0:T(8,128)}, f32[2,2,64,512]{3,2,1,0:T(8,128)}, f32[6,64,512]{2,1,0:T(8,128)}, f32[7,64,512]{2,1,0:T(8,128)}, f32[1,64,512]{2,1,0:T(8,128)}, /*index=5*/f32[2,64,512]{2,1,0:T(8,128)}) custom-call(f32[2,16,64,512]{3,2,1,0:T(8,128)} %value.9, f32[2,16,64,512]{3,2,1,0:T(8,128)} %density.3, ...), custom_call_target="tpu_custom_call" | custom-call | tf_op jit(solution)/shard_map/edges/pallas_call | solution.py:124
  40.4 3.6 %collective-permute-start.5 = (f32[7,64,512]{2,1,0:T(8,128)}, f32[7,64,512]{2,1,0:T(8,128)}, u32[]{:S(2)}, u32[]{:S(2)}) collective-permute-start(f32[7,64,512]{2,1,0:T(8,128)} %get-tuple-element.31), channel_id=1, source_target_pairs={{0,6},{8,14},{16,16},{24,24},{1,1},{9,9},{17,19},{25,27},{2,0},{10... | collective-permute-start | bytes 2752520 | tf_op jit(solution)/shard_map/ppermute | solution.py:491
  44.0 2.4 %collective-permute-start.6 = (f32[2,64,512]{2,1,0:T(8,128)}, f32[2,64,512]{2,1,0:T(8,128)S(1)}, u32[]{:S(2)}, u32[]{:S(2)}) collective-permute-start(f32[2,64,512]{2,1,0:T(8,128)} %get-tuple-element.32), channel_id=1, source_target_pairs={{0,6},{8,14},{16,16},{24,24},{1,1},{9,9},{17,19},{25,27},{2,0},{10... | collective-permute-start | bytes 786440 | tf_op jit(solution)/shard_map/ppermute | solution.py:491
  46.3 2.1 %value_rows.5 = f32[12,32,512]{2,1,0:T(8,128)} custom-call(f32[2,16,64,512]{3,2,1,0:T(8,128)} %value.9), custom_call_target="tpu_custom_call" | custom-call | tf_op jit(solution)/shard_map/value_rows/pallas_call | solution.py:95
  48.5 2.6 %collective-permute-start.2 = (f32[12,32,512]{2,1,0:T(8,128)}, f32[12,32,512]{2,1,0:T(8,128)S(1)}, u32[]{:S(2)}, u32[]{:S(2)}) collective-permute-start(f32[12,32,512]{2,1,0:T(8,128)} %value_rows.5), channel_id=1, source_target_pairs={{0,1},{8,9},{16,23},{24,31},{1,2},{9,10},{17,16},{25,24},{2,3},{10... | collective-permute-start | bytes 2359304 | tf_op jit(solution)/shard_map/ppermute | solution.py:487
  51.2 2.5 %reduce_sum.9 = f32[2,512]{1,0:T(2,128)S(1)} reduce(f32[2,16,64,512]{3,2,1,0:T(8,128)} %density.3, f32[]{:T(128)} %constant.2.clone.1), dimensions={1,2}, to_apply=%region_0.0 | reduce | flops 1047552 | bytes 4198404 | tf_op jit(solution)/shard_map/reduce_sum | solution.py:492
  53.6 6.6 %psum.7 = f32[2,512]{1,0:T(2,128)S(1)} all-reduce(f32[2,512]{1,0:T(2,128)S(1)} %reduce_sum.9), channel_id=1, replica_groups=mesh['vel'=4,'pos'=8] {'vel'}, use_global_device_ids=true, to_apply=%region_1.0 | all-reduce | flops 1024 | bytes 8192 | tf_op jit(solution)/shard_map/psum | solution.py:492
  60.3 1.5 %collective-permute-start.3 = (f32[2,2,64,512]{3,2,1,0:T(8,128)}, f32[2,2,64,512]{3,2,1,0:T(8,128)S(1)}, u32[]{:S(2)}, u32[]{:S(2)}) collective-permute-start(f32[2,2,64,512]{3,2,1,0:T(8,128)} %get-tuple-element.29), channel_id=1, source_target_pairs={{0,8},{8,16},{16,24},{1,9},{9,17},{17,25},{2,10},{10,18},{18,26},{... | collective-permute-start | bytes 1572872 | tf_op jit(solution)/shard_map/ppermute | solution.py:495
  61.7 7.9 %collective-permute-done.6 = f32[2,64,512]{2,1,0:T(8,128)S(1)} collective-permute-done((f32[2,64,512]{2,1,0:T(8,128)}, f32[2,64,512]{2,1,0:T(8,128)S(1)}, u32[]{:S(2)}, u32[]{:S(2)}) %collective-permute-start.6) | collective-permute-done | bytes 262176 | tf_op jit(solution)/shard_map/ppermute | solution.py:491
  69.6 1.3 %collective-permute-start.4 = (f32[2,2,64,512]{3,2,1,0:T(8,128)}, f32[2,2,64,512]{3,2,1,0:T(8,128)S(1)}, u32[]{:S(2)}, u32[]{:S(2)}) collective-permute-start(f32[2,2,64,512]{3,2,1,0:T(8,128)} %get-tuple-element.30), channel_id=1, source_target_pairs={{8,0},{16,8},{24,16},{9,1},{17,9},{25,17},{10,2},{18,10},{26,18},{... | collective-permute-start | bytes 1572872 | tf_op jit(solution)/shard_map/ppermute | solution.py:496
  70.9 0.0 collective-permute-done.5
  70.9 0.1 collective-permute-start.10
  71.0 2.6 %collective-permute-done.4.high = f32[2,2,64,512]{3,2,1,0:T(8,128)S(1)} collective-permute-done((f32[2,2,64,512]{3,2,1,0:T(8,128)}, f32[2,2,64,512]{3,2,1,0:T(8,128)S(1)}, u32[]{:S(2)}, u32[]{:S(2)}) %collective-permute-start.4) | collective-permute-done | bytes 524320 | tf_op jit(solution)/shard_map/ppermute | solution.py:496
  73.6 0.0 collective-permute-done.2.rest_2_
  73.6 0.0 collective-permute-done.1.rest_1_
  73.6 2.1 %collective-permute-start.9 = (f32[6,64,512]{2,1,0:T(8,128)}, f32[6,64,512]{2,1,0:T(8,128)S(1)}, u32[]{:S(2)}, u32[]{:S(2)}) collective-permute-start(f32[6,64,512]{2,1,0:T(8,128)} %get-tuple-element.43), channel_id=1, source_target_pairs={{0,7},{8,15},{16,17},{24,25},{1,0},{9,8},{17,18},{25,26},{2,1},{10... | collective-permute-start | bytes 2359304 | tf_op jit(solution)/shard_map/ppermute | solution.py:501
  75.7 10.2 %value_step.1 = (f32[2,16,64,512]{3,2,1,0:T(8,128)}, f32[2,64,512]{2,1,0:T(8,128)S(1)}, f32[2,64,512]{2,1,0:T(8,128)S(1)}) custom-call(f32[2,16,64,512]{3,2,1,0:T(8,128)} %value.9, f32[2,2,64,512]{3,2,1,0:T(8,128)S(1)} %collective-permute-done.3.low, f32[2,2,64,512]{3,2,1,0:T(8,128)S(1)} %collective-permute-done.4.high, ...), custom_call_target="tpu_custom_call" | custom-call | tf_op jit(solution)/shard_map/value_step/pallas_call | solution.py:245
  85.9 10.0 %collective-permute-start.7 = (f32[2,64,512]{2,1,0:T(8,128)S(1)}, f32[2,64,512]{2,1,0:T(8,128)S(1)}, u32[]{:S(2)}, u32[]{:S(2)}) collective-permute-start(f32[2,64,512]{2,1,0:T(8,128)S(1)} %get-tuple-element.40), channel_id=1, source_target_pairs={{0,8},{8,16},{16,24},{1,9},{9,17},{17,25},{2,10},{10,18},{18,26},{... | collective-permute-start | bytes 786440 | tf_op jit(solution)/shard_map/ppermute | solution.py:504
  95.9 1.3 %collective-permute-start.8 = (f32[2,64,512]{2,1,0:T(8,128)S(1)}, f32[2,64,512]{2,1,0:T(8,128)S(1)}, u32[]{:S(2)}, u32[]{:S(2)}) collective-permute-start(f32[2,64,512]{2,1,0:T(8,128)S(1)} %get-tuple-element.41), channel_id=1, source_target_pairs={{8,0},{16,8},{24,16},{9,1},{17,9},{25,17},{10,2},{18,10},{26,18},{... | collective-permute-start | bytes 786440 | tf_op jit(solution)/shard_map/ppermute | solution.py:505
  97.2 0.1 collective-permute-start.11
  97.3 1.1 collective-permute-start.12
  98.4 0.9 collective-permute-done.8.high_now
  99.3 13.6 %density_step.1 = (f32[2,16,64,512]{3,2,1,0:T(8,128)}, f32[3,64,512]{2,1,0:T(8,128)S(1)}) custom-call(f32[2,16,64,512]{3,2,1,0:T(8,128)} %density.3, f32[2,16,64,512]{3,2,1,0:T(8,128)} %get-tuple-element.22.control, f32[2,2,64,512]{3,2,1,0:T(8,128)S(1)} %collective-permute-done.3.low, f32[2,2,64,512]{3,2,1,0:T(8,128)S(1)} %collective-permute-done.4.high, ...), custom_call_target="tpu_custom_call" | custom-call | tf_op jit(solution)/shard_map/density_step/pallas_call | solution.py:346
  113.0 4.0 %arrive.1.partial = f32[2,16,64,512]{3,2,1,0:T(8,128)} custom-call(f32[2,16,64,512]{3,2,1,0:T(8,128)} %get-tuple-element.42.partial, f32[6,64,512]{2,1,0:T(8,128)S(1)} %collective-permute-done.9.refs_0_, f32[7,64,512]{2,1,0:T(8,128)S(1)} %collective-permute-done.10.refs_1_), custom_call_target="tpu_custom_call", output_to_operand_aliasing={{}: (0, {})} | custom-call | tf_op jit(solution)/shard_map/arrive/pallas_call | solution.py:396
  117.0 0.7 arrive_rest.2.partial
  117.8 1.8 %collective-permute-done.12.halo = f32[1,64,512]{2,1,0:T(8,128)S(1)} collective-permute-done((f32[1,64,512]{2,1,0:T(8,128)S(1)}, f32[1,64,512]{2,1,0:T(8,128)S(1)}, u32[]{:S(2)}, u32[]{:S(2)}) %collective-permute-start.12) | collective-permute-done | bytes 131104 | tf_op jit(solution)/shard_map/ppermute | solution.py:501
  119.5 0.7 arrive_rest.3
  (8 shorter events, 0.0 us)
Async XLA Ops:
  2.1 71.5 %collective-permute-start.1 = (f32[18,32,512]{2,1,0:T(8,128)S(1)}, f32[18,32,512]{2,1,0:T(8,128)S(1)}, u32[]{:S(2)}, u32[]{:S(2)}) collective-permute-start(f32[18,32,512]{2,1,0:T(8,128)S(1)} %value_rows.4), channel_id=1, source_target_pairs={{0,1},{8,9},{16,23},{24,31},{1,2},{9,10},{17,16},{25,24},{2,3},{10... | collective-permute-start | bytes 3538952 | tf_op jit(solution)/shard_map/ppermute | solution.py:487
  6.0 30.9 %collective-permute-start = (f32[2,32,512]{2,1,0:T(8,128)S(1)}, f32[2,32,512]{2,1,0:T(8,128)S(1)}, u32[]{:S(2)}, u32[]{:S(2)}) collective-permute-start(f32[2,32,512]{2,1,0:T(8,128)S(1)} %value_rows.3), channel_id=1, source_target_pairs={{0,1},{8,9},{16,23},{24,31},{1,2},{9,10},{17,16},{25,24},{2,3},{10... | collective-permute-start | bytes 393224 | tf_op jit(solution)/shard_map/ppermute | solution.py:487
  40.4 30.6 %collective-permute-start.5 = (f32[7,64,512]{2,1,0:T(8,128)}, f32[7,64,512]{2,1,0:T(8,128)}, u32[]{:S(2)}, u32[]{:S(2)}) collective-permute-start(f32[7,64,512]{2,1,0:T(8,128)} %get-tuple-element.31), channel_id=1, source_target_pairs={{0,6},{8,14},{16,16},{24,24},{1,1},{9,9},{17,19},{25,27},{2,0},{10... | collective-permute-start | bytes 2752520 | tf_op jit(solution)/shard_map/ppermute | solution.py:491
  44.0 25.6 %collective-permute-start.6 = (f32[2,64,512]{2,1,0:T(8,128)}, f32[2,64,512]{2,1,0:T(8,128)S(1)}, u32[]{:S(2)}, u32[]{:S(2)}) collective-permute-start(f32[2,64,512]{2,1,0:T(8,128)} %get-tuple-element.32), channel_id=1, source_target_pairs={{0,6},{8,14},{16,16},{24,24},{1,1},{9,9},{17,19},{25,27},{2,0},{10... | collective-permute-start | bytes 786440 | tf_op jit(solution)/shard_map/ppermute | solution.py:491
  48.5 25.1 %collective-permute-start.2 = (f32[12,32,512]{2,1,0:T(8,128)}, f32[12,32,512]{2,1,0:T(8,128)S(1)}, u32[]{:S(2)}, u32[]{:S(2)}) collective-permute-start(f32[12,32,512]{2,1,0:T(8,128)} %value_rows.5), channel_id=1, source_target_pairs={{0,1},{8,9},{16,23},{24,31},{1,2},{9,10},{17,16},{25,24},{2,3},{10... | collective-permute-start | bytes 2359304 | tf_op jit(solution)/shard_map/ppermute | solution.py:487
  60.3 37.0 %copy-start = (f32[1,64,512]{2,1,0:T(8,128)S(1)}, f32[1,64,512]{2,1,0:T(8,128)}, u32[]{:S(2)}) copy-start(f32[1,64,512]{2,1,0:T(8,128)} %get-tuple-element.45) | copy-start | bytes 393220
  60.3 10.7 %collective-permute-start.3 = (f32[2,2,64,512]{3,2,1,0:T(8,128)}, f32[2,2,64,512]{3,2,1,0:T(8,128)S(1)}, u32[]{:S(2)}, u32[]{:S(2)}) collective-permute-start(f32[2,2,64,512]{3,2,1,0:T(8,128)} %get-tuple-element.29), channel_id=1, source_target_pairs={{0,8},{8,16},{16,24},{1,9},{9,17},{17,25},{2,10},{10,18},{18,26},{... | collective-permute-start | bytes 1572872 | tf_op jit(solution)/shard_map/ppermute | solution.py:495
  69.6 4.0 %collective-permute-start.4 = (f32[2,2,64,512]{3,2,1,0:T(8,128)}, f32[2,2,64,512]{3,2,1,0:T(8,128)S(1)}, u32[]{:S(2)}, u32[]{:S(2)}) collective-permute-start(f32[2,2,64,512]{3,2,1,0:T(8,128)} %get-tuple-element.30), channel_id=1, source_target_pairs={{8,0},{16,8},{24,16},{9,1},{17,9},{25,17},{10,2},{18,10},{26,18},{... | collective-permute-start | bytes 1572872 | tf_op jit(solution)/shard_map/ppermute | solution.py:496
  70.9 42.0 %collective-permute-start.10 = (f32[7,64,512]{2,1,0:T(8,128)}, f32[7,64,512]{2,1,0:T(8,128)S(1)}, u32[]{:S(2)}, u32[]{:S(2)}) collective-permute-start(f32[7,64,512]{2,1,0:T(8,128)} %collective-permute-done.5), channel_id=1, source_target_pairs={{0,1},{8,9},{16,17},{24,25},{1,0},{9,8},{17,16},{25,24},{2,3},{10,... | collective-permute-start | bytes 2752520 | tf_op jit(solution)/shard_map/ppermute | solution.py:500
  73.6 39.3 %collective-permute-start.9 = (f32[6,64,512]{2,1,0:T(8,128)}, f32[6,64,512]{2,1,0:T(8,128)S(1)}, u32[]{:S(2)}, u32[]{:S(2)}) collective-permute-start(f32[6,64,512]{2,1,0:T(8,128)} %get-tuple-element.43), channel_id=1, source_target_pairs={{0,7},{8,15},{16,17},{24,25},{1,0},{9,8},{17,18},{25,26},{2,1},{10... | collective-permute-start | bytes 2359304 | tf_op jit(solution)/shard_map/ppermute | solution.py:501
  85.9 11.3 %collective-permute-start.7 = (f32[2,64,512]{2,1,0:T(8,128)S(1)}, f32[2,64,512]{2,1,0:T(8,128)S(1)}, u32[]{:S(2)}, u32[]{:S(2)}) collective-permute-start(f32[2,64,512]{2,1,0:T(8,128)S(1)} %get-tuple-element.40), channel_id=1, source_target_pairs={{0,8},{8,16},{16,24},{1,9},{9,17},{17,25},{2,10},{10,18},{18,26},{... | collective-permute-start | bytes 786440 | tf_op jit(solution)/shard_map/ppermute | solution.py:504
  95.9 3.4 %collective-permute-start.8 = (f32[2,64,512]{2,1,0:T(8,128)S(1)}, f32[2,64,512]{2,1,0:T(8,128)S(1)}, u32[]{:S(2)}, u32[]{:S(2)}) collective-permute-start(f32[2,64,512]{2,1,0:T(8,128)S(1)} %get-tuple-element.41), channel_id=1, source_target_pairs={{8,0},{16,8},{24,16},{9,1},{17,9},{25,17},{10,2},{18,10},{26,18},{... | collective-permute-start | bytes 786440 | tf_op jit(solution)/shard_map/ppermute | solution.py:505
  97.2 19.8 %collective-permute-start.11 = (f32[2,64,512]{2,1,0:T(8,128)S(1)}, f32[2,64,512]{2,1,0:T(8,128)S(1)}, u32[]{:S(2)}, u32[]{:S(2)}) collective-permute-start(f32[2,64,512]{2,1,0:T(8,128)S(1)} %collective-permute-done.6), channel_id=1, source_target_pairs={{0,1},{8,9},{16,17},{24,25},{1,0},{9,8},{17,16},{25,24},{2,3},{10,... | collective-permute-start | bytes 786440 | tf_op jit(solution)/shard_map/ppermute | solution.py:500
  97.3 22.2 %collective-permute-start.12 = (f32[1,64,512]{2,1,0:T(8,128)S(1)}, f32[1,64,512]{2,1,0:T(8,128)S(1)}, u32[]{:S(2)}, u32[]{:S(2)}) collective-permute-start(f32[1,64,512]{2,1,0:T(8,128)S(1)} %copy-done), channel_id=1, source_target_pairs={{0,7},{8,15},{16,17},{24,25},{1,0},{9,8},{17,18},{25,26},{2,1},{10... | collective-permute-start | bytes 393224 | tf_op jit(solution)/shard_map/ppermute | solution.py:501
